TPU v7x, 512 devices: a whole 4x4x16 slice. The times are simulated.
512 devices in a mesh: section: 32 (over z_lo, y), dp: 16 (over z_hi, x, core).
Axes of the slice: x: 4, y: 4, z: 16 (z_hi: 2, z_lo: 8; z = z_hi * 8 + z_lo), core: 2. Of those that a mesh axis runs over, the one named last changes fastest.
Arguments:
- section_inputs: bfloat16 [32, 12, 1536, 512], P('section', None, 'dp'), may hold values from -6 to 6
- cotangent: bfloat16 [12, 1536, 512], P(None, 'dp'), may hold values from -6 to 6
- weight_in: bfloat16 [32, 512, 512], P('section', 'dp'), may hold values from -0.25 to 0.25
- weight_out: bfloat16 [32, 512, 512], P('section', 'dp'), may hold values from -0.25 to 0.25
Outputs:
- grad_in: float32 [32, 512, 512], P('section', 'dp')
- grad_out: float32 [32, 512, 512], P('section', 'dp')
- input_grad: bfloat16 [32, 12, 1536, 512], P('section', None, 'dp')
All inputs are finite; a program needn't handle non-finite values.
Results may differ from a plain program's by a relative error of at most 0.029.
Values may be sent and summed in bfloat16 or wider, within the bound.
No kernel may reach another device: no remote copies, remote signals or barrier semaphores. Data moves between devices by JAX's collectives and lax.ppermute only.
A program may use at most 64 MiB of HBM per device.

v0:
```python
import jax
import jax.numpy as jnp
from jax import lax
from jax.sharding import PartitionSpec as P

RHO = 0.25


def passed_along(block, axis, distance):
    devices = range(lax.axis_size(axis))
    route = [(i - distance, i) for i in devices if i - distance in devices]
    return lax.ppermute(block, axis, route)


def contract_rows(left, right):
    return lax.dot_general(
        left, right, (((0,), (0,)), ((), ())), preferred_element_type=jnp.float32
    )


def contract_cols(left, right):
    return lax.dot_general(
        left, right, (((1,), (1,)), ((), ())), preferred_element_type=jnp.float32
    )


def body(section_inputs, cotangent, weight_in, weight_out):
    sections = lax.axis_size("section")
    position = lax.axis_index("section")
    full_in, full_out = (
        lax.all_gather(weight_in, "dp", axis=1, tiled=True),
        lax.all_gather(weight_out, "dp", axis=1, tiled=True),
    )
    w_in = full_in[0]
    w_out = full_out[0]
    inputs = section_inputs[0]
    micro = inputs.shape[0]
    rows = inputs.shape[1]
    width = inputs.shape[2]
    is_last = position == sections - 1

    def forward(x):
        z = jnp.dot(x, w_in, preferred_element_type=jnp.float32)
        return (z, jax.nn.silu(z).astype(jnp.bfloat16))

    def tick(step, carry):
        arriving, grad_a, grad_b, input_grads, kept = carry
        turn = step - (sections - 1 - position)
        active = (turn >= 0) & (turn < micro)
        slot = jnp.clip(turn, 0, micro - 1)
        x = lax.dynamic_index_in_dim(inputs, slot, 0, keepdims=False)
        given = lax.dynamic_index_in_dim(cotangent, slot, 0, keepdims=False)
        g = jnp.where(is_last, given, arriving)

        def work(unused):
            z, h = forward(x)
            sig = jax.nn.sigmoid(z)
            dz = (RHO * contract_cols(g, w_out) * sig * (1.0 + z * (1.0 - sig))).astype(
                jnp.bfloat16
            )
            dx = (g.astype(jnp.float32) + contract_cols(dz, w_in)).astype(jnp.bfloat16)
            new_inputs = lax.dynamic_update_index_in_dim(input_grads, dx, slot, 0)
            return (
                dx,
                grad_a + contract_rows(x, dz),
                grad_b + RHO * contract_rows(h, g),
                new_inputs,
                kept,
            )

        def skip(unused):
            return (jnp.zeros((rows, width), jnp.bfloat16), grad_a, grad_b, input_grads, kept)

        sending, grad_a, grad_b, input_grads, kept = lax.cond(active, work, skip, None)
        arriving = passed_along(sending, "section", -1)
        return (arriving, grad_a, grad_b, input_grads, kept)

    blank = jnp.zeros((micro, rows, width), jnp.bfloat16)
    kept_start = ()
    start = (
        jnp.zeros((rows, width), jnp.bfloat16),
        jnp.zeros((width, width), jnp.float32),
        jnp.zeros((width, width), jnp.float32),
        blank,
        kept_start,
    )
    arriving, grad_a, grad_b, input_grads, kept = lax.fori_loop(
        0, sections + micro - 1, tick, start
    )
    share_a, share_b = (
        lax.psum_scatter(grad_a[None], "dp", scatter_dimension=1, tiled=True),
        lax.psum_scatter(grad_b[None], "dp", scatter_dimension=1, tiled=True),
    )
    factor = 4.0 / jnp.sqrt(jnp.float32(micro * rows * lax.axis_size("dp")))
    return (share_a * factor, share_b * factor, input_grads[None])


def solution(mesh):
    return jax.shard_map(
        body,
        mesh=mesh,
        in_specs=(
            P("section", None, "dp", None),
            P(None, "dp", None),
            P("section", "dp", None),
            P("section", "dp", None),
        ),
        out_specs=(
            P("section", "dp", None),
            P("section", "dp", None),
            P("section", None, "dp", None),
        ),
        check_vma=False,
    )
```

profile of v0, /device:TPU:1, one launch (start us, length us, event | category | flops | bytes accessed | tf_op | source)
XLA Modules:
  0.0 816.0 jit_solution(8440488998786143246)
XLA Ops:
  7.2 52.4 %all_gather.7 = bf16[1,512,512]{2,1,0:T(8,128)(2,1)S(1)} all-gather(bf16[1,32,512]{2,1,0:T(8,128)(2,1)} %param.10), channel_id=1, replica_groups=mesh['section'=32,'dp'=16] {'dp'}, dimensions={1}, use_global_device_ids=true | all-gather | bytes 557056 | tf_op jit(solution)/shard_map/all_gather | solution.py:31
  59.6 38.5 %all_gather.6 = bf16[1,512,512]{2,1,0:T(8,128)(2,1)S(1)} all-gather(bf16[1,32,512]{2,1,0:T(8,128)(2,1)} %param.11), channel_id=1, replica_groups=mesh['section'=32,'dp'=16] {'dp'}, dimensions={1}, use_global_device_ids=true | all-gather | bytes 557056 | tf_op jit(solution)/shard_map/all_gather | solution.py:32
  99.5 464.3 %while.21 = (s32[]{:T(128)}, bf16[96,512]{1,0:T(8,128)(2,1)S(1)}, f32[512,512]{1,0:T(8,128)S(1)}, f32[512,512]{1,0:T(8,128)S(1)}, bf16[12,96,512]{2,1,0:T(8,128)...) while((s32[]{:T(128)}, bf16[96,512]{1,0:T(8,128)(2,1)S(1)}, ...), condition=%wide.region_3.4_spmd, body=%wide.region_0.3_spmd.sunk | while | flops 253378560 | bytes 8028548 | solution.py:87
  153.9 7.5 collective-permute-done
  170.3 6.6 collective-permute-done
  215.6 7.5 collective-permute-done
  224.4 6.6 collective-permute-done
  269.7 6.3 collective-permute-done
  277.3 7.5 collective-permute-done
  286.1 6.6 collective-permute-done
  323.9 77.5 %collective-permute-done = bf16[96,512]{1,0:T(8,128)(2,1)S(1)} collective-permute-done((bf16[96,512]{1,0:T(8,128)(2,1)S(1)}, bf16[96,512]{1,0:T(8,128)(2,1)S(1)}, u32[]{:S(2)}, u32[]{:S(2)}) %collective-permute-start) | collective-permute-done | bytes 98336 | tf_op jit(solution)/shard_map/while/body/eval_jaxpr/ppermute | solution.py:12
  407.5 9.3 %collective-permute-done = bf16[96,512]{1,0:T(8,128)(2,1)S(1)} collective-permute-done((bf16[96,512]{1,0:T(8,128)(2,1)S(1)}, bf16[96,512]{1,0:T(8,128)(2,1)S(1)}, u32[]{:S(2)}, u32[]{:S(2)}) %collective-permute-start) | collective-permute-done | bytes 98336 | tf_op jit(solution)/shard_map/while/body/eval_jaxpr/ppermute | solution.py:12
  423.0 7.2 collective-permute-done
  436.4 8.7 %collective-permute-done = bf16[96,512]{1,0:T(8,128)(2,1)S(1)} collective-permute-done((bf16[96,512]{1,0:T(8,128)(2,1)S(1)}, bf16[96,512]{1,0:T(8,128)(2,1)S(1)}, u32[]{:S(2)}, u32[]{:S(2)}) %collective-permute-start) | collective-permute-done | bytes 98336 | tf_op jit(solution)/shard_map/while/body/eval_jaxpr/ppermute | solution.py:12
  451.3 7.8 collective-permute-done
  465.3 7.1 collective-permute-done
  478.5 8.1 collective-permute-done
  492.7 7.1 collective-permute-done
  506.0 7.0 collective-permute-done
  519.2 8.0 collective-permute-done
  533.3 7.2 collective-permute-done
  546.7 6.9 collective-permute-done
  565.6 138.3 %reduce-scatter.5.cloned.1.call-done = f32[1,32,512]{2,1,0:T(8,128)} async-done(((f32[1,512,512]{2,1,0:T(8,128)}), f32[1,32,512]{2,1,0:T(8,128)}) %reduce-scatter.5.cloned.1.call-update) | async-done | bytes 65552 | tf_op jit(solution)/shard_map/reduce_scatter | solution.py:92
  705.4 102.3 %reduce-scatter.3.cloned.1.call-done = f32[1,32,512]{2,1,0:T(8,128)} async-done(((f32[1,512,512]{2,1,0:T(8,128)}), f32[1,32,512]{2,1,0:T(8,128)}) %reduce-scatter.3.cloned.1.call-update) | async-done | bytes 65552 | tf_op jit(solution)/shard_map/reduce_scatter | solution.py:91
  (227 shorter events, 317.5 us)
Async XLA Ops:
  7.2 696.8 %reduce-scatter.5.cloned.1.call-start = ((), (), s32[]{:S(2)}) async-start(), calls=%async_computation.3 | async-start | bytes 1114112 | tf_op jit(solution)/shard_map/reduce_scatter | solution.py:92
  152.6 8.9 %collective-permute-start = (bf16[96,512]{1,0:T(8,128)(2,1)S(1)}, bf16[96,512]{1,0:T(8,128)(2,1)S(1)}, u32[]{:S(2)}, u32[]{:S(2)}) collective-permute-start(bf16[96,512]{1,0:T(8,128)(2,1)S(1)} %get-tuple-element.493), channel_id=1, source_target_pairs={{16,0},{32,16},{48,32},{64,48},{80,64},{96,80},{112,96},{128,112},... | collective-permute-start | bytes 294920 | tf_op jit(solution)/shard_map/while/body/eval_jaxpr/ppermute | solution.py:12
  169.0 7.9 collective-permute-start
  206.6 7.6 collective-permute-start
  214.3 8.8 %collective-permute-start = (bf16[96,512]{1,0:T(8,128)(2,1)S(1)}, bf16[96,512]{1,0:T(8,128)(2,1)S(1)}, u32[]{:S(2)}, u32[]{:S(2)}) collective-permute-start(bf16[96,512]{1,0:T(8,128)(2,1)S(1)} %get-tuple-element.493), channel_id=1, source_target_pairs={{16,0},{32,16},{48,32},{64,48},{80,64},{96,80},{112,96},{128,112},... | collective-permute-start | bytes 294920 | tf_op jit(solution)/shard_map/while/body/eval_jaxpr/ppermute | solution.py:12
  223.1 7.9 collective-permute-start
  231.1 7.6 collective-permute-start
  268.4 7.6 collective-permute-start
  276.0 8.8 %collective-permute-start = (bf16[96,512]{1,0:T(8,128)(2,1)S(1)}, bf16[96,512]{1,0:T(8,128)(2,1)S(1)}, u32[]{:S(2)}, u32[]{:S(2)}) collective-permute-start(bf16[96,512]{1,0:T(8,128)(2,1)S(1)} %get-tuple-element.493), channel_id=1, source_target_pairs={{16,0},{32,16},{48,32},{64,48},{80,64},{96,80},{112,96},{128,112},... | collective-permute-start | bytes 294920 | tf_op jit(solution)/shard_map/while/body/eval_jaxpr/ppermute | solution.py:12
  284.8 7.9 collective-permute-start
  292.8 7.6 collective-permute-start
  322.6 78.8 %collective-permute-start = (bf16[96,512]{1,0:T(8,128)(2,1)S(1)}, bf16[96,512]{1,0:T(8,128)(2,1)S(1)}, u32[]{:S(2)}, u32[]{:S(2)}) collective-permute-start(bf16[96,512]{1,0:T(8,128)(2,1)S(1)} %get-tuple-element.493), channel_id=1, source_target_pairs={{16,0},{32,16},{48,32},{64,48},{80,64},{96,80},{112,96},{128,112},... | collective-permute-start | bytes 294920 | tf_op jit(solution)/shard_map/while/body/eval_jaxpr/ppermute | solution.py:12
  406.2 10.6 %collective-permute-start = (bf16[96,512]{1,0:T(8,128)(2,1)S(1)}, bf16[96,512]{1,0:T(8,128)(2,1)S(1)}, u32[]{:S(2)}, u32[]{:S(2)}) collective-permute-start(bf16[96,512]{1,0:T(8,128)(2,1)S(1)} %get-tuple-element.493), channel_id=1, source_target_pairs={{16,0},{32,16},{48,32},{64,48},{80,64},{96,80},{112,96},{128,112},... | collective-permute-start | bytes 294920 | tf_op jit(solution)/shard_map/while/body/eval_jaxpr/ppermute | solution.py:12
  421.7 8.5 %collective-permute-start = (bf16[96,512]{1,0:T(8,128)(2,1)S(1)}, bf16[96,512]{1,0:T(8,128)(2,1)S(1)}, u32[]{:S(2)}, u32[]{:S(2)}) collective-permute-start(bf16[96,512]{1,0:T(8,128)(2,1)S(1)} %get-tuple-element.493), channel_id=1, source_target_pairs={{16,0},{32,16},{48,32},{64,48},{80,64},{96,80},{112,96},{128,112},... | collective-permute-start | bytes 294920 | tf_op jit(solution)/shard_map/while/body/eval_jaxpr/ppermute | solution.py:12
  435.1 10.0 %collective-permute-start = (bf16[96,512]{1,0:T(8,128)(2,1)S(1)}, bf16[96,512]{1,0:T(8,128)(2,1)S(1)}, u32[]{:S(2)}, u32[]{:S(2)}) collective-permute-start(bf16[96,512]{1,0:T(8,128)(2,1)S(1)} %get-tuple-element.493), channel_id=1, source_target_pairs={{16,0},{32,16},{48,32},{64,48},{80,64},{96,80},{112,96},{128,112},... | collective-permute-start | bytes 294920 | tf_op jit(solution)/shard_map/while/body/eval_jaxpr/ppermute | solution.py:12
  450.0 9.1 %collective-permute-start = (bf16[96,512]{1,0:T(8,128)(2,1)S(1)}, bf16[96,512]{1,0:T(8,128)(2,1)S(1)}, u32[]{:S(2)}, u32[]{:S(2)}) collective-permute-start(bf16[96,512]{1,0:T(8,128)(2,1)S(1)} %get-tuple-element.493), channel_id=1, source_target_pairs={{16,0},{32,16},{48,32},{64,48},{80,64},{96,80},{112,96},{128,112},... | collective-permute-start | bytes 294920 | tf_op jit(solution)/shard_map/while/body/eval_jaxpr/ppermute | solution.py:12
  464.0 8.4 %collective-permute-start = (bf16[96,512]{1,0:T(8,128)(2,1)S(1)}, bf16[96,512]{1,0:T(8,128)(2,1)S(1)}, u32[]{:S(2)}, u32[]{:S(2)}) collective-permute-start(bf16[96,512]{1,0:T(8,128)(2,1)S(1)} %get-tuple-element.493), channel_id=1, source_target_pairs={{16,0},{32,16},{48,32},{64,48},{80,64},{96,80},{112,96},{128,112},... | collective-permute-start | bytes 294920 | tf_op jit(solution)/shard_map/while/body/eval_jaxpr/ppermute | solution.py:12
  477.2 9.4 %collective-permute-start = (bf16[96,512]{1,0:T(8,128)(2,1)S(1)}, bf16[96,512]{1,0:T(8,128)(2,1)S(1)}, u32[]{:S(2)}, u32[]{:S(2)}) collective-permute-start(bf16[96,512]{1,0:T(8,128)(2,1)S(1)} %get-tuple-element.493), channel_id=1, source_target_pairs={{16,0},{32,16},{48,32},{64,48},{80,64},{96,80},{112,96},{128,112},... | collective-permute-start | bytes 294920 | tf_op jit(solution)/shard_map/while/body/eval_jaxpr/ppermute | solution.py:12
  491.4 8.4 %collective-permute-start = (bf16[96,512]{1,0:T(8,128)(2,1)S(1)}, bf16[96,512]{1,0:T(8,128)(2,1)S(1)}, u32[]{:S(2)}, u32[]{:S(2)}) collective-permute-start(bf16[96,512]{1,0:T(8,128)(2,1)S(1)} %get-tuple-element.493), channel_id=1, source_target_pairs={{16,0},{32,16},{48,32},{64,48},{80,64},{96,80},{112,96},{128,112},... | collective-permute-start | bytes 294920 | tf_op jit(solution)/shard_map/while/body/eval_jaxpr/ppermute | solution.py:12
  504.7 8.3 %collective-permute-start = (bf16[96,512]{1,0:T(8,128)(2,1)S(1)}, bf16[96,512]{1,0:T(8,128)(2,1)S(1)}, u32[]{:S(2)}, u32[]{:S(2)}) collective-permute-start(bf16[96,512]{1,0:T(8,128)(2,1)S(1)} %get-tuple-element.493), channel_id=1, source_target_pairs={{16,0},{32,16},{48,32},{64,48},{80,64},{96,80},{112,96},{128,112},... | collective-permute-start | bytes 294920 | tf_op jit(solution)/shard_map/while/body/eval_jaxpr/ppermute | solution.py:12
  517.9 9.3 %collective-permute-start = (bf16[96,512]{1,0:T(8,128)(2,1)S(1)}, bf16[96,512]{1,0:T(8,128)(2,1)S(1)}, u32[]{:S(2)}, u32[]{:S(2)}) collective-permute-start(bf16[96,512]{1,0:T(8,128)(2,1)S(1)} %get-tuple-element.493), channel_id=1, source_target_pairs={{16,0},{32,16},{48,32},{64,48},{80,64},{96,80},{112,96},{128,112},... | collective-permute-start | bytes 294920 | tf_op jit(solution)/shard_map/while/body/eval_jaxpr/ppermute | solution.py:12
  532.0 8.5 %collective-permute-start = (bf16[96,512]{1,0:T(8,128)(2,1)S(1)}, bf16[96,512]{1,0:T(8,128)(2,1)S(1)}, u32[]{:S(2)}, u32[]{:S(2)}) collective-permute-start(bf16[96,512]{1,0:T(8,128)(2,1)S(1)} %get-tuple-element.493), channel_id=1, source_target_pairs={{16,0},{32,16},{48,32},{64,48},{80,64},{96,80},{112,96},{128,112},... | collective-permute-start | bytes 294920 | tf_op jit(solution)/shard_map/while/body/eval_jaxpr/ppermute | solution.py:12
  545.4 8.2 %collective-permute-start = (bf16[96,512]{1,0:T(8,128)(2,1)S(1)}, bf16[96,512]{1,0:T(8,128)(2,1)S(1)}, u32[]{:S(2)}, u32[]{:S(2)}) collective-permute-start(bf16[96,512]{1,0:T(8,128)(2,1)S(1)} %get-tuple-element.493), channel_id=1, source_target_pairs={{16,0},{32,16},{48,32},{64,48},{80,64},{96,80},{112,96},{128,112},... | collective-permute-start | bytes 294920 | tf_op jit(solution)/shard_map/while/body/eval_jaxpr/ppermute | solution.py:12
  564.9 242.8 %reduce-scatter.3.cloned.1.call-start = ((), (), s32[]{:S(2)}) async-start(), calls=%async_computation.2 | async-start | bytes 1114112 | tf_op jit(solution)/shard_map/reduce_scatter | solution.py:91
  (23 other events, 149.3 us)
Sparse Core Ops, SparseCore 0:
  565.0 138.8 reduce-scatter.4
  709.3 98.2 reduce-scatter.2
where the time goes:
time: 819 us; the launch traced here: 816 us
  waiting for transfers between devices  590 us (72%)
  blocking collectives  90.9 us (11%)
  starting transfers between devices  55.6 us (7%)
  matrix products  47.2 us (6%)
  between operations  14.1 us (2%)
  other arithmetic  13.8 us (2%)
    ppermute x43, waiting for transfers between devices, passed_along(): return lax.ppermute(block, axis, route)  349 us
    reduce_scatter x1, waiting for transfers between devices, body(): lax.psum_scatter(grad_b[None], 'dp', scatter_dimension=1, tiled=True)  138 us
    reduce_scatter x1, waiting for transfers between devices, body(): lax.psum_scatter(grad_a[None], 'dp', scatter_dimension=1, tiled=True)  102 us
    ppermute x43, starting transfers between devices, passed_along(): return lax.ppermute(block, axis, route)  55.6 us
    all_gather x1, blocking collectives, body(): lax.all_gather(weight_in, 'dp', axis=1, tiled=True)  52.4 us
    all_gather x1, blocking collectives, body(): lax.all_gather(weight_out, 'dp', axis=1, tiled=True)  38.5 us
    dot_general x24, matrix products, contract_rows(): lax.dot_general(left, right, (((0,), (0,)), ((), ())), preferred_element_...  18.8 us
  transfers between devices with their start and end apart: 45, of which 45 were waited for; matrix products, arithmetic and copies ran while one was open for 0% of the time, Pallas kernels for 0%

commit v1 on v0

v1 whole, which is shorter than its diff:
```python
import jax
import jax.numpy as jnp
from jax import lax
from jax.sharding import PartitionSpec as P

RHO = 0.25
NY = 4
NZ = 8
NX = 4


def section_route(step_z, step_y):
    route = []
    for z in range(NZ):
        for y in range(NY):
            to_z = z + step_z
            if 0 <= to_z < NZ:
                route.append((z * NY + y, to_z * NY + (y + step_y) % NY))
    return route


def stage_route(source_z):
    return [(source_z * NY + y, (source_z - 1) * NY + y) for y in range(NY)]


def replica_route(step_zh, step_x, step_core):
    route = []
    for zh in range(2):
        for x in range(NX):
            for core in range(2):
                to = ((zh + step_zh) % 2, (x + step_x) % NX, (core + step_core) % 2)
                route.append(((zh * NX + x) * 2 + core, (to[0] * NX + to[1]) * 2 + to[2]))
    return route


def pick(array, index, axis):
    return lax.dynamic_index_in_dim(array, index, axis, keepdims=False)


def put(array, piece, index, axis):
    return lax.dynamic_update_index_in_dim(array, piece, index, axis)


def dot(left, right, left_dim, right_dim):
    return lax.dot_general(
        left, right, (((left_dim,), (right_dim,)), ((), ())), preferred_element_type=jnp.float32
    )


def slope(z):
    sig = jax.nn.sigmoid(z)
    return RHO * sig * (1.0 + z * (1.0 - sig))


def gather_weights(weight_in, weight_out, y, zh, x, core):
    own = jnp.concatenate([weight_in, weight_out], axis=0)
    rows, width = own.shape[1:]
    other = lax.ppermute(own, "dp", replica_route(1, 0, 0))
    both = put(jnp.stack([other, other]), own, zh, 0)
    sections = jnp.zeros((NY, 2, 2, rows, width), own.dtype)
    for step in range(NY):
        piece = both if step == 0 else lax.ppermute(both, "section", section_route(0, step))
        sections = put(sections, piece, (y - step) % NY, 0)
    along_x = jnp.zeros((NY, 2, 2, NX, rows, width), own.dtype)
    for step in range(NX):
        piece = sections if step == 0 else lax.ppermute(sections, "dp", replica_route(0, step, 0))
        along_x = put(along_x, piece, (x - step) % NX, 3)
    other = lax.ppermute(along_x, "dp", replica_route(0, 0, 1))
    full = put(jnp.stack([other, other], axis=4), along_x, core, 4)
    full = full.transpose(0, 2, 1, 3, 4, 5, 6)
    return full.reshape(NY, 2, 2 * NX * 2 * rows, width)


def exchange_rows(home, y):
    out = jnp.zeros_like(home)
    for step in range(NY):
        piece = pick(home, (y + step) % NY, 0)
        if step:
            piece = lax.ppermute(piece, "section", section_route(0, step))
        out = put(out, piece, (y - step) % NY, 0)
    return out


def reduce_replicas(grads, zh, x, core):
    width = grads.shape[-1]
    rows = grads.shape[1] // (2 * NX * 2)
    parts = grads.reshape(2, 2, NX, 2, rows, width)
    sent = pick(parts, 1 - core, 3).astype(jnp.bfloat16)
    total = pick(parts, core, 3) + lax.ppermute(sent, "dp", replica_route(0, 0, 1))
    acc = pick(total, x, 2)
    for step in range(1, NX):
        sent = pick(total, (x + step) % NX, 2).astype(jnp.bfloat16)
        acc = acc + lax.ppermute(sent, "dp", replica_route(0, step, 0))
    sent = pick(acc, 1 - zh, 1).astype(jnp.bfloat16)
    return pick(acc, zh, 1) + lax.ppermute(sent, "dp", replica_route(1, 0, 0))


def body(section_inputs, cotangent, weight_in, weight_out):
    position = lax.axis_index("section")
    replica = lax.axis_index("dp")
    z_stage, y = position // NY, position % NY
    zh, x, core = replica // (2 * NX), (replica // 2) % NX, replica % 2
    micro, rows, width = section_inputs.shape[1:]
    share = micro * rows // NY
    home_x = section_inputs[0].reshape(NY, share, width)

    weights = gather_weights(weight_in, weight_out, y, zh, x, core)
    stage_x = exchange_rows(home_x, y)
    slopes = [slope(dot(stage_x[s], weights[s, 0], 1, 0)) for s in range(NY)]

    given = pick(cotangent.reshape(NY, share, width), y, 0)
    g = jnp.where(z_stage == NZ - 1, given, jnp.zeros_like(given))
    kept = jnp.zeros((NY, share, width), jnp.bfloat16)
    for tick in range(NZ):
        active = z_stage == NZ - 1 - tick
        chain = [g]
        for s in reversed(range(0 if tick < NZ - 1 else 1, NY)):
            now = chain[-1]
            dz = (dot(now, weights[s, 1], 1, 1) * slopes[s]).astype(jnp.bfloat16)
            chain.append((now.astype(jnp.float32) + dot(dz, weights[s, 0], 1, 1)).astype(jnp.bfloat16))
        kept = jnp.where(active, jnp.stack(chain[NY - 1 :: -1]), kept)
        if tick < NZ - 1:
            g = lax.ppermute(chain[NY], "section", stage_route(NZ - 1 - tick))

    home_g = exchange_rows(kept, y).reshape(micro * rows, width)
    w_in, w_out = pick(weights[:, 0], y, 0), pick(weights[:, 1], y, 0)
    flat_x = section_inputs[0].reshape(micro * rows, width)
    flat_x, w_in, w_out, kept = lax.optimization_barrier((flat_x, w_in, w_out, kept))
    zed = dot(flat_x, w_in, 1, 0)
    h = jax.nn.silu(zed).astype(jnp.bfloat16)
    dz = (dot(home_g, w_out, 1, 1) * slope(zed)).astype(jnp.bfloat16)
    dx = (home_g.astype(jnp.float32) + dot(dz, w_in, 1, 1)).astype(jnp.bfloat16)
    grads = jnp.stack([dot(flat_x, dz, 0, 0), RHO * dot(h, home_g, 0, 0)])
    reduced = reduce_replicas(grads, zh, x, core)
    factor = 4.0 / jnp.sqrt(jnp.float32(micro * rows * lax.axis_size("dp")))
    reduced = reduced * factor
    return (reduced[0:1], reduced[1:2], dx.reshape(1, micro, rows, width))


def solution(mesh):
    return jax.shard_map(
        body,
        mesh=mesh,
        in_specs=(
            P("section", None, "dp", None),
            P(None, "dp", None),
            P("section", "dp", None),
            P("section", "dp", None),
        ),
        out_specs=(
            P("section", "dp", None),
            P("section", "dp", None),
            P("section", None, "dp", None),
        ),
        check_vma=False,
    )
```

time: 819 us -> 303 us (0.37)
  waiting for transfers between devices: 590 us -> 84.8 us
  blocking collectives: 90.9 us -> 0 us
  matrix products: 47.2 us -> 87 us
  starting transfers between devices: 55.6 us -> 94 us
  local copies, waits for them, and re-layouts: 2.9 us -> 20.6 us
  between operations: 14.1 us -> 2.06 us
    ppermute x43 -> x26, waiting for transfers between devices: 349 us -> 84.8 us  [the longest x7 47 us: body(): g = lax.ppermute(chain[NY], 'section', stage_route(NZ - 1 - tick))]
    reduce_scatter x2 -> x0, waiting for transfers between devices: 241 us -> none  [the longest x1 138 us: body(): lax.psum_scatter(grad_b[None], 'dp', scatter_dimension=1, tiled=True)]
    all_gather x2 -> x0, blocking collectives: 90.9 us -> none  [the longest x1 52.4 us: body(): lax.all_gather(weight_in, 'dp', axis=1, tiled=True)]
    dot_general x60 -> x40, matrix products: 47.2 us -> 87 us  [dot(): lax.dot_general(left, right, (((left_dim,), (right_dim,)), ((), ())), pre...]
    ppermute x43 -> x26, starting transfers between devices: 55.6 us -> 94 us  [the longest x6 21.9 us: exchange_rows(): piece = lax.ppermute(piece, 'section', section_route(0, step))]
    dynamic_update_slice x0 -> x16, local copies, waits for them, and re-layouts: none -> 11.4 us  [put(): return lax.dynamic_update_index_in_dim(array, piece, index, axis)]
  transfers between devices with their start and end apart: 45 -> 26, of which waited for: 45 -> 14; matrix products, arithmetic and copies ran while one was open for 0% -> 7% of each run, Pallas kernels for 0% -> 0%
where the time goes in v1:
time: 303 us; the launch traced here: 299 us
  starting transfers between devices  94 us (31%)
  matrix products  87 us (29%)
  waiting for transfers between devices  84.8 us (28%)
  local copies, waits for them, and re-layouts  20.6 us (7%)
  other arithmetic  10.3 us (3%)
    dot_general x40, matrix products, dot(): lax.dot_general(left, right, (((left_dim,), (right_dim,)), ((), ())), pre...  87 us
    ppermute x7, waiting for transfers between devices, body(): g = lax.ppermute(chain[NY], 'section', stage_route(NZ - 1 - tick))  47 us
    ppermute x6, starting transfers between devices, exchange_rows(): piece = lax.ppermute(piece, 'section', section_route(0, step))  21.9 us
    ppermute x1, starting transfers between devices, gather_weights(): other = lax.ppermute(own, 'dp', replica_route(1, 0, 0))  16.3 us
    ppermute x3, waiting for transfers between devices, gather_weights(): lax.ppermute(sections, 'dp', replica_route(0, step, 0))  14.8 us
    ppermute x6, waiting for transfers between devices, exchange_rows(): piece = lax.ppermute(piece, 'section', section_route(0, step))  11.6 us
    dynamic_update_slice x16, local copies, waits for them, and re-layouts, put(): return lax.dynamic_update_index_in_dim(array, piece, index, axis)  11.4 us
    ppermute x3, starting transfers between devices, gather_weights(): lax.ppermute(both, 'section', section_route(0, step))  10.7 us
  transfers between devices with their start and end apart: 26, of which 14 were waited for; matrix products, arithmetic and copies ran while one was open for 7% of the time, Pallas kernels for 0%

profile of v1, /device:TPU:1, one launch (start us, length us, event | category | flops | bytes accessed | tf_op | source)
XLA Modules:
  0.0 298.7 jit_solution(16566013449394619380)
XLA Ops:
  2.2 16.3 %collective-permute-start = (bf16[2,32,512]{2,1,0:T(8,128)(2,1)S(1)}, bf16[2,32,512]{2,1,0:T(8,128)(2,1)S(1)}, u32[]{:S(2)}, u32[]{:S(2)}) collective-permute-start(bf16[2,32,512]{2,1,0:T(8,128)(2,1)S(1)} %constant_dynamic-update-slice_fusion), channel_id=1, source_target_pairs={{0,8},{1,9},{2,10},{3,11},{4,12},{5,13},{6,14},{7,15},{8,0},{9,1},... | collective-permute-start | bytes 196616 | tf_op jit(solution)/shard_map/ppermute | solution.py:58
  20.3 3.2 %collective-permute-start.1 = (bf16[2,2,32,512]{3,2,0,1:T(8,128)(2,1)S(1)}, bf16[2,2,32,512]{3,2,0,1:T(8,128)(2,1)S(1)}, u32[]{:S(2)}, u32[]{:S(2)}) collective-permute-start(bf16[2,2,32,512]{3,2,0,1:T(8,128)(2,1)S(1)} %bitcast_dynamic-update-slice_fusion.15), channel_id=1, source_target_pairs={{0,16},{16,32},{32,48},{48,0},{64,80},{80,96},{96,112},{112,64},{1... | collective-permute-start | bytes 393224 | tf_op jit(solution)/shard_map/ppermute | solution.py:62
  23.5 4.5 %collective-permute-start.2 = (bf16[2,2,32,512]{3,2,0,1:T(8,128)(2,1)S(1)}, bf16[2,2,32,512]{3,2,0,1:T(8,128)(2,1)S(1)}, u32[]{:S(2)}, u32[]{:S(2)}) collective-permute-start(bf16[2,2,32,512]{3,2,0,1:T(8,128)(2,1)S(1)} %bitcast_dynamic-update-slice_fusion.15), channel_id=1, source_target_pairs={{0,32},{16,48},{32,0},{48,16},{64,96},{80,112},{96,64},{112,80},{1... | collective-permute-start | bytes 393224 | tf_op jit(solution)/shard_map/ppermute | solution.py:62
  28.1 3.0 collective-permute-start.3
  35.8 3.2 %collective-permute-start.4 = (bf16[4,2,2,32,512]{4,3,1,2,0:T(8,128)(2,1)}, bf16[4,2,2,32,512]{4,3,1,2,0:T(8,128)(2,1)}, u32[]{:S(2)}, u32[]{:S(2)}) collective-permute-start(bf16[4,2,2,32,512]{4,3,1,2,0:T(8,128)(2,1)} %bitcast_dynamic-update-slice_fusion.11), channel_id=1, source_target_pairs={{0,2},{1,3},{2,4},{3,5},{4,6},{5,7},{6,0},{7,1},{8,10},{9,11},{10,... | collective-permute-start | bytes 1572872 | tf_op jit(solution)/shard_map/ppermute | solution.py:66
  39.0 4.4 %collective-permute-start.5 = (bf16[4,2,2,32,512]{4,3,1,2,0:T(8,128)(2,1)}, bf16[4,2,2,32,512]{4,3,1,2,0:T(8,128)(2,1)}, u32[]{:S(2)}, u32[]{:S(2)}) collective-permute-start(bf16[4,2,2,32,512]{4,3,1,2,0:T(8,128)(2,1)} %bitcast_dynamic-update-slice_fusion.11), channel_id=1, source_target_pairs={{0,4},{1,5},{2,6},{3,7},{4,0},{5,1},{6,2},{7,3},{8,12},{9,13},{10,... | collective-permute-start | bytes 1572872 | tf_op jit(solution)/shard_map/ppermute | solution.py:66
  43.4 3.1 %collective-permute-start.6 = (bf16[4,2,2,32,512]{4,3,1,2,0:T(8,128)(2,1)}, bf16[4,2,2,32,512]{4,3,1,2,0:T(8,128)(2,1)S(1)}, u32[]{:S(2)}, u32[]{:S(2)}) collective-permute-start(bf16[4,2,2,32,512]{4,3,1,2,0:T(8,128)(2,1)} %bitcast_dynamic-update-slice_fusion.11), channel_id=1, source_target_pairs={{0,6},{1,7},{2,0},{3,1},{4,2},{5,3},{6,4},{7,5},{8,14},{9,15},{10,... | collective-permute-start | bytes 1572872 | tf_op jit(solution)/shard_map/ppermute | solution.py:66
  50.0 11.3 %collective-permute-done.5 = bf16[4,2,2,32,512]{4,3,1,2,0:T(8,128)(2,1)} collective-permute-done((bf16[4,2,2,32,512]{4,3,1,2,0:T(8,128)(2,1)}, bf16[4,2,2,32,512]{4,3,1,2,0:T(8,128)(2,1)}, u32[]{:S(2)}, u32[]{:S(2)}) %collective-permute-start.5) | collective-permute-done | bytes 524320 | tf_op jit(solution)/shard_map/ppermute | solution.py:66
  64.8 4.3 %collective-permute-start.7 = (bf16[4,2,2,4,32,512]{5,4,3,1,2,0:T(8,128)(2,1)S(1)}, bf16[4,2,2,4,32,512]{5,4,3,1,2,0:T(8,128)(2,1)}, u32[]{:S(2)}, u32[]{:S(2)}) collective-permute-start(bf16[4,2,2,4,32,512]{5,4,3,1,2,0:T(8,128)(2,1)S(1)} %bitcast_dynamic-update-slice_fusion.4), channel_id=1, source_target_pairs={{0,1},{1,0},{2,3},{3,2},{4,5},{5,4},{6,7},{7,6},{8,9},{9,8},{10,11... | collective-permute-start | bytes 6291464 | tf_op jit(solution)/shard_map/ppermute | solution.py:68
  73.3 5.4 %collective-permute-start.9 = (bf16[288,512]{1,0:T(8,128)(2,1)}, bf16[288,512]{1,0:T(8,128)(2,1)}, u32[]{:S(2)}, u32[]{:S(2)}) collective-permute-start(bf16[288,512]{1,0:T(8,128)(2,1)} %get-tuple-element.16), channel_id=1, source_target_pairs={{0,32},{16,48},{32,0},{48,16},{64,96},{80,112},{96,64},{112,80},{1... | collective-permute-start | bytes 884744 | tf_op jit(solution)/shard_map/ppermute | solution.py:79
  85.1 5.5 %collective-permute-done.9 = bf16[288,512]{1,0:T(8,128)(2,1)} collective-permute-done((bf16[288,512]{1,0:T(8,128)(2,1)}, bf16[288,512]{1,0:T(8,128)(2,1)}, u32[]{:S(2)}, u32[]{:S(2)}) %collective-permute-start.9) | collective-permute-done | bytes 294944 | tf_op jit(solution)/shard_map/ppermute | solution.py:79
  121.5 2.9 fusion.14
  177.2 47.0 %collective-permute-done.17 = bf16[288,512]{1,0:T(8,128)(2,1)} collective-permute-done((bf16[288,512]{1,0:T(8,128)(2,1)}, bf16[288,512]{1,0:T(8,128)(2,1)}, u32[]{:S(2)}, u32[]{:S(2)}) %collective-permute-start.17) | collective-permute-done | bytes 294944 | tf_op jit(solution)/shard_map/ppermute | solution.py:123
  232.7 4.6 %maximum_select_fusion = bf16[4,288,512]{2,1,0:T(8,128)(2,1)S(1)} fusion(bf16[1,288,512]{2,1,0:T(8,128)(2,1)} %bitcast.45, bf16[1,288,512]{2,1,0:T(8,128)(2,1)} %bitcast.399, bf16[1,288,512]{2,1,0:T(8,128)(2,1)} %bitcast.400, bf16[1,288,512]{2,1,0:T(8,128)(2,1)} %fusion.49, bf16[1,288,512]{2,1,0:T(8,128)(2,1)} %bitcast.395, ...), kind=kLoop, calls=%fused_computation.108 | loop fusion | flops 18874368 | bytes 10616840 | tf_op jit(solution)/shard_map/jit(_where)/select_n | solution.py:121
  237.5 6.5 %collective-permute-start.18 = (bf16[288,512]{1,0:T(8,128)(2,1)S(1)}, bf16[288,512]{1,0:T(8,128)(2,1)S(1)}, u32[]{:S(2)}, u32[]{:S(2)}) collective-permute-start(bf16[288,512]{1,0:T(8,128)(2,1)S(1)} %get-tuple-element.13), channel_id=1, source_target_pairs={{0,16},{16,32},{32,48},{48,0},{64,80},{80,96},{96,112},{112,64},{1... | collective-permute-start | bytes 884744 | tf_op jit(solution)/shard_map/ppermute | solution.py:79
  244.0 3.7 %collective-permute-start.19 = (bf16[288,512]{1,0:T(8,128)(2,1)S(1)}, bf16[288,512]{1,0:T(8,128)(2,1)S(1)}, u32[]{:S(2)}, u32[]{:S(2)}) collective-permute-start(bf16[288,512]{1,0:T(8,128)(2,1)S(1)} %get-tuple-element.12), channel_id=1, source_target_pairs={{0,32},{16,48},{32,0},{48,16},{64,96},{80,112},{96,64},{112,80},{1... | collective-permute-start | bytes 884744 | tf_op jit(solution)/shard_map/ppermute | solution.py:79
  253.2 3.1 %collective-permute-done.20 = bf16[288,512]{1,0:T(8,128)(2,1)S(1)} collective-permute-done((bf16[288,512]{1,0:T(8,128)(2,1)S(1)}, bf16[288,512]{1,0:T(8,128)(2,1)S(1)}, u32[]{:S(2)}, u32[]{:S(2)}) %collective-permute-start.20) | collective-permute-done | bytes 294944 | tf_op jit(solution)/shard_map/ppermute | solution.py:79
  259.8 8.4 %collective-permute-start.21 = (bf16[2,2,4,32,512]{4,3,0,1,2:T(8,128)(2,1)S(1)}, bf16[2,2,4,32,512]{4,3,0,1,2:T(8,128)(2,1)}, u32[]{:S(2)}, u32[]{:S(2)}) collective-permute-start(bf16[2,2,4,32,512]{4,3,0,1,2:T(8,128)(2,1)S(1)} %fusion.67), channel_id=1, source_target_pairs={{0,1},{1,0},{2,3},{3,2},{4,5},{5,4},{6,7},{7,6},{8,9},{9,8},{10,11... | collective-permute-start | bytes 1572872 | tf_op jit(solution)/shard_map/ppermute | solution.py:89
  271.2 4.0 %collective-permute-start.22 = (bf16[2,2,32,512]{3,2,0,1:T(8,128)(2,1)S(1)}, bf16[2,2,32,512]{3,2,0,1:T(8,128)(2,1)S(1)}, u32[]{:S(2)}, u32[]{:S(2)}) collective-permute-start(bf16[2,2,32,512]{3,2,0,1:T(8,128)(2,1)S(1)} %get-tuple-element.19), channel_id=1, source_target_pairs={{0,2},{1,3},{2,4},{3,5},{4,6},{5,7},{6,0},{7,1},{8,10},{9,11},{10,... | collective-permute-start | bytes 393224 | tf_op jit(solution)/shard_map/ppermute | solution.py:93
  275.2 3.3 %collective-permute-start.23 = (bf16[2,2,32,512]{3,2,0,1:T(8,128)(2,1)S(1)}, bf16[2,2,32,512]{3,2,0,1:T(8,128)(2,1)S(1)}, u32[]{:S(2)}, u32[]{:S(2)}) collective-permute-start(bf16[2,2,32,512]{3,2,0,1:T(8,128)(2,1)S(1)} %get-tuple-element.21), channel_id=1, source_target_pairs={{0,4},{1,5},{2,6},{3,7},{4,0},{5,1},{6,2},{7,3},{8,12},{9,13},{10,... | collective-permute-start | bytes 393224 | tf_op jit(solution)/shard_map/ppermute | solution.py:93
  278.5 3.2 %collective-permute-start.24 = (bf16[2,2,32,512]{3,2,0,1:T(8,128)(2,1)S(1)}, bf16[2,2,32,512]{3,2,0,1:T(8,128)(2,1)S(1)}, u32[]{:S(2)}, u32[]{:S(2)}) collective-permute-start(bf16[2,2,32,512]{3,2,0,1:T(8,128)(2,1)S(1)} %get-tuple-element.20), channel_id=1, source_target_pairs={{0,6},{1,7},{2,0},{3,1},{4,2},{5,3},{6,4},{7,5},{8,14},{9,15},{10,... | collective-permute-start | bytes 393224 | tf_op jit(solution)/shard_map/ppermute | solution.py:93
  284.3 5.7 %collective-permute-start.25 = (bf16[2,32,512]{2,1,0:T(8,128)(2,1)S(1)}, bf16[2,32,512]{2,1,0:T(8,128)(2,1)S(1)}, u32[]{:S(2)}, u32[]{:S(2)}) collective-permute-start(bf16[2,32,512]{2,1,0:T(8,128)(2,1)S(1)} %fusion.80), channel_id=1, source_target_pairs={{0,8},{1,9},{2,10},{3,11},{4,12},{5,13},{6,14},{7,15},{8,0},{9,1},... | collective-permute-start | bytes 196616 | tf_op jit(solution)/shard_map/ppermute | solution.py:95
  290.0 3.6 %add_convert_fusion = bf16[1152,512]{1,0:T(8,128)(2,1)} fusion(bf16[4,288,512]{2,1,0:T(8,128)(2,1)} %copy-done.4, bf16[1152,512]{1,0:T(8,128)(2,1)} %copy-done.30, bf16[512,512]{1,0:T(8,128)(2,1)} %copy-done.2), kind=kOutput, calls=%fused_computation.7 | convolution fusion | flops 605749248 | bytes 4063232 | tf_op jit(solution)/shard_map/dot_general | solution.py:45
  293.7 4.4 %collective-permute-done.25 = bf16[2,32,512]{2,1,0:T(8,128)(2,1)S(1)} collective-permute-done((bf16[2,32,512]{2,1,0:T(8,128)(2,1)S(1)}, bf16[2,32,512]{2,1,0:T(8,128)(2,1)S(1)}, u32[]{:S(2)}, u32[]{:S(2)}) %collective-permute-start.25) | collective-permute-done | bytes 65568 | tf_op jit(solution)/shard_map/ppermute | solution.py:95
  (169 shorter events, 132.2 us)
Async XLA Ops:
  2.2 18.1 %collective-permute-start = (bf16[2,32,512]{2,1,0:T(8,128)(2,1)S(1)}, bf16[2,32,512]{2,1,0:T(8,128)(2,1)S(1)}, u32[]{:S(2)}, u32[]{:S(2)}) collective-permute-start(bf16[2,32,512]{2,1,0:T(8,128)(2,1)S(1)} %constant_dynamic-update-slice_fusion), channel_id=1, source_target_pairs={{0,8},{1,9},{2,10},{3,11},{4,12},{5,13},{6,14},{7,15},{8,0},{9,1},... | collective-permute-start | bytes 196616 | tf_op jit(solution)/shard_map/ppermute | solution.py:58
  20.3 12.2 %collective-permute-start.1 = (bf16[2,2,32,512]{3,2,0,1:T(8,128)(2,1)S(1)}, bf16[2,2,32,512]{3,2,0,1:T(8,128)(2,1)S(1)}, u32[]{:S(2)}, u32[]{:S(2)}) collective-permute-start(bf16[2,2,32,512]{3,2,0,1:T(8,128)(2,1)S(1)} %bitcast_dynamic-update-slice_fusion.15), channel_id=1, source_target_pairs={{0,16},{16,32},{32,48},{48,0},{64,80},{80,96},{96,112},{112,64},{1... | collective-permute-start | bytes 393224 | tf_op jit(solution)/shard_map/ppermute | solution.py:62
  23.5 9.7 %collective-permute-start.2 = (bf16[2,2,32,512]{3,2,0,1:T(8,128)(2,1)S(1)}, bf16[2,2,32,512]{3,2,0,1:T(8,128)(2,1)S(1)}, u32[]{:S(2)}, u32[]{:S(2)}) collective-permute-start(bf16[2,2,32,512]{3,2,0,1:T(8,128)(2,1)S(1)} %bitcast_dynamic-update-slice_fusion.15), channel_id=1, source_target_pairs={{0,32},{16,48},{32,0},{48,16},{64,96},{80,112},{96,64},{112,80},{1... | collective-permute-start | bytes 393224 | tf_op jit(solution)/shard_map/ppermute | solution.py:62
  28.1 7.0 %collective-permute-start.3 = (bf16[2,2,32,512]{3,2,0,1:T(8,128)(2,1)S(1)}, bf16[2,2,32,512]{3,2,0,1:T(8,128)(2,1)S(1)}, u32[]{:S(2)}, u32[]{:S(2)}) collective-permute-start(bf16[2,2,32,512]{3,2,0,1:T(8,128)(2,1)S(1)} %bitcast_dynamic-update-slice_fusion.15), channel_id=1, source_target_pairs={{0,48},{16,0},{32,16},{48,32},{64,112},{80,64},{96,80},{112,96},{1... | collective-permute-start | bytes 393224 | tf_op jit(solution)/shard_map/ppermute | solution.py:62
  35.8 13.1 %collective-permute-start.4 = (bf16[4,2,2,32,512]{4,3,1,2,0:T(8,128)(2,1)}, bf16[4,2,2,32,512]{4,3,1,2,0:T(8,128)(2,1)}, u32[]{:S(2)}, u32[]{:S(2)}) collective-permute-start(bf16[4,2,2,32,512]{4,3,1,2,0:T(8,128)(2,1)} %bitcast_dynamic-update-slice_fusion.11), channel_id=1, source_target_pairs={{0,2},{1,3},{2,4},{3,5},{4,6},{5,7},{6,0},{7,1},{8,10},{9,11},{10,... | collective-permute-start | bytes 1572872 | tf_op jit(solution)/shard_map/ppermute | solution.py:66
  39.0 22.3 %collective-permute-start.5 = (bf16[4,2,2,32,512]{4,3,1,2,0:T(8,128)(2,1)}, bf16[4,2,2,32,512]{4,3,1,2,0:T(8,128)(2,1)}, u32[]{:S(2)}, u32[]{:S(2)}) collective-permute-start(bf16[4,2,2,32,512]{4,3,1,2,0:T(8,128)(2,1)} %bitcast_dynamic-update-slice_fusion.11), channel_id=1, source_target_pairs={{0,4},{1,5},{2,6},{3,7},{4,0},{5,1},{6,2},{7,3},{8,12},{9,13},{10,... | collective-permute-start | bytes 1572872 | tf_op jit(solution)/shard_map/ppermute | solution.py:66
  43.4 21.4 %collective-permute-start.6 = (bf16[4,2,2,32,512]{4,3,1,2,0:T(8,128)(2,1)}, bf16[4,2,2,32,512]{4,3,1,2,0:T(8,128)(2,1)S(1)}, u32[]{:S(2)}, u32[]{:S(2)}) collective-permute-start(bf16[4,2,2,32,512]{4,3,1,2,0:T(8,128)(2,1)} %bitcast_dynamic-update-slice_fusion.11), channel_id=1, source_target_pairs={{0,6},{1,7},{2,0},{3,1},{4,2},{5,3},{6,4},{7,5},{8,14},{9,15},{10,... | collective-permute-start | bytes 1572872 | tf_op jit(solution)/shard_map/ppermute | solution.py:66
  64.8 29.1 %collective-permute-start.7 = (bf16[4,2,2,4,32,512]{5,4,3,1,2,0:T(8,128)(2,1)S(1)}, bf16[4,2,2,4,32,512]{5,4,3,1,2,0:T(8,128)(2,1)}, u32[]{:S(2)}, u32[]{:S(2)}) collective-permute-start(bf16[4,2,2,4,32,512]{5,4,3,1,2,0:T(8,128)(2,1)S(1)} %bitcast_dynamic-update-slice_fusion.4), channel_id=1, source_target_pairs={{0,1},{1,0},{2,3},{3,2},{4,5},{5,4},{6,7},{7,6},{8,9},{9,8},{10,11... | collective-permute-start | bytes 6291464 | tf_op jit(solution)/shard_map/ppermute | solution.py:68
  71.3 12.0 %collective-permute-start.8 = (bf16[288,512]{1,0:T(8,128)(2,1)}, bf16[288,512]{1,0:T(8,128)(2,1)}, u32[]{:S(2)}, u32[]{:S(2)}) collective-permute-start(bf16[288,512]{1,0:T(8,128)(2,1)} %get-tuple-element.17), channel_id=1, source_target_pairs={{0,16},{16,32},{32,48},{48,0},{64,80},{80,96},{96,112},{112,64},{1... | collective-permute-start | bytes 884744 | tf_op jit(solution)/shard_map/ppermute | solution.py:79
  73.3 17.3 %collective-permute-start.9 = (bf16[288,512]{1,0:T(8,128)(2,1)}, bf16[288,512]{1,0:T(8,128)(2,1)}, u32[]{:S(2)}, u32[]{:S(2)}) collective-permute-start(bf16[288,512]{1,0:T(8,128)(2,1)} %get-tuple-element.16), channel_id=1, source_target_pairs={{0,32},{16,48},{32,0},{48,16},{64,96},{80,112},{96,64},{112,80},{1... | collective-permute-start | bytes 884744 | tf_op jit(solution)/shard_map/ppermute | solution.py:79
  78.7 13.6 %collective-permute-start.10 = (bf16[288,512]{1,0:T(8,128)(2,1)}, bf16[288,512]{1,0:T(8,128)(2,1)}, u32[]{:S(2)}, u32[]{:S(2)}) collective-permute-start(bf16[288,512]{1,0:T(8,128)(2,1)} %get-tuple-element.15), channel_id=1, source_target_pairs={{0,48},{16,0},{32,16},{48,32},{64,112},{80,64},{96,80},{112,96},{1... | collective-permute-start | bytes 884744 | tf_op jit(solution)/shard_map/ppermute | solution.py:79
  113.9 0.7 collective-permute-start.11
  124.4 0.7 collective-permute-start.12
  153.6 0.9 collective-permute-start.15
  163.5 0.7 collective-permute-start.16
  173.3 50.9 %collective-permute-start.17 = (bf16[288,512]{1,0:T(8,128)(2,1)}, bf16[288,512]{1,0:T(8,128)(2,1)}, u32[]{:S(2)}, u32[]{:S(2)}) collective-permute-start(bf16[288,512]{1,0:T(8,128)(2,1)} %fusion.44), channel_id=1, source_target_pairs={{64,0},{80,16},{96,32},{112,48},{65,1},{81,17},{97,33},{113,49},{6... | collective-permute-start | bytes 884744 | tf_op jit(solution)/shard_map/ppermute | solution.py:123
  237.5 13.5 %collective-permute-start.18 = (bf16[288,512]{1,0:T(8,128)(2,1)S(1)}, bf16[288,512]{1,0:T(8,128)(2,1)S(1)}, u32[]{:S(2)}, u32[]{:S(2)}) collective-permute-start(bf16[288,512]{1,0:T(8,128)(2,1)S(1)} %get-tuple-element.13), channel_id=1, source_target_pairs={{0,16},{16,32},{32,48},{48,0},{64,80},{80,96},{96,112},{112,64},{1... | collective-permute-start | bytes 884744 | tf_op jit(solution)/shard_map/ppermute | solution.py:79
  244.0 9.1 %collective-permute-start.19 = (bf16[288,512]{1,0:T(8,128)(2,1)S(1)}, bf16[288,512]{1,0:T(8,128)(2,1)S(1)}, u32[]{:S(2)}, u32[]{:S(2)}) collective-permute-start(bf16[288,512]{1,0:T(8,128)(2,1)S(1)} %get-tuple-element.12), channel_id=1, source_target_pairs={{0,32},{16,48},{32,0},{48,16},{64,96},{80,112},{96,64},{112,80},{1... | collective-permute-start | bytes 884744 | tf_op jit(solution)/shard_map/ppermute | solution.py:79
  247.7 8.5 %collective-permute-start.20 = (bf16[288,512]{1,0:T(8,128)(2,1)S(1)}, bf16[288,512]{1,0:T(8,128)(2,1)S(1)}, u32[]{:S(2)}, u32[]{:S(2)}) collective-permute-start(bf16[288,512]{1,0:T(8,128)(2,1)S(1)} %get-tuple-element.11), channel_id=1, source_target_pairs={{0,48},{16,0},{32,16},{48,32},{64,112},{80,64},{96,80},{112,96},{1... | collective-permute-start | bytes 884744 | tf_op jit(solution)/shard_map/ppermute | solution.py:79
  259.8 10.1 %collective-permute-start.21 = (bf16[2,2,4,32,512]{4,3,0,1,2:T(8,128)(2,1)S(1)}, bf16[2,2,4,32,512]{4,3,0,1,2:T(8,128)(2,1)}, u32[]{:S(2)}, u32[]{:S(2)}) collective-permute-start(bf16[2,2,4,32,512]{4,3,0,1,2:T(8,128)(2,1)S(1)} %fusion.67), channel_id=1, source_target_pairs={{0,1},{1,0},{2,3},{3,2},{4,5},{5,4},{6,7},{7,6},{8,9},{9,8},{10,11... | collective-permute-start | bytes 1572872 | tf_op jit(solution)/shard_map/ppermute | solution.py:89
  271.2 10.6 %collective-permute-start.22 = (bf16[2,2,32,512]{3,2,0,1:T(8,128)(2,1)S(1)}, bf16[2,2,32,512]{3,2,0,1:T(8,128)(2,1)S(1)}, u32[]{:S(2)}, u32[]{:S(2)}) collective-permute-start(bf16[2,2,32,512]{3,2,0,1:T(8,128)(2,1)S(1)} %get-tuple-element.19), channel_id=1, source_target_pairs={{0,2},{1,3},{2,4},{3,5},{4,6},{5,7},{6,0},{7,1},{8,10},{9,11},{10,... | collective-permute-start | bytes 393224 | tf_op jit(solution)/shard_map/ppermute | solution.py:93
  275.2 7.8 %collective-permute-start.23 = (bf16[2,2,32,512]{3,2,0,1:T(8,128)(2,1)S(1)}, bf16[2,2,32,512]{3,2,0,1:T(8,128)(2,1)S(1)}, u32[]{:S(2)}, u32[]{:S(2)}) collective-permute-start(bf16[2,2,32,512]{3,2,0,1:T(8,128)(2,1)S(1)} %get-tuple-element.21), channel_id=1, source_target_pairs={{0,4},{1,5},{2,6},{3,7},{4,0},{5,1},{6,2},{7,3},{8,12},{9,13},{10,... | collective-permute-start | bytes 393224 | tf_op jit(solution)/shard_map/ppermute | solution.py:93
  278.5 5.7 %collective-permute-start.24 = (bf16[2,2,32,512]{3,2,0,1:T(8,128)(2,1)S(1)}, bf16[2,2,32,512]{3,2,0,1:T(8,128)(2,1)S(1)}, u32[]{:S(2)}, u32[]{:S(2)}) collective-permute-start(bf16[2,2,32,512]{3,2,0,1:T(8,128)(2,1)S(1)} %get-tuple-element.20), channel_id=1, source_target_pairs={{0,6},{1,7},{2,0},{3,1},{4,2},{5,3},{6,4},{7,5},{8,14},{9,15},{10,... | collective-permute-start | bytes 393224 | tf_op jit(solution)/shard_map/ppermute | solution.py:93
  284.3 13.7 %collective-permute-start.25 = (bf16[2,32,512]{2,1,0:T(8,128)(2,1)S(1)}, bf16[2,32,512]{2,1,0:T(8,128)(2,1)S(1)}, u32[]{:S(2)}, u32[]{:S(2)}) collective-permute-start(bf16[2,32,512]{2,1,0:T(8,128)(2,1)S(1)} %fusion.80), channel_id=1, source_target_pairs={{0,8},{1,9},{2,10},{3,11},{4,12},{5,13},{6,14},{7,15},{8,0},{9,1},... | collective-permute-start | bytes 196616 | tf_op jit(solution)/shard_map/ppermute | solution.py:95
  (33 other events, 239.1 us)

commit v2 on v1

v2 whole, which is shorter than its diff:
```python
import functools

import jax
import jax.numpy as jnp
from jax import lax
from jax.experimental import pallas as pl
from jax.experimental.pallas import tpu as pltpu
from jax.sharding import PartitionSpec as P

RHO = 0.25
NY = 4
NZ = 8
NX = 4
VMEM_LIMIT = 32 * 1024 * 1024


def stage_route(source_z):
    return [(source_z * NY + y, (source_z - 1) * NY + y) for y in range(NY)]


def replica_route(step_zh, step_core):
    route = []
    for zh in range(2):
        for x in range(NX):
            for core in range(2):
                to = ((zh + step_zh) % 2, (core + step_core) % 2)
                route.append(((zh * NX + x) * 2 + core, (to[0] * NX + x) * 2 + to[1]))
    return route


def over_y(pieces):
    groups = [[z * NY + y for y in range(NY)] for z in range(NZ)]
    return lax.all_to_all(pieces, "section", 0, 0, axis_index_groups=groups)


def over_x(pieces):
    groups = [
        [(zh * NX + x) * 2 + core for x in range(NX)] for zh in range(2) for core in range(2)
    ]
    return lax.all_to_all(pieces, "dp", 0, 0, axis_index_groups=groups)


def dot(left, right, left_dim, right_dim):
    return lax.dot_general(
        left, right, (((left_dim,), (right_dim,)), ((), ())), preferred_element_type=jnp.float32
    )


def slope(z):
    sig = 1.0 / (1.0 + jnp.exp(-z))
    return RHO * sig * (1.0 + z * (1.0 - sig))


def call(kernel, out_shape, *operands, flops=0):
    whole = pl.BlockSpec(memory_space=pltpu.VMEM)
    specs = [
        pl.BlockSpec(memory_space=pltpu.SMEM) if o.dtype == jnp.int32 else whole for o in operands
    ]
    return pl.pallas_call(
        kernel,
        out_shape=out_shape,
        in_specs=specs,
        out_specs=jax.tree.map(lambda _: whole, out_shape),
        cost_estimate=pl.CostEstimate(flops=flops, bytes_accessed=0, transcendentals=0),
        compiler_params=pltpu.CompilerParams(vmem_limit_bytes=VMEM_LIMIT),
    )(*operands)


def prepare_kernel(lead, place, mine, other, arrived, weights, slopes):
    rows = mine.shape[4]
    own_at = place[1] * rows
    other_at = rows - own_at
    for s in reversed(range(NY)):
        for w in range(2):
            for zh in range(2):
                for x in range(NX):
                    base = (zh * NX + x) * 2 * rows
                    weights[s, w, pl.ds(pl.multiple_of(base + own_at, rows), rows)] = mine[x, s, zh, w]
                    weights[s, w, pl.ds(pl.multiple_of(base + other_at, rows), rows)] = other[x, s, zh, w]
        slopes[s] = slope(dot(arrived[s, lead:], weights[s, 0], 1, 0))


def stage_kernel(tick, place, arriving, weights, slopes, kept_in, kept, sending):
    last = tick == NZ - 1

    @pl.when(place[0] == NZ - 1 - tick)
    def _():
        g = arriving[...]
        for s in reversed(range(NY)):
            kept[s] = g
            if s == 0 and last:
                break
            dz = (dot(g, weights[s, 1], 1, 1) * slopes[s]).astype(jnp.bfloat16)
            g = (g.astype(jnp.float32) + dot(dz, weights[s, 0], 1, 1)).astype(jnp.bfloat16)
        if not last:
            sending[...] = g

    @pl.when(place[0] != NZ - 1 - tick)
    def _():
        kept[...] = kept_in[...]


def reduce_replicas(grads, zh, core):
    width = grads.shape[-1]
    rows = grads.shape[1] // (2 * NX * 2)
    parts = grads.reshape(2, 2, NX, 2, rows, width).transpose(2, 1, 0, 3, 4, 5)
    sent = lax.dynamic_index_in_dim(parts, 1 - core, 3, keepdims=False).astype(jnp.bfloat16)
    total = lax.dynamic_index_in_dim(parts, core, 3, keepdims=False)
    total = total + lax.ppermute(sent, "dp", replica_route(0, 1))
    total = over_x(total.astype(jnp.bfloat16)).astype(jnp.float32).sum(axis=0)
    sent = lax.dynamic_index_in_dim(total, 1 - zh, 0, keepdims=False).astype(jnp.bfloat16)
    own = lax.dynamic_index_in_dim(total, zh, 0, keepdims=False)
    return own + lax.ppermute(sent, "dp", replica_route(1, 0))


def body(section_inputs, cotangent, weight_in, weight_out):
    position = lax.axis_index("section")
    replica = lax.axis_index("dp")
    y = position % NY
    zh, core = replica // (2 * NX), replica % 2
    place = jnp.stack([position // NY, core]).astype(jnp.int32)
    micro, rows, width = section_inputs.shape[1:]
    shard = weight_in.shape[1]
    share = micro * rows // NY
    flat_x = section_inputs[0].reshape(micro * rows, width)

    own = jnp.concatenate([weight_in, weight_out], axis=0)
    other = lax.ppermute(own, "dp", replica_route(1, 0))
    both = jnp.where(zh == 0, jnp.stack([own, other]), jnp.stack([other, own]))
    lead = 4 * shard
    pieces = jnp.concatenate(
        [
            jnp.broadcast_to(both.reshape(1, lead, width), (NY, lead, width)),
            flat_x.reshape(NY, share, width),
        ],
        axis=1,
    )
    arrived = over_y(pieces)
    mine = over_x(jnp.broadcast_to(arrived[:, :lead].reshape(1, NY * lead, width), (NX, NY * lead, width)))
    mine = mine.reshape(NX, NY, 2, 2, shard, width)
    other = lax.ppermute(mine, "dp", replica_route(0, 1))
    weights, slopes = call(
        functools.partial(prepare_kernel, lead),
        (
            jax.ShapeDtypeStruct((NY, 2, width, width), jnp.bfloat16),
            jax.ShapeDtypeStruct((NY, share, width), jnp.float32),
        ),
        place,
        mine,
        other,
        arrived,
        flops=2 * NY * share * width * width,
    )

    arriving = lax.dynamic_index_in_dim(cotangent.reshape(NY, share, width), y, 0, keepdims=False)
    kept = jnp.zeros((NY, share, width), jnp.bfloat16)
    block = jax.ShapeDtypeStruct((share, width), jnp.bfloat16)
    home_at = NZ - 3
    for tick in range(NZ):
        kept, sending = call(
            functools.partial(stage_kernel, tick),
            (jax.ShapeDtypeStruct(kept.shape, kept.dtype), block),
            place,
            arriving,
            weights,
            slopes,
            kept,
            flops=4 * NY * share * width * width,
        )
        if tick == NZ - 1:
            break
        arriving = lax.ppermute(sending, "section", stage_route(NZ - 1 - tick))
        if tick == home_at:
            home_w = lax.dynamic_index_in_dim(weights, y, 0, keepdims=False)
            home_w, home_x, kept = lax.optimization_barrier((home_w, flat_x, kept))
            zed = dot(home_x, home_w[0], 1, 0)
            home_h = jax.nn.silu(zed).astype(jnp.bfloat16)
            home_slope = slope(zed)
            arriving, home_h, home_slope = lax.optimization_barrier((arriving, home_h, home_slope))

    home_g = over_y(kept).reshape(micro * rows, width)
    dz = (dot(home_g, home_w[1], 1, 1) * home_slope).astype(jnp.bfloat16)
    dx = (home_g.astype(jnp.float32) + dot(dz, home_w[0], 1, 1)).astype(jnp.bfloat16)
    grads = jnp.stack([dot(home_x, dz, 0, 0), RHO * dot(home_h, home_g, 0, 0)])
    factor = 4.0 / jnp.sqrt(jnp.float32(micro * rows * lax.axis_size("dp")))
    reduced = reduce_replicas(grads, zh, core) * factor
    return (reduced[0:1], reduced[1:2], dx.reshape(1, micro, rows, width))


def solution(mesh):
    return jax.shard_map(
        body,
        mesh=mesh,
        in_specs=(
            P("section", None, "dp", None),
            P(None, "dp", None),
            P("section", "dp", None),
            P("section", "dp", None),
        ),
        out_specs=(
            P("section", "dp", None),
            P("section", "dp", None),
            P("section", None, "dp", None),
        ),
        check_vma=False,
    )
```

time: 303 us -> 228 us (0.75); the launches traced: 299 us -> 227 us
  matrix products: 87 us -> 10.9 us
  blocking collectives: 0 us -> 47.4 us
  starting transfers between devices: 94 us -> 49.1 us
  local copies, waits for them, and re-layouts: 20.6 us -> 3.87 us
  waiting for transfers between devices: 84.8 us -> 97.9 us
  Pallas kernels: 0 us -> 11.3 us
  other arithmetic: 10.3 us -> 5.8 us
    dot_general x40 -> x5, matrix products: 87 us -> 10.9 us  [dot(): lax.dot_general(left, right, (((left_dim,), (right_dim,)), ((), ())), pre...]
    ppermute x26 -> x11, starting transfers between devices: 94 us -> 41.3 us  [the longest x1 16.3 us: body(): other = lax.ppermute(own, 'dp', replica_route(1, 0))]
    all_to_all x0 -> x2, blocking collectives: none -> 47.4 us  [the longest x1 25.1 us: over_x(): return lax.all_to_all(pieces, 'dp', 0, 0, axis_index_groups=groups)]
    all_to_all x0 -> x2, waiting for transfers between devices: none -> 19.7 us  [the longest x1 10.4 us: over_y(): return lax.all_to_all(pieces, 'section', 0, 0, axis_index_groups=groups)]
    dynamic_update_slice x16 -> x0, local copies, waits for them, and re-layouts: 11.4 us -> none  [put(): return lax.dynamic_update_index_in_dim(array, piece, index, axis)]
    pallas_call x0 -> x9, Pallas kernels: none -> 11.3 us  [call(): pl.pallas_call(kernel, out_shape=out_shape, in_specs=specs, out_specs=jax...]
    all_to_all x0 -> x2, starting transfers between devices: none -> 7.8 us  [the longest x1 4.27 us: over_x(): return lax.all_to_all(pieces, 'dp', 0, 0, axis_index_groups=groups)]
    ppermute x26 -> x11, waiting for transfers between devices: 84.8 us -> 78.2 us  [the longest x7 62.6 us: body(): arriving = lax.ppermute(sending, 'section', stage_route(NZ - 1 - tick))]
  transfers between devices with their start and end apart: 26 -> 13, of which waited for: 14 -> 7; matrix products, arithmetic and copies ran while one was open for 7% -> 3% of each run, Pallas kernels for 0% -> 0%
where the time goes in v2:
time: 228 us; the launch traced here: 227 us
  waiting for transfers between devices  97.9 us (43%)
  starting transfers between devices  49.1 us (22%)
  blocking collectives  47.4 us (21%)
  Pallas kernels  11.3 us (5%)
  matrix products  10.9 us (5%)
  other arithmetic  5.8 us (3%)
  local copies, waits for them, and re-layouts  3.87 us (2%)
    ppermute x7, waiting for transfers between devices, body(): arriving = lax.ppermute(sending, 'section', stage_route(NZ - 1 - tick))  62.6 us
    all_to_all x1, blocking collectives, over_x(): return lax.all_to_all(pieces, 'dp', 0, 0, axis_index_groups=groups)  25.1 us
    all_to_all x1, blocking collectives, over_y(): return lax.all_to_all(pieces, 'section', 0, 0, axis_index_groups=groups)  22.3 us
    ppermute x1, starting transfers between devices, body(): other = lax.ppermute(own, 'dp', replica_route(1, 0))  16.3 us
    pallas_call x9, Pallas kernels, call(): pl.pallas_call(kernel, out_shape=out_shape, in_specs=specs, out_specs=jax...  11.3 us
    dot_general x5, matrix products, dot(): lax.dot_general(left, right, (((left_dim,), (right_dim,)), ((), ())), pre...  10.9 us
    all_to_all x1, waiting for transfers between devices, over_y(): return lax.all_to_all(pieces, 'section', 0, 0, axis_index_groups=groups)  10.4 us
    all_to_all x1, waiting for transfers between devices, over_x(): return lax.all_to_all(pieces, 'dp', 0, 0, axis_index_groups=groups)  9.28 us
  transfers between devices with their start and end apart: 13, of which 7 were waited for; matrix products, arithmetic and copies ran while one was open for 3% of the time, Pallas kernels for 0%

profile of v2, /device:TPU:1, one launch (start us, length us, event | category | flops | bytes accessed | tf_op | source)
XLA Modules:
  0.0 227.4 jit_solution(9791896142067882332)
XLA Ops:
  2.3 16.3 %collective-permute-start = (bf16[2,32,512]{2,1,0:T(8,128)(2,1)S(1)}, bf16[2,32,512]{2,1,0:T(8,128)(2,1)S(1)}, u32[]{:S(2)}, u32[]{:S(2)}) collective-permute-start(bf16[2,32,512]{2,1,0:T(8,128)(2,1)S(1)} %constant_dynamic-update-slice_fusion), channel_id=1, source_target_pairs={{0,8},{1,9},{2,10},{3,11},{4,12},{5,13},{6,14},{7,15},{8,0},{9,1},... | collective-permute-start | bytes 196616 | tf_op jit(solution)/shard_map/ppermute | solution.py:128
  18.5 1.8 collective-permute-done
  20.4 1.4 pad_maximum_fusion
  21.8 22.3 %all_to_all.20.arrived = bf16[4,416,512]{2,1,0:T(8,128)(2,1)S(1)} all-to-all(bf16[4,416,512]{2,1,0:T(8,128)(2,1)S(1)} %pad_maximum_fusion), channel_id=1, replica_groups={{0,16,32,48},{64,80,96,112},{128,144,160,176},{192,208,224,240},{256,27..., dimensions={0} | all-to-all | bytes 3407872 | tf_op jit(solution)/shard_map/all_to_all | solution.py:33
  44.4 25.1 %all_to_all.21 = bf16[4,512,512]{2,1,0:T(8,128)(2,1)} all-to-all(bf16[4,512,512]{2,1,0:T(8,128)(2,1)S(1)} %broadcast_in_dim.17), channel_id=1, replica_groups={{0,2,4,6},{1,3,5,7},{8,10,12,14},{9,11,13,15},{16,18,20,22},{17,19,21,2..., dimensions={0} | all-to-all | bytes 4194304 | tf_op jit(solution)/shard_map/all_to_all | solution.py:40
  69.5 8.0 %collective-permute-start.1 = (bf16[4,4,2,2,32,512]{5,4,3,2,1,0:T(8,128)(2,1)}, bf16[4,4,2,2,32,512]{5,4,3,2,1,0:T(8,128)(2,1)}, u32[]{:S(2)}, u32[]{:S(2)}) collective-permute-start(bf16[4,4,2,2,32,512]{5,4,3,2,1,0:T(8,128)(2,1)} %bitcast.7.mine), channel_id=1, source_target_pairs={{0,1},{1,0},{2,3},{3,2},{4,5},{5,4},{6,7},{7,6},{8,9},{9,8},{10,11... | collective-permute-start | bytes 6291464 | tf_op jit(solution)/shard_map/ppermute | solution.py:141
  77.6 4.0 %collective-permute-done.1.other = bf16[4,4,2,2,32,512]{5,4,3,2,1,0:T(8,128)(2,1)} collective-permute-done((bf16[4,4,2,2,32,512]{5,4,3,2,1,0:T(8,128)(2,1)}, bf16[4,4,2,2,32,512]{5,4,3,2,1,0:T(8,128)(2,1)}, u32[]{:S(2)}, u32[]{:S(2)}) %collective-permute-start.1) | collective-permute-done | bytes 2097184 | tf_op jit(solution)/shard_map/ppermute | solution.py:141
  81.6 3.6 %shard_map.67 = (bf16[4,2,512,512]{3,2,1,0:T(8,128)(2,1)S(1)}, f32[4,288,512]{2,1,0:T(8,128)S(1)}) custom-call(s32[2]{0:T(128)S(1)} %pad_add_fusion.place, bf16[4,4,2,2,32,512]{5,4,3,2,1,0:T(8,128)(2,1)} %bitcast.7.mine, bf16[4,4,2,2,32,512]{5,4,3,2,1,0:T(8,128)(2,1)} %collective-permute-done.1.other, bf16[4,416,512]{2,1,0:T(8,128)(2,1)S(1)} %all_to_all.20.arrived), custom_call_target="tpu_custom_call" | custom-call | flops 603979776 | tf_op jit(solution)/shard_map/pallas_call | solution.py:59
  93.7 3.4 %add_multiply_fusion = (f32[1152,512]{1,0:T(8,128)}, bf16[1152,512]{1,0:T(8,128)(2,1)}) fusion(bf16[1152,512]{1,0:T(8,128)(2,1)S(1)} %bitcast.65, bf16[2,512,512]{2,1,0:T(8,128)(2,1)S(1)} %dynamic-slice_bitcast_fusion), kind=kOutput, calls=%fused_computation.7 | convolution fusion | flops 609878016 | bytes 5242880 | tf_op jit(solution)/shard_map/dot_general | solution.py:44
  98.0 1.3 collective-permute-start.8
  99.3 62.6 %collective-permute-done.8.arriving = bf16[288,512]{1,0:T(8,128)(2,1)S(1)} collective-permute-done((bf16[288,512]{1,0:T(8,128)(2,1)S(1)}, bf16[288,512]{1,0:T(8,128)(2,1)S(1)}, u32[]{:S(2)}, u32[]{:S(2)}) %collective-permute-start.8) | collective-permute-done | bytes 294944 | tf_op jit(solution)/shard_map/ppermute | solution.py:172
  161.9 3.1 %shard_map.75 = (bf16[4,288,512]{2,1,0:T(8,128)(2,1)}, bf16[288,512]{1,0:T(8,128)(2,1)}) custom-call(s32[2]{0:T(128)S(1)} %pad_add_fusion.place, bf16[288,512]{1,0:T(8,128)(2,1)S(1)} %collective-permute-done.8.arriving, bf16[4,2,512,512]{3,2,1,0:T(8,128)(2,1)S(1)} %get-tuple-element.26.weights, f32[4,288,512]{2,1,0:T(8,128)S(1)} %get-tuple-element.27.slopes, ...), custom_call_target="tpu_custom_call" | custom-call | flops 1207959552 | tf_op jit(solution)/shard_map/pallas_call | solution.py:59
  165.0 3.5 %all-to-all-start.2 = ((bf16[4,288,512]{2,1,0:T(8,128)(2,1)}), bf16[4,288,512]{2,1,0:T(8,128)(2,1)S(1)}, u32[]{:S(2)}, u32[]{:S(2)}) async-start(bf16[4,288,512]{2,1,0:T(8,128)(2,1)} %get-tuple-element.46), calls=%async_computation.2 | async-start | bytes 2359296 | tf_op jit(solution)/shard_map/all_to_all | solution.py:33
  168.6 10.4 %all-to-all-done.2 = bf16[4,288,512]{2,1,0:T(8,128)(2,1)S(1)} async-done(((bf16[4,288,512]{2,1,0:T(8,128)(2,1)}), bf16[4,288,512]{2,1,0:T(8,128)(2,1)S(1)}, u32[]{:S(2)}, u32[]{:S(2)}) %all-to-all-start.2) | async-done | bytes 1179680 | tf_op jit(solution)/shard_map/all_to_all | solution.py:33
  179.0 2.6 %fusion = bf16[1152,512]{1,0:T(8,128)(2,1)S(1)} fusion(f32[1152,512]{1,0:T(8,128)} %get-tuple-element.47, bf16[1152,512]{1,0:T(8,128)(2,1)S(1)} %bitcast.56, bf16[2,512,512]{2,1,0:T(8,128)(2,1)S(1)} %dynamic-slice_bitcast_fusion), kind=kOutput, calls=%fused_computation.1 | convolution fusion | flops 605159424 | bytes 5242880 | tf_op jit(solution)/shard_map/dot_general | solution.py:44
  185.3 8.9 %collective-permute-start.9 = (bf16[4,2,2,32,512]{4,3,1,2,0:T(8,128)(2,1)}, bf16[4,2,2,32,512]{4,3,1,2,0:T(8,128)(2,1)}, u32[]{:S(2)}, u32[]{:S(2)}) collective-permute-start(bf16[4,2,2,32,512]{4,3,1,2,0:T(8,128)(2,1)} %fusion.5), channel_id=1, source_target_pairs={{0,1},{1,0},{2,3},{3,2},{4,5},{5,4},{6,7},{7,6},{8,9},{9,8},{10,11... | collective-permute-start | bytes 1572872 | tf_op jit(solution)/shard_map/ppermute | solution.py:109
  194.2 1.8 collective-permute-done.9
  196.1 2.2 fusion.4
  198.2 4.3 %all-to-all-start.3 = ((bf16[4,2,2,32,512]{4,3,1,2,0:T(8,128)(2,1)}), bf16[4,2,2,32,512]{4,3,1,2,0:T(8,128)(2,1)}, u32[]{:S(2)}, u32[]{:S(2)}) async-start(bf16[4,2,2,32,512]{4,3,1,2,0:T(8,128)(2,1)} %fusion.4), calls=%async_computation.3 | async-start | bytes 1048576 | tf_op jit(solution)/shard_map/all_to_all | solution.py:40
  202.5 9.3 %all-to-all-done.3 = bf16[4,2,2,32,512]{4,3,1,2,0:T(8,128)(2,1)} async-done(((bf16[4,2,2,32,512]{4,3,1,2,0:T(8,128)(2,1)}), bf16[4,2,2,32,512]{4,3,1,2,0:T(8,128)(2,1)}, u32[]{:S(2)}, u32[]{:S(2)}) %all-to-all-start.3) | async-done | bytes 524320 | tf_op jit(solution)/shard_map/all_to_all | solution.py:40
  211.8 1.1 convert_reduce_fusion
  213.0 2.7 %collective-permute-start.10 = (bf16[2,32,512]{2,1,0:T(8,128)(2,1)S(1)}, bf16[2,32,512]{2,1,0:T(8,128)(2,1)S(1)}, u32[]{:S(2)}, u32[]{:S(2)}) collective-permute-start(bf16[2,32,512]{2,1,0:T(8,128)(2,1)S(1)} %fusion.17), channel_id=1, source_target_pairs={{0,8},{1,9},{2,10},{3,11},{4,12},{5,13},{6,14},{7,15},{8,0},{9,1},... | collective-permute-start | bytes 196616 | tf_op jit(solution)/shard_map/ppermute | solution.py:113
  215.6 3.1 %add_convert_fusion = bf16[1152,512]{1,0:T(8,128)(2,1)} fusion(bf16[1152,512]{1,0:T(8,128)(2,1)S(1)} %bitcast.58, bf16[1152,512]{1,0:T(8,128)(2,1)} %copy-done.4, bf16[2,512,512]{2,1,0:T(8,128)(2,1)S(1)} %copy-done.3), kind=kOutput, calls=%fused_computation.6 | convolution fusion | flops 605749248 | bytes 4063232 | tf_op jit(solution)/shard_map/dot_general | solution.py:44
  218.7 7.9 %collective-permute-done.10 = bf16[2,32,512]{2,1,0:T(8,128)(2,1)S(1)} collective-permute-done((bf16[2,32,512]{2,1,0:T(8,128)(2,1)S(1)}, bf16[2,32,512]{2,1,0:T(8,128)(2,1)S(1)}, u32[]{:S(2)}, u32[]{:S(2)}) %collective-permute-start.10) | collective-permute-done | bytes 65568 | tf_op jit(solution)/shard_map/ppermute | solution.py:113
  (51 shorter events, 15.5 us)
Async XLA Ops:
  0.6 77.0 %copy-start = (bf16[12,96,512]{2,1,0:T(8,128)(2,1)S(1)}, bf16[12,96,512]{2,1,0:T(8,128)(2,1)}, u32[]{:S(2)}) copy-start(bf16[12,96,512]{2,1,0:T(8,128)(2,1)} %param.5) | copy-start | bytes 3538948
  2.3 18.1 %collective-permute-start = (bf16[2,32,512]{2,1,0:T(8,128)(2,1)S(1)}, bf16[2,32,512]{2,1,0:T(8,128)(2,1)S(1)}, u32[]{:S(2)}, u32[]{:S(2)}) collective-permute-start(bf16[2,32,512]{2,1,0:T(8,128)(2,1)S(1)} %constant_dynamic-update-slice_fusion), channel_id=1, source_target_pairs={{0,8},{1,9},{2,10},{3,11},{4,12},{5,13},{6,14},{7,15},{8,0},{9,1},... | collective-permute-start | bytes 196616 | tf_op jit(solution)/shard_map/ppermute | solution.py:128
  69.5 12.1 %collective-permute-start.1 = (bf16[4,4,2,2,32,512]{5,4,3,2,1,0:T(8,128)(2,1)}, bf16[4,4,2,2,32,512]{5,4,3,2,1,0:T(8,128)(2,1)}, u32[]{:S(2)}, u32[]{:S(2)}) collective-permute-start(bf16[4,4,2,2,32,512]{5,4,3,2,1,0:T(8,128)(2,1)} %bitcast.7.mine), channel_id=1, source_target_pairs={{0,1},{1,0},{2,3},{3,2},{4,5},{5,4},{6,7},{7,6},{8,9},{9,8},{10,11... | collective-permute-start | bytes 6291464 | tf_op jit(solution)/shard_map/ppermute | solution.py:141
  86.0 0.7 collective-permute-start.2
  87.3 0.7 collective-permute-start.3
  88.6 0.7 collective-permute-start.4
  90.0 0.7 collective-permute-start.5
  91.3 0.8 collective-permute-start.6
  92.1 86.9 %copy-start.2 = (bf16[2,512,512]{2,1,0:T(8,128)(2,1)}, bf16[2,512,512]{2,1,0:T(8,128)(2,1)S(1)}, u32[]{:S(2)}) copy-start(bf16[2,512,512]{2,1,0:T(8,128)(2,1)S(1)} %dynamic-slice_bitcast_fusion) | copy-start | bytes 3145732
  92.1 1.6 copy-start.5
  92.7 4.4 %collective-permute-start.7 = (bf16[288,512]{1,0:T(8,128)(2,1)S(1)}, bf16[288,512]{1,0:T(8,128)(2,1)S(1)}, u32[]{:S(2)}, u32[]{:S(2)}) collective-permute-start(bf16[288,512]{1,0:T(8,128)(2,1)S(1)} %get-tuple-element.40), channel_id=1, source_target_pairs={{128,64},{144,80},{160,96},{176,112},{129,65},{145,81},{161,97},{1... | collective-permute-start | bytes 884744 | tf_op jit(solution)/shard_map/ppermute | solution.py:172
  98.0 63.9 %collective-permute-start.8 = (bf16[288,512]{1,0:T(8,128)(2,1)S(1)}, bf16[288,512]{1,0:T(8,128)(2,1)S(1)}, u32[]{:S(2)}, u32[]{:S(2)}) collective-permute-start(bf16[288,512]{1,0:T(8,128)(2,1)S(1)} %get-tuple-element.44), channel_id=1, source_target_pairs={{64,0},{80,16},{96,32},{112,48},{65,1},{81,17},{97,33},{113,49},{6... | collective-permute-start | bytes 884744 | tf_op jit(solution)/shard_map/ppermute | solution.py:172
  165.0 14.0 %all-to-all-start.2 = ((bf16[4,288,512]{2,1,0:T(8,128)(2,1)}), bf16[4,288,512]{2,1,0:T(8,128)(2,1)S(1)}, u32[]{:S(2)}, u32[]{:S(2)}) async-start(bf16[4,288,512]{2,1,0:T(8,128)(2,1)} %get-tuple-element.46), calls=%async_computation.2 | async-start | bytes 2359296 | tf_op jit(solution)/shard_map/all_to_all | solution.py:33
  179.0 2.6 %copy-start.7 = (bf16[1152,512]{1,0:T(8,128)(2,1)S(1)}, bf16[1152,512]{1,0:T(8,128)(2,1)}, u32[]{:S(2)}) copy-start(bf16[1152,512]{1,0:T(8,128)(2,1)} %get-tuple-element.48) | copy-start | bytes 3538948
  181.6 1.0 copy-start.4
  181.6 1.7 copy-start.6
  184.2 1.1 copy-start.1
  185.3 10.7 %collective-permute-start.9 = (bf16[4,2,2,32,512]{4,3,1,2,0:T(8,128)(2,1)}, bf16[4,2,2,32,512]{4,3,1,2,0:T(8,128)(2,1)}, u32[]{:S(2)}, u32[]{:S(2)}) collective-permute-start(bf16[4,2,2,32,512]{4,3,1,2,0:T(8,128)(2,1)} %fusion.5), channel_id=1, source_target_pairs={{0,1},{1,0},{2,3},{3,2},{4,5},{5,4},{6,7},{7,6},{8,9},{9,8},{10,11... | collective-permute-start | bytes 1572872 | tf_op jit(solution)/shard_map/ppermute | solution.py:109
  198.2 17.4 %copy-start.3 = (bf16[2,512,512]{2,1,0:T(8,128)(2,1)S(1)}, bf16[2,512,512]{2,1,0:T(8,128)(2,1)}, u32[]{:S(2)}) copy-start(bf16[2,512,512]{2,1,0:T(8,128)(2,1)} %copy-done.2) | copy-start | bytes 3145732
  198.2 13.6 %all-to-all-start.3 = ((bf16[4,2,2,32,512]{4,3,1,2,0:T(8,128)(2,1)}), bf16[4,2,2,32,512]{4,3,1,2,0:T(8,128)(2,1)}, u32[]{:S(2)}, u32[]{:S(2)}) async-start(bf16[4,2,2,32,512]{4,3,1,2,0:T(8,128)(2,1)} %fusion.4), calls=%async_computation.3 | async-start | bytes 1048576 | tf_op jit(solution)/shard_map/all_to_all | solution.py:40
  213.0 13.7 %collective-permute-start.10 = (bf16[2,32,512]{2,1,0:T(8,128)(2,1)S(1)}, bf16[2,32,512]{2,1,0:T(8,128)(2,1)S(1)}, u32[]{:S(2)}, u32[]{:S(2)}) collective-permute-start(bf16[2,32,512]{2,1,0:T(8,128)(2,1)S(1)} %fusion.17), channel_id=1, source_target_pairs={{0,8},{1,9},{2,10},{3,11},{4,12},{5,13},{6,14},{7,15},{8,0},{9,1},... | collective-permute-start | bytes 196616 | tf_op jit(solution)/shard_map/ppermute | solution.py:113

commit v3 on v0

v3 whole, which is shorter than its diff:
```python
import functools

import jax
import jax.numpy as jnp
from jax import lax
from jax.experimental import pallas as pl
from jax.experimental.pallas import tpu as pltpu
from jax.sharding import Mesh
from jax.sharding import PartitionSpec as P

RHO = 0.25
NZ, NY, NH, NX, NC = 8, 4, 2, 4, 2
AXES = ("z_lo", "y", "z_hi", "x", "core")
PLANE = ("y", "x")
CHUNKS = 2
HOME_AT = NZ - 3
MIB = 1024 * 1024
BF16, F32 = jnp.bfloat16, jnp.float32
SWAP = [(0, 1), (1, 0)]


def struct(shape, dtype):
    return jax.ShapeDtypeStruct(shape, dtype)


def dot(left, right, left_dim, right_dim):
    return lax.dot_general(
        left, right, (((left_dim,), (right_dim,)), ((), ())), preferred_element_type=F32
    )


def slope(z):
    sig = 1.0 / (1.0 + jnp.exp(-z))
    return RHO * sig * (1.0 + z * (1.0 - sig))


def skip_first(kernel, _, *refs):
    kernel(*refs)


def call(kernel, out_shape, *operands, after=None, scratch=(), vmem=32, flops=0):
    whole = pl.BlockSpec(memory_space=pltpu.VMEM)
    specs = [
        pl.BlockSpec(memory_space=pltpu.SMEM) if o.dtype == jnp.int32 else whole for o in operands
    ]
    if after is not None:
        operands, specs = (after, *operands), [pl.BlockSpec(memory_space=pl.ANY), *specs]
        kernel = functools.partial(skip_first, kernel)
    return pl.pallas_call(
        kernel,
        out_shape=out_shape,
        in_specs=specs,
        out_specs=jax.tree.map(lambda _: whole, out_shape),
        scratch_shapes=list(scratch),
        cost_estimate=pl.CostEstimate(flops=flops, bytes_accessed=0, transcendentals=0),
        compiler_params=pltpu.CompilerParams(vmem_limit_bytes=vmem * MIB),
    )(*operands)


def prepare_kernel(place, mine, other, inputs, weights, slopes):
    rows = mine.shape[4]
    near_at = place[2] * (NX * NC * rows)
    far_at = NX * NC * rows - near_at
    mine_at = place[1] * rows
    other_at = rows - mine_at
    for s in reversed(range(NY)):
        for source, core_at in ((mine, mine_at), (other, other_at)):
            for half, half_at in enumerate((near_at, far_at)):
                for x in range(NX):
                    at = pl.multiple_of(half_at + x * NC * rows + core_at, rows)
                    for w in range(2):
                        weights[s, w, pl.ds(at, rows)] = source[s, x, half, w]
        slopes[s] = slope(dot(inputs[s], weights[s, 0], 1, 0))


def stage_kernel(stage, chunk, place, arriving, weights, slopes, kept_in, *rest):
    last = stage == NZ - 1
    joined = last and chunk == CHUNKS - 1
    earlier, outs = rest[: chunk if joined else 0], rest[chunk if joined else 0 :]
    part = arriving.shape[0]
    own = pl.ds(chunk * part, part)
    into = own if joined else pl.ds(0, part)
    for m, rows in enumerate(earlier):
        for s in range(NY):
            outs[0][s, pl.ds(m * part, part)] = rows[s]

    @pl.when(place[0] == NZ - 1 - stage)
    def _():
        g = arriving[...]
        for s in reversed(range(NY)):
            outs[0][s, into] = g
            if s == 0 and last:
                break
            dz = (dot(g, weights[s, 1], 1, 1) * slopes[s, own]).astype(BF16)
            g = (g.astype(F32) + dot(dz, weights[s, 0], 1, 1)).astype(BF16)
        if not last:
            outs[1][...] = g

    @pl.when(place[0] != NZ - 1 - stage)
    def _():
        for s in range(NY):
            outs[0][s, into] = kept_in[s]


def home_kernel(place, home_g, weights, slopes, inputs_t, h_t, dz, sent, own, grad):
    part = home_g.shape[0] // NY
    for block in range(NY):
        at = pl.ds(block * part, part)
        dz[at] = (dot(home_g[at], weights[1], 1, 1) * slopes[at]).astype(BF16)
    rows = sent.shape[3]
    for w, (left, right) in enumerate(((inputs_t, dz), (h_t, home_g))):
        product = dot(left[...], right[...], 1, 0)
        grad[...] = product * RHO if w else product
        for x in range(NX):
            for zh in range(NH):
                base = (zh * NX + x) * NC * rows
                at = pl.multiple_of(base + place[1] * rows, rows)
                own[x, zh, w] = grad[pl.ds(at, rows)]
                at = pl.multiple_of(base + (1 - place[1]) * rows, rows)
                sent[x, zh, w] = grad[pl.ds(at, rows)].astype(BF16)


def reduce_replicas(sent, own, zh):
    total = own + lax.ppermute(sent, "core", SWAP)
    total = lax.all_to_all(total.astype(BF16), "x", 0, 0).astype(F32).sum(axis=0)
    sent = lax.dynamic_index_in_dim(total, 1 - zh, 0, keepdims=False).astype(BF16)
    own = lax.dynamic_index_in_dim(total, zh, 0, keepdims=False)
    return own + lax.ppermute(sent, "z_hi", SWAP)


def body(section_inputs, cotangent, weight_in, weight_out):
    z, y, zh, _, core = (lax.axis_index(axis) for axis in AXES)
    place = jnp.stack([z, core, zh]).astype(jnp.int32)
    micro, rows, width = section_inputs.shape[1:]
    shard = weight_in.shape[1]
    share = micro * rows // NY
    part = share // CHUNKS
    flat_x = section_inputs.reshape(micro * rows, width)

    stage_x = lax.all_to_all(flat_x.reshape(NY, share, width), "y", 0, 0)
    own = jnp.concatenate([weight_in, weight_out], axis=0)
    far = lax.ppermute(own, "z_hi", SWAP)
    far, stage_x = lax.optimization_barrier((far, stage_x))
    block = jnp.concatenate([own, far], axis=0).reshape(1, 4 * shard, width)
    block = jnp.broadcast_to(block, (NY * NX, 4 * shard, width))
    mine = lax.all_to_all(block, PLANE, 0, 0).reshape(NY, NX, 2, 2, shard, width)
    other = lax.ppermute(mine, "core", SWAP)
    weights, slopes = call(
        prepare_kernel,
        (struct((NY, 2, width, width), BF16), struct((NY, share, width), F32)),
        place,
        mine,
        other,
        stage_x,
        flops=2 * NY * share * width * width,
    )

    given = lax.dynamic_index_in_dim(cotangent.reshape(NY, share, width), y, 0, keepdims=False)
    arriving = [given[m * part : (m + 1) * part] for m in range(CHUNKS)]
    kept = [jnp.zeros((NY, part, width), BF16) for _ in range(CHUNKS)]
    sending = None
    for stage in range(NZ):
        for m in range(CHUNKS):
            joined = stage == NZ - 1 and m == CHUNKS - 1
            outs = [struct((NY, share if joined else part, width), BF16)]
            if stage < NZ - 1:
                outs.append(struct((part, width), BF16))
            result = call(
                functools.partial(stage_kernel, stage, m),
                tuple(outs),
                place,
                arriving[m],
                weights,
                slopes,
                kept[m],
                *(kept[:m] if joined else ()),
                after=sending,
                flops=4 * NY * part * width * width,
            )
            kept[m] = result[0]
            if stage < NZ - 1:
                sending = result[1]
                arriving[m] = lax.ppermute(sending, "z_lo", [(NZ - 1 - stage, NZ - 2 - stage)])
        if stage == HOME_AT:
            home_w = lax.dynamic_index_in_dim(weights, y, 0, keepdims=False)
            home_w, home_x, _ = lax.optimization_barrier((home_w, flat_x, sending))
            home_slope = slope(dot(home_x, home_w[0], 1, 0))
            home_ht = jax.nn.silu(dot(home_w[0], home_x, 0, 1)).astype(BF16)
            home_xt = home_x.T
            arriving[0], home_slope, home_ht, home_xt, home_w = lax.optimization_barrier(
                (arriving[0], home_slope, home_ht, home_xt, home_w)
            )

    home_g = lax.all_to_all(kept[-1], "y", 0, 0).reshape(micro * rows, width)
    half = (NX, NH, 2, shard, width)
    dz, sent, own = call(
        home_kernel,
        (struct(home_g.shape, BF16), struct(half, BF16), struct(half, F32)),
        place,
        home_g,
        home_w,
        home_slope,
        home_xt,
        home_ht,
        scratch=[pltpu.VMEM((width, width), F32)],
        flops=6 * micro * rows * width * width,
    )
    dx = (home_g.astype(F32) + dot(dz, home_w[0], 1, 1)).astype(BF16)
    factor = 4.0 / jnp.sqrt(F32(micro * rows * NH * NX * NC))
    reduced = reduce_replicas(sent, own, zh) * factor
    return (reduced[0:1], reduced[1:2], dx.reshape(1, micro, rows, width))


def solution(mesh):
    named = Mesh(mesh.devices.reshape(NZ, NY, NH, NX, NC), AXES)
    section, dp = ("z_lo", "y"), ("z_hi", "x", "core")
    return jax.shard_map(
        body,
        mesh=named,
        in_specs=(
            P(section, None, dp, None),
            P(None, dp, None),
            P(section, dp, None),
            P(section, dp, None),
        ),
        out_specs=(
            P(section, dp, None),
            P(section, dp, None),
            P(section, None, dp, None),
        ),
        check_vma=False,
    )
```

time: 819 us -> 199 us (0.24)
  waiting for transfers between devices: 590 us -> 51.2 us
  blocking collectives: 90.9 us -> 44.5 us
  matrix products: 47.2 us -> 6.8 us
  Pallas kernels: 0 us -> 20.2 us
  between operations: 14.1 us -> 1.15 us
  other arithmetic: 13.8 us -> 2.22 us
  local copies, waits for them, and re-layouts: 2.9 us -> 11.8 us
    ppermute x43 -> x18, waiting for transfers between devices: 349 us -> 41.9 us  [the longest x14 30.3 us: body(): lax.ppermute(sending, 'z_lo', [(NZ - 1 - stage, NZ - 2 - stage)])]
    reduce_scatter x2 -> x0, waiting for transfers between devices: 241 us -> none  [the longest x1 138 us: body(): lax.psum_scatter(grad_b[None], 'dp', scatter_dimension=1, tiled=True)]
    all_gather x2 -> x0, blocking collectives: 90.9 us -> none  [the longest x1 52.4 us: body(): lax.all_gather(weight_in, 'dp', axis=1, tiled=True)]
    all_to_all x0 -> x2, blocking collectives: none -> 44.5 us  [the longest x1 31.5 us: body(): lax.all_to_all(block, PLANE, 0, 0).reshape(NY, NX, 2, 2, shard, width)]
    dot_general x60 -> x3, matrix products: 47.2 us -> 6.8 us  [dot(): lax.dot_general(left, right, (((left_dim,), (right_dim,)), ((), ())), pre...]
    pallas_call x0 -> x18, Pallas kernels: none -> 20.2 us  [call(): pl.pallas_call(kernel, out_shape=out_shape, in_specs=specs, out_specs=jax...]
    select_n x12 -> x0, other arithmetic: 10.9 us -> none  [tick(): g = jnp.where(is_last, given, arriving)]
    all_to_all x0 -> x2, starting transfers between devices: none -> 9.3 us  [the longest x1 5.16 us: body(): stage_x = lax.all_to_all(flat_x.reshape(NY, share, width), 'y', 0, 0)]
  transfers between devices with their start and end apart: 45 -> 20, of which waited for: 45 -> 7; matrix products, arithmetic and copies ran while one was open for 0% -> 5% of each run, Pallas kernels for 0% -> 6%
where the time goes in v3:
time: 199 us
  starting transfers between devices  60.8 us (31%)
  waiting for transfers between devices  51.2 us (26%)
  blocking collectives  44.5 us (22%)
  Pallas kernels  20.2 us (10%)
  local copies, waits for them, and re-layouts  11.8 us (6%)
  matrix products  6.8 us (3%)
  other arithmetic  2.22 us (1%)
    all_to_all x1, blocking collectives, body(): lax.all_to_all(block, PLANE, 0, 0).reshape(NY, NX, 2, 2, shard, width)  31.5 us
    ppermute x14, waiting for transfers between devices, body(): lax.ppermute(sending, 'z_lo', [(NZ - 1 - stage, NZ - 2 - stage)])  30.3 us
    pallas_call x18, Pallas kernels, call(): pl.pallas_call(kernel, out_shape=out_shape, in_specs=specs, out_specs=jax...  20.2 us
    ppermute x1, starting transfers between devices, body(): far = lax.ppermute(own, 'z_hi', SWAP)  15.4 us
    all_to_all x1, blocking collectives, body(): home_g = lax.all_to_all(kept[-1], 'y', 0, 0).reshape(micro * rows, width)  13 us
    ppermute x14, starting transfers between devices, body(): lax.ppermute(sending, 'z_lo', [(NZ - 1 - stage, NZ - 2 - stage)])  11.9 us
    ppermute x1, starting transfers between devices, reduce_replicas(): total = own + lax.ppermute(sent, 'core', SWAP)  11.8 us
    all_to_all x1, waiting for transfers between devices, reduce_replicas(): lax.all_to_all(total.astype(BF16), 'x', 0, 0).astype(F32).sum(axis=0)  9.29 us
  transfers between devices with their start and end apart: 20, of which 7 were waited for; matrix products, arithmetic and copies ran while one was open for 5% of the time, Pallas kernels for 6%

profile of v3, /device:TPU:1, one launch (start us, length us, event | category | flops | bytes accessed | tf_op | source)
XLA Modules:
  0.0 198.6 jit_solution(10123288498118344961)
XLA Ops:
  0.7 5.2 %all-to-all-start = ((bf16[4,288,512]{2,1,0:T(8,128)(2,1)}), bf16[4,288,512]{2,1,0:T(8,128)(2,1)S(1)}, u32[]{:S(2)}, u32[]{:S(2)}) async-start(bf16[4,288,512]{2,1,0:T(8,128)(2,1)} %bitcast.45), calls=%async_computation | async-start | bytes 2359296 | tf_op jit(solution)/shard_map/all_to_all | solution.py:140
  5.8 15.4 %collective-permute-start = (bf16[2,32,512]{2,1,0:T(8,128)(2,1)S(1)}, bf16[2,32,512]{2,1,0:T(8,128)(2,1)S(1)}, u32[]{:S(2)}, u32[]{:S(2)}) collective-permute-start(bf16[2,32,512]{2,1,0:T(8,128)(2,1)S(1)} %pad_maximum_fusion.1), channel_id=1, source_target_pairs={{0,8},{8,0},{1,9},{9,1},{2,10},{10,2},{3,11},{11,3},{4,12},{12,4},... | collective-permute-start | bytes 196616 | tf_op jit(solution)/shard_map/ppermute | solution.py:142
  21.3 1.8 collective-permute-done
  23.3 31.5 %all_to_all.20 = bf16[16,128,512]{2,1,0:T(8,128)(2,1)S(1)} all-to-all(bf16[16,128,512]{2,1,0:T(8,128)(2,1)S(1)} %broadcast_in_dim.8), channel_id=1, replica_groups=mesh['z_lo'=8,'y'=4,'z_hi'=2,'x'=4,'core'=2] {'y','x'}, dimensions={0} | all-to-all | bytes 4194304 | tf_op jit(solution)/shard_map/all_to_all | solution.py:146
  54.8 6.6 %collective-permute-start.1 = (bf16[4,4,2,2,32,512]{5,4,3,2,1,0:T(8,128)(2,1)S(1)}, bf16[4,4,2,2,32,512]{5,4,3,2,1,0:T(8,128)(2,1)}, u32[]{:S(2)}, u32[]{:S(2)}) collective-permute-start(bf16[4,4,2,2,32,512]{5,4,3,2,1,0:T(8,128)(2,1)S(1)} %bitcast.40), channel_id=1, source_target_pairs={{0,1},{1,0},{2,3},{3,2},{4,5},{5,4},{6,7},{7,6},{8,9},{9,8},{10,11... | collective-permute-start | bytes 6291464 | tf_op jit(solution)/shard_map/ppermute | solution.py:147
  65.2 1.6 copy-done.3
  66.8 3.0 %shard_map.67 = (bf16[4,2,512,512]{3,2,1,0:T(8,128)(2,1)S(1)}, f32[4,288,512]{2,1,0:T(8,128)S(1)}) custom-call(s32[3]{0:T(128)S(1)} %pad_add_fusion.place.refs_0_, bf16[4,4,2,2,32,512]{5,4,3,2,1,0:T(8,128)(2,1)S(1)} %bitcast.41, bf16[4,4,2,2,32,512]{5,4,3,2,1,0:T(8,128)(2,1)} %collective-permute-done.1.other, bf16[4,288,512]{2,1,0:T(8,128)(2,1)S(1)} %all-to-all-done.inputs), custom_call_target="tpu_custom_call" | custom-call | flops 603979776 | tf_op jit(solution)/shard_map/pallas_call | solution.py:49
  89.1 2.9 %add_multiply_fusion.slopes = f32[1152,512]{1,0:T(8,128)} fusion(bf16[1152,512]{1,0:T(8,128)(2,1)S(1)} %bitcast.47, bf16[2,512,512]{2,1,0:T(8,128)(2,1)S(1)} %dynamic-slice_bitcast_fusion.weights), kind=kOutput, calls=%fused_computation.2 | convolution fusion | flops 608698368 | bytes 4063232 | tf_op jit(solution)/shard_map/dot_general | solution.py:27
  91.9 2.1 %multiply_convert_fusion.h_t = bf16[512,1152]{1,0:T(8,128)(2,1)} fusion(bf16[1152,512]{1,0:T(8,128)(2,1)S(1)} %bitcast.48, bf16[2,512,512]{2,1,0:T(8,128)(2,1)S(1)} %dynamic-slice_bitcast_fusion.weights), kind=kOutput, calls=%fused_computation.1 | convolution fusion | flops 606928896 | bytes 2883584 | tf_op jit(solution)/shard_map/dot_general | solution.py:27
  94.0 1.7 copy.8
  95.7 2.2 %copy-done.1 = bf16[4,2,512,512]{3,2,1,0:T(8,128)(2,1)S(1)} copy-done((bf16[4,2,512,512]{3,2,1,0:T(8,128)(2,1)S(1)}, bf16[4,2,512,512]{3,2,1,0:T(8,128)(2,1)}, u32[]{:S(2)}) %copy-start.1) | copy-done | bytes 4194328
  103.6 28.1 %collective-permute-done.15.refs_1_ = bf16[144,512]{1,0:T(8,128)(2,1)S(1)} collective-permute-done((bf16[144,512]{1,0:T(8,128)(2,1)S(1)}, bf16[144,512]{1,0:T(8,128)(2,1)S(1)}, u32[]{:S(2)}, u32[]{:S(2)}) %collective-permute-start.15) | collective-permute-done | bytes 147488 | tf_op jit(solution)/shard_map/ppermute | solution.py:183
  131.7 1.9 shard_map.82.refs_5_
  133.6 2.1 %collective-permute-done.14.refs_1_ = bf16[144,512]{1,0:T(8,128)(2,1)S(1)} collective-permute-done((bf16[144,512]{1,0:T(8,128)(2,1)S(1)}, bf16[144,512]{1,0:T(8,128)(2,1)S(1)}, u32[]{:S(2)}, u32[]{:S(2)}) %collective-permute-start.14) | collective-permute-done | bytes 147488 | tf_op jit(solution)/shard_map/ppermute | solution.py:183
  135.8 1.9 shard_map.83
  137.7 13.0 %all_to_all.21 = bf16[4,288,512]{2,1,0:T(8,128)(2,1)S(1)} all-to-all(bf16[4,288,512]{2,1,0:T(8,128)(2,1)S(1)} %shard_map.83), channel_id=1, replica_groups=mesh['z_lo'=8,'y'=4,'z_hi'=2,'x'=4,'core'=2] {'y'}, dimensions={0} | all-to-all | bytes 2359296 | tf_op jit(solution)/shard_map/all_to_all | solution.py:194
  150.8 2.8 %shard_map.84 = (bf16[1152,512]{1,0:T(8,128)(2,1)S(1)}, bf16[4,2,2,32,512]{4,3,2,1,0:T(8,128)(2,1)S(1)}, f32[4,2,2,32,512]{4,3,2,1,0:T(8,128)S(1)}) custom-call(s32[3]{0:T(128)S(1)} %pad_add_fusion.place.refs_0_, bf16[1152,512]{1,0:T(8,128)(2,1)S(1)} %bitcast.42, bf16[2,512,512]{2,1,0:T(8,128)(2,1)S(1)} %copy-done.5, f32[1152,512]{1,0:T(8,128)S(1)} %copy-done.6, ...), custom_call_target="tpu_custom_call" | custom-call | flops 1811939328 | tf_op jit(solution)/shard_map/pallas_call | solution.py:49
  154.6 11.8 %collective-permute-start.16 = (bf16[4,2,2,32,512]{4,3,2,1,0:T(8,128)(2,1)S(1)}, bf16[4,2,2,32,512]{4,3,2,1,0:T(8,128)(2,1)S(1)}, u32[]{:S(2)}, u32[]{:S(2)}) collective-permute-start(bf16[4,2,2,32,512]{4,3,2,1,0:T(8,128)(2,1)S(1)} %get-tuple-element.85), channel_id=1, source_target_pairs={{0,1},{1,0},{2,3},{3,2},{4,5},{5,4},{6,7},{7,6},{8,9},{9,8},{10,11... | collective-permute-start | bytes 1572872 | tf_op jit(solution)/shard_map/ppermute | solution.py:124
  166.4 1.5 collective-permute-done.16
  168.9 4.1 %all-to-all-start.3 = ((bf16[4,2,2,32,512]{4,3,2,1,0:T(8,128)(2,1)}), bf16[4,2,2,32,512]{4,3,2,1,0:T(8,128)(2,1)}, u32[]{:S(2)}, u32[]{:S(2)}) async-start(bf16[4,2,2,32,512]{4,3,2,1,0:T(8,128)(2,1)} %add_convert_fusion.1), calls=%async_computation.3 | async-start | bytes 1048576 | tf_op jit(solution)/shard_map/all_to_all | solution.py:125
  173.0 9.3 %all-to-all-done.3 = bf16[4,2,2,32,512]{4,3,2,1,0:T(8,128)(2,1)} async-done(((bf16[4,2,2,32,512]{4,3,2,1,0:T(8,128)(2,1)}), bf16[4,2,2,32,512]{4,3,2,1,0:T(8,128)(2,1)}, u32[]{:S(2)}, u32[]{:S(2)}) %all-to-all-start.3) | async-done | bytes 524320 | tf_op jit(solution)/shard_map/all_to_all | solution.py:125
  183.5 5.7 %collective-permute-start.17 = (bf16[2,32,512]{2,1,0:T(8,128)(2,1)S(1)}, bf16[2,32,512]{2,1,0:T(8,128)(2,1)S(1)}, u32[]{:S(2)}, u32[]{:S(2)}) collective-permute-start(bf16[2,32,512]{2,1,0:T(8,128)(2,1)S(1)} %fusion.16), channel_id=1, source_target_pairs={{0,8},{8,0},{1,9},{9,1},{2,10},{10,2},{3,11},{11,3},{4,12},{12,4},... | collective-permute-start | bytes 196616 | tf_op jit(solution)/shard_map/ppermute | solution.py:128
  189.2 1.8 add_convert_fusion
  191.1 6.9 %collective-permute-done.17 = bf16[2,32,512]{2,1,0:T(8,128)(2,1)S(1)} collective-permute-done((bf16[2,32,512]{2,1,0:T(8,128)(2,1)S(1)}, bf16[2,32,512]{2,1,0:T(8,128)(2,1)S(1)}, u32[]{:S(2)}, u32[]{:S(2)}) %collective-permute-start.17) | collective-permute-done | bytes 65568 | tf_op jit(solution)/shard_map/ppermute | solution.py:128
  (86 shorter events, 32.6 us)
Async XLA Ops:
  0.7 22.4 %all-to-all-start = ((bf16[4,288,512]{2,1,0:T(8,128)(2,1)}), bf16[4,288,512]{2,1,0:T(8,128)(2,1)S(1)}, u32[]{:S(2)}, u32[]{:S(2)}) async-start(bf16[4,288,512]{2,1,0:T(8,128)(2,1)} %bitcast.45), calls=%async_computation | async-start | bytes 2359296 | tf_op jit(solution)/shard_map/all_to_all | solution.py:140
  5.8 17.2 %collective-permute-start = (bf16[2,32,512]{2,1,0:T(8,128)(2,1)S(1)}, bf16[2,32,512]{2,1,0:T(8,128)(2,1)S(1)}, u32[]{:S(2)}, u32[]{:S(2)}) collective-permute-start(bf16[2,32,512]{2,1,0:T(8,128)(2,1)S(1)} %pad_maximum_fusion.1), channel_id=1, source_target_pairs={{0,8},{8,0},{1,9},{9,1},{2,10},{10,2},{3,11},{11,3},{4,12},{12,4},... | collective-permute-start | bytes 196616 | tf_op jit(solution)/shard_map/ppermute | solution.py:142
  54.8 10.5 %collective-permute-start.1 = (bf16[4,4,2,2,32,512]{5,4,3,2,1,0:T(8,128)(2,1)S(1)}, bf16[4,4,2,2,32,512]{5,4,3,2,1,0:T(8,128)(2,1)}, u32[]{:S(2)}, u32[]{:S(2)}) collective-permute-start(bf16[4,4,2,2,32,512]{5,4,3,2,1,0:T(8,128)(2,1)S(1)} %bitcast.40), channel_id=1, source_target_pairs={{0,1},{1,0},{2,3},{3,2},{4,5},{5,4},{6,7},{7,6},{8,9},{9,8},{10,11... | collective-permute-start | bytes 6291464 | tf_op jit(solution)/shard_map/ppermute | solution.py:147
  69.8 16.5 %copy-start = (bf16[4,2,512,512]{3,2,1,0:T(8,128)(2,1)}, bf16[4,2,512,512]{3,2,1,0:T(8,128)(2,1)S(1)}, u32[]{:S(2)}) copy-start(bf16[4,2,512,512]{3,2,1,0:T(8,128)(2,1)S(1)} %get-tuple-element.47.weights.refs_2_) | copy-start | bytes 12582916
  70.5 2.0 collective-permute-start.2
  71.8 2.0 collective-permute-start.3
  73.1 2.0 collective-permute-start.4
  74.3 2.0 collective-permute-start.5
  75.6 2.0 collective-permute-start.6
  76.9 2.0 collective-permute-start.7
  78.2 2.0 collective-permute-start.8
  79.5 2.0 collective-permute-start.9
  80.8 2.1 %collective-permute-start.10 = (bf16[144,512]{1,0:T(8,128)(2,1)S(1)}, bf16[144,512]{1,0:T(8,128)(2,1)S(1)}, u32[]{:S(2)}, u32[]{:S(2)}) collective-permute-start(bf16[144,512]{1,0:T(8,128)(2,1)S(1)} %get-tuple-element.64._), channel_id=1, source_target_pairs={{192,128},{193,129},{194,130},{195,131},{196,132},{197,133},{198,1... | collective-permute-start | bytes 442376 | tf_op jit(solution)/shard_map/ppermute | solution.py:183
  82.1 4.2 %collective-permute-start.11 = (bf16[144,512]{1,0:T(8,128)(2,1)S(1)}, bf16[144,512]{1,0:T(8,128)(2,1)S(1)}, u32[]{:S(2)}, u32[]{:S(2)}) collective-permute-start(bf16[144,512]{1,0:T(8,128)(2,1)S(1)} %get-tuple-element.66._), channel_id=1, source_target_pairs={{192,128},{193,129},{194,130},{195,131},{196,132},{197,133},{198,1... | collective-permute-start | bytes 442376 | tf_op jit(solution)/shard_map/ppermute | solution.py:183
  85.0 10.7 %collective-permute-start.12 = (bf16[144,512]{1,0:T(8,128)(2,1)}, bf16[144,512]{1,0:T(8,128)(2,1)}, u32[]{:S(2)}, u32[]{:S(2)}) collective-permute-start(bf16[144,512]{1,0:T(8,128)(2,1)} %get-tuple-element.68._), channel_id=1, source_target_pairs={{128,64},{129,65},{130,66},{131,67},{132,68},{133,69},{134,70},{13... | collective-permute-start | bytes 442376 | tf_op jit(solution)/shard_map/ppermute | solution.py:183
  87.7 13.6 %collective-permute-start.13 = (bf16[144,512]{1,0:T(8,128)(2,1)}, bf16[144,512]{1,0:T(8,128)(2,1)}, u32[]{:S(2)}, u32[]{:S(2)}) collective-permute-start(bf16[144,512]{1,0:T(8,128)(2,1)} %get-tuple-element.70._), channel_id=1, source_target_pairs={{128,64},{129,65},{130,66},{131,67},{132,68},{133,69},{134,70},{13... | collective-permute-start | bytes 442376 | tf_op jit(solution)/shard_map/ppermute | solution.py:183
  100.0 31.7 %collective-permute-start.15 = (bf16[144,512]{1,0:T(8,128)(2,1)S(1)}, bf16[144,512]{1,0:T(8,128)(2,1)S(1)}, u32[]{:S(2)}, u32[]{:S(2)}) collective-permute-start(bf16[144,512]{1,0:T(8,128)(2,1)S(1)} %get-tuple-element.75._), channel_id=1, source_target_pairs={{64,0},{65,1},{66,2},{67,3},{68,4},{69,5},{70,6},{71,7},{72,8},{73... | collective-permute-start | bytes 442376 | tf_op jit(solution)/shard_map/ppermute | solution.py:183
  102.3 33.5 %collective-permute-start.14 = (bf16[144,512]{1,0:T(8,128)(2,1)S(1)}, bf16[144,512]{1,0:T(8,128)(2,1)S(1)}, u32[]{:S(2)}, u32[]{:S(2)}) collective-permute-start(bf16[144,512]{1,0:T(8,128)(2,1)S(1)} %get-tuple-element.77._), channel_id=1, source_target_pairs={{64,0},{65,1},{66,2},{67,3},{68,4},{69,5},{70,6},{71,7},{72,8},{73... | collective-permute-start | bytes 442376 | tf_op jit(solution)/shard_map/ppermute | solution.py:183
  135.8 15.0 %copy-start.6 = (f32[1152,512]{1,0:T(8,128)S(1)}, f32[1152,512]{1,0:T(8,128)}, u32[]{:S(2)}) copy-start(f32[1152,512]{1,0:T(8,128)} %add_multiply_fusion.slopes) | copy-start | bytes 7077892
  137.7 13.0 %copy-start.5 = (bf16[2,512,512]{2,1,0:T(8,128)(2,1)S(1)}, bf16[2,512,512]{2,1,0:T(8,128)(2,1)}, u32[]{:S(2)}) copy-start(bf16[2,512,512]{2,1,0:T(8,128)(2,1)} %copy-done.4) | copy-start | bytes 3145732
  154.6 34.7 %copy-start.13 = (bf16[1152,512]{1,0:T(8,128)(2,1)S(1)}, bf16[1152,512]{1,0:T(8,128)(2,1)}, u32[]{:S(2)}) copy-start(bf16[1152,512]{1,0:T(8,128)(2,1)} %copy-done.12) | copy-start | bytes 3538948
  154.6 13.3 %collective-permute-start.16 = (bf16[4,2,2,32,512]{4,3,2,1,0:T(8,128)(2,1)S(1)}, bf16[4,2,2,32,512]{4,3,2,1,0:T(8,128)(2,1)S(1)}, u32[]{:S(2)}, u32[]{:S(2)}) collective-permute-start(bf16[4,2,2,32,512]{4,3,2,1,0:T(8,128)(2,1)S(1)} %get-tuple-element.85), channel_id=1, source_target_pairs={{0,1},{1,0},{2,3},{3,2},{4,5},{5,4},{6,7},{7,6},{8,9},{9,8},{10,11... | collective-permute-start | bytes 1572872 | tf_op jit(solution)/shard_map/ppermute | solution.py:124
  168.9 13.4 %all-to-all-start.3 = ((bf16[4,2,2,32,512]{4,3,2,1,0:T(8,128)(2,1)}), bf16[4,2,2,32,512]{4,3,2,1,0:T(8,128)(2,1)}, u32[]{:S(2)}, u32[]{:S(2)}) async-start(bf16[4,2,2,32,512]{4,3,2,1,0:T(8,128)(2,1)} %add_convert_fusion.1), calls=%async_computation.3 | async-start | bytes 1048576 | tf_op jit(solution)/shard_map/all_to_all | solution.py:125
  183.5 14.4 %collective-permute-start.17 = (bf16[2,32,512]{2,1,0:T(8,128)(2,1)S(1)}, bf16[2,32,512]{2,1,0:T(8,128)(2,1)S(1)}, u32[]{:S(2)}, u32[]{:S(2)}) collective-permute-start(bf16[2,32,512]{2,1,0:T(8,128)(2,1)S(1)} %fusion.16), channel_id=1, source_target_pairs={{0,8},{8,0},{1,9},{9,1},{2,10},{10,2},{3,11},{11,3},{4,12},{12,4},... | collective-permute-start | bytes 196616 | tf_op jit(solution)/shard_map/ppermute | solution.py:128
  (13 other events, 49.8 us)

commit v4 on v3

--- a/solution.py
+++ b/solution.py
@@ -12,7 +12,7 @@
 NZ, NY, NH, NX, NC = 8, 4, 2, 4, 2
 AXES = ("z_lo", "y", "z_hi", "x", "core")
 PLANE = ("y", "x")
-CHUNKS = 2
+CHUNKS = 3
 HOME_AT = NZ - 3
 MIB = 1024 * 1024
 BF16, F32 = jnp.bfloat16, jnp.float32
@@ -57,7 +57,7 @@
     )(*operands)
 
 
-def prepare_kernel(place, mine, other, inputs, weights, slopes):
+def prepare_kernel(place, mine, other, inputs, weights, slopes, natural):
     rows = mine.shape[4]
     near_at = place[2] * (NX * NC * rows)
     far_at = NX * NC * rows - near_at
@@ -69,8 +69,10 @@
                 for x in range(NX):
                     at = pl.multiple_of(half_at + x * NC * rows + core_at, rows)
                     for w in range(2):
-                        weights[s, w, pl.ds(at, rows)] = source[s, x, half, w]
-        slopes[s] = slope(dot(inputs[s], weights[s, 0], 1, 0))
+                        natural[s, w, pl.ds(at, rows)] = source[s, x, half, w]
+        slopes[s] = slope(dot(inputs[s], natural[s, 0], 1, 0))
+        for w in range(2):
+            weights[s, w] = natural[s, w].T
 
 
 def stage_kernel(stage, chunk, place, arriving, weights, slopes, kept_in, *rest):
@@ -91,8 +93,8 @@
             outs[0][s, into] = g
             if s == 0 and last:
                 break
-            dz = (dot(g, weights[s, 1], 1, 1) * slopes[s, own]).astype(BF16)
-            g = (g.astype(F32) + dot(dz, weights[s, 0], 1, 1)).astype(BF16)
+            dz = (dot(g, weights[s, 1], 1, 0) * slopes[s, own]).astype(BF16)
+            g = (g.astype(F32) + dot(dz, weights[s, 0], 1, 0)).astype(BF16)
         if not last:
             outs[1][...] = g
 
@@ -102,11 +104,37 @@
             outs[0][s, into] = kept_in[s]
 
 
-def home_kernel(place, home_g, weights, slopes, inputs_t, h_t, dz, sent, own, grad):
+def forward_kernel(place, inputs, weights, slopes, inputs_t, h_t):
+    w_in = weights[place[3], 0]
+    part = inputs.shape[0] // 3
+    for block in range(3):
+        at = pl.ds(block * part, part)
+        x = inputs[at]
+        zed = dot(x, w_in, 1, 1)
+        sig = 1.0 / (1.0 + jnp.exp(-zed))
+        slopes[at] = RHO * sig * (1.0 + zed * (1.0 - sig))
+        h_t[:, at] = (zed * sig).astype(BF16).T
+        inputs_t[:, at] = x.T
+
+
+def add_kernel(own, arrived, total):
+    total[...] = (own[...] + arrived[...].astype(F32)).astype(BF16)
+
+
+def input_kernel(place, home_g, dz, weights, dx):
+    w_in = weights[place[3], 0]
     part = home_g.shape[0] // NY
     for block in range(NY):
         at = pl.ds(block * part, part)
-        dz[at] = (dot(home_g[at], weights[1], 1, 1) * slopes[at]).astype(BF16)
+        dx[at] = (home_g[at].astype(F32) + dot(dz[at], w_in, 1, 0)).astype(BF16)
+
+
+def home_kernel(place, home_g, weights, slopes, inputs_t, h_t, dz, sent, own, grad):
+    w_out = weights[place[3], 1]
+    part = home_g.shape[0] // NY
+    for block in range(NY):
+        at = pl.ds(block * part, part)
+        dz[at] = (dot(home_g[at], w_out, 1, 0) * slopes[at]).astype(BF16)
     rows = sent.shape[3]
     for w, (left, right) in enumerate(((inputs_t, dz), (h_t, home_g))):
         product = dot(left[...], right[...], 1, 0)
@@ -120,17 +148,9 @@
                 sent[x, zh, w] = grad[pl.ds(at, rows)].astype(BF16)
 
 
-def reduce_replicas(sent, own, zh):
-    total = own + lax.ppermute(sent, "core", SWAP)
-    total = lax.all_to_all(total.astype(BF16), "x", 0, 0).astype(F32).sum(axis=0)
-    sent = lax.dynamic_index_in_dim(total, 1 - zh, 0, keepdims=False).astype(BF16)
-    own = lax.dynamic_index_in_dim(total, zh, 0, keepdims=False)
-    return own + lax.ppermute(sent, "z_hi", SWAP)
-
-
 def body(section_inputs, cotangent, weight_in, weight_out):
     z, y, zh, _, core = (lax.axis_index(axis) for axis in AXES)
-    place = jnp.stack([z, core, zh]).astype(jnp.int32)
+    place = jnp.stack([z, core, zh, y]).astype(jnp.int32)
     micro, rows, width = section_inputs.shape[1:]
     shard = weight_in.shape[1]
     share = micro * rows // NY
@@ -140,7 +160,9 @@
     stage_x = lax.all_to_all(flat_x.reshape(NY, share, width), "y", 0, 0)
     own = jnp.concatenate([weight_in, weight_out], axis=0)
     far = lax.ppermute(own, "z_hi", SWAP)
-    far, stage_x = lax.optimization_barrier((far, stage_x))
+    given = lax.dynamic_index_in_dim(cotangent.reshape(NY, share, width), y, 0, keepdims=False)
+    arriving = [given[m * part : (m + 1) * part] for m in range(CHUNKS)]
+    far, stage_x, *arriving = lax.optimization_barrier((far, stage_x, *arriving))
     block = jnp.concatenate([own, far], axis=0).reshape(1, 4 * shard, width)
     block = jnp.broadcast_to(block, (NY * NX, 4 * shard, width))
     mine = lax.all_to_all(block, PLANE, 0, 0).reshape(NY, NX, 2, 2, shard, width)
@@ -152,11 +174,10 @@
         mine,
         other,
         stage_x,
+        scratch=[pltpu.VMEM((NY, 2, width, width), BF16)],
         flops=2 * NY * share * width * width,
     )
 
-    given = lax.dynamic_index_in_dim(cotangent.reshape(NY, share, width), y, 0, keepdims=False)
-    arriving = [given[m * part : (m + 1) * part] for m in range(CHUNKS)]
     kept = [jnp.zeros((NY, part, width), BF16) for _ in range(CHUNKS)]
     sending = None
     for stage in range(NZ):
@@ -177,19 +198,21 @@
                 after=sending,
                 flops=4 * NY * part * width * width,
             )
-            kept[m] = result[0]
+            kept[m], sending = result[0], result[-1]
             if stage < NZ - 1:
-                sending = result[1]
                 arriving[m] = lax.ppermute(sending, "z_lo", [(NZ - 1 - stage, NZ - 2 - stage)])
         if stage == HOME_AT:
-            home_w = lax.dynamic_index_in_dim(weights, y, 0, keepdims=False)
-            home_w, home_x, _ = lax.optimization_barrier((home_w, flat_x, sending))
-            home_slope = slope(dot(home_x, home_w[0], 1, 0))
-            home_ht = jax.nn.silu(dot(home_w[0], home_x, 0, 1)).astype(BF16)
-            home_xt = home_x.T
-            arriving[0], home_slope, home_ht, home_xt, home_w = lax.optimization_barrier(
-                (arriving[0], home_slope, home_ht, home_xt, home_w)
+            wide = struct((width, micro * rows), BF16)
+            home = call(
+                forward_kernel,
+                (struct(flat_x.shape, F32), wide, wide),
+                place,
+                flat_x,
+                weights,
+                after=sending,
+                flops=2 * micro * rows * width * width,
             )
+            arriving[0], *home = lax.optimization_barrier((arriving[0], *home))
 
     home_g = lax.all_to_all(kept[-1], "y", 0, 0).reshape(micro * rows, width)
     half = (NX, NH, 2, shard, width)
@@ -198,16 +221,28 @@
         (struct(home_g.shape, BF16), struct(half, BF16), struct(half, F32)),
         place,
         home_g,
-        home_w,
-        home_slope,
-        home_xt,
-        home_ht,
+        weights,
+        *home,
         scratch=[pltpu.VMEM((width, width), F32)],
         flops=6 * micro * rows * width * width,
     )
-    dx = (home_g.astype(F32) + dot(dz, home_w[0], 1, 1)).astype(BF16)
+    (total,) = call(add_kernel, (struct(half, BF16),), own, lax.ppermute(sent, "core", SWAP))
+    parts = lax.all_to_all(total, "x", 0, 0)
+    (dx,) = call(
+        input_kernel,
+        (struct(home_g.shape, BF16),),
+        place,
+        home_g,
+        dz,
+        weights,
+        after=parts,
+        flops=2 * micro * rows * width * width,
+    )
+    total = parts.astype(F32).sum(axis=0)
+    sent = lax.dynamic_index_in_dim(total, 1 - zh, 0, keepdims=False).astype(BF16)
+    own = lax.dynamic_index_in_dim(total, zh, 0, keepdims=False)
     factor = 4.0 / jnp.sqrt(F32(micro * rows * NH * NX * NC))
-    reduced = reduce_replicas(sent, own, zh) * factor
+    reduced = (own + lax.ppermute(sent, "z_hi", SWAP)) * factor
     return (reduced[0:1], reduced[1:2], dx.reshape(1, micro, rows, width))
 
 

time: 199 us -> 185 us (0.930)
  Pallas kernels: 20.2 us -> 28.5 us
  local copies, waits for them, and re-layouts: 11.8 us -> 4.76 us
  matrix products: 6.8 us -> 0 us
  waiting for transfers between devices: 51.2 us -> 44.5 us
  other arithmetic: 2.22 us -> 0.19 us
    pallas_call x18 -> x29, Pallas kernels: 20.2 us -> 28.5 us  [call(): pl.pallas_call(kernel, out_shape=out_shape, in_specs=specs, out_specs=jax...]
    dot_general x3 -> x0, matrix products: 6.8 us -> none  [dot(): lax.dot_general(left, right, (((left_dim,), (right_dim,)), ((), ())), pre...]
    unnamed x34 -> x12, local copies, waits for them, and re-layouts: 8.11 us -> 2.2 us
    ppermute x14 -> x21, waiting for transfers between devices: 30.3 us -> 24.6 us  [body(): lax.ppermute(sending, 'z_lo', [(NZ - 1 - stage, NZ - 2 - stage)])]
    ppermute x2, starting transfers between devices: 17.5 us -> 12.9 us  [the longest x1 8.21 us: body(): lax.ppermute(sent, 'core', SWAP)]
    ppermute x14 -> x21, starting transfers between devices: 11.9 us -> 15.9 us  [body(): lax.ppermute(sending, 'z_lo', [(NZ - 1 - stage, NZ - 2 - stage)])]
    ppermute x1, waiting for transfers between devices: 1.45 us -> 3.81 us  [body(): other = lax.ppermute(mine, 'core', SWAP)]
  transfers between devices with their start and end apart: 20 -> 27, of which waited for: 7 -> 8; matrix products, arithmetic and copies ran while one was open for 5% -> 1% of each run, Pallas kernels for 6% -> 10%
where the time goes in v4:
time: 185 us; the launch traced here: 184 us
  starting transfers between devices  59.5 us (32%)
  blocking collectives  45.1 us (24%)
  waiting for transfers between devices  44.5 us (24%)
  Pallas kernels  28.5 us (15%)
  local copies, waits for them, and re-layouts  4.76 us (3%)
    all_to_all x1, blocking collectives, body(): lax.all_to_all(block, PLANE, 0, 0).reshape(NY, NX, 2, 2, shard, width)  31.5 us
    pallas_call x29, Pallas kernels, call(): pl.pallas_call(kernel, out_shape=out_shape, in_specs=specs, out_specs=jax...  28.5 us
    ppermute x21, waiting for transfers between devices, body(): lax.ppermute(sending, 'z_lo', [(NZ - 1 - stage, NZ - 2 - stage)])  24.6 us
    ppermute x21, starting transfers between devices, body(): lax.ppermute(sending, 'z_lo', [(NZ - 1 - stage, NZ - 2 - stage)])  15.9 us
    ppermute x1, starting transfers between devices, body(): far = lax.ppermute(own, 'z_hi', SWAP)  15.4 us
    all_to_all x1, blocking collectives, body(): home_g = lax.all_to_all(kept[-1], 'y', 0, 0).reshape(micro * rows, width)  13.6 us
    all_to_all x1, waiting for transfers between devices, body(): parts = lax.all_to_all(total, 'x', 0, 0)  9.2 us
    ppermute x1, starting transfers between devices, body(): lax.ppermute(sent, 'core', SWAP)  8.21 us
  transfers between devices with their start and end apart: 27, of which 8 were waited for; matrix products, arithmetic and copies ran while one was open for 1% of the time, Pallas kernels for 10%

profile of v4, /device:TPU:1, one launch (start us, length us, event | category | flops | bytes accessed | tf_op | source)
XLA Modules:
  0.0 183.7 jit_solution(10978609164804837062)
XLA Ops:
  0.7 5.2 %all-to-all-start = ((bf16[4,288,512]{2,1,0:T(8,128)(2,1)}), bf16[4,288,512]{2,1,0:T(8,128)(2,1)S(1)}, u32[]{:S(2)}, u32[]{:S(2)}) async-start(bf16[4,288,512]{2,1,0:T(8,128)(2,1)} %bitcast.27), calls=%async_computation | async-start | bytes 2359296 | tf_op jit(solution)/shard_map/all_to_all | solution.py:160
  5.8 15.4 %collective-permute-start = (bf16[2,32,512]{2,1,0:T(8,128)(2,1)S(1)}, bf16[2,32,512]{2,1,0:T(8,128)(2,1)S(1)}, u32[]{:S(2)}, u32[]{:S(2)}) collective-permute-start(bf16[2,32,512]{2,1,0:T(8,128)(2,1)S(1)} %pad_maximum_fusion.1), channel_id=1, source_target_pairs={{0,8},{8,0},{1,9},{9,1},{2,10},{10,2},{3,11},{11,3},{4,12},{12,4},... | collective-permute-start | bytes 196616 | tf_op jit(solution)/shard_map/ppermute | solution.py:162
  21.3 1.7 dynamic-slice_bitcast_fusion
  23.3 31.5 %all_to_all.20 = bf16[16,128,512]{2,1,0:T(8,128)(2,1)S(1)} all-to-all(bf16[16,128,512]{2,1,0:T(8,128)(2,1)S(1)} %broadcast_in_dim.8), channel_id=1, replica_groups=mesh['z_lo'=8,'y'=4,'z_hi'=2,'x'=4,'core'=2] {'y','x'}, dimensions={0} | all-to-all | bytes 4194304 | tf_op jit(solution)/shard_map/all_to_all | solution.py:168
  54.8 6.6 %collective-permute-start.1 = (bf16[4,4,2,2,32,512]{5,4,3,2,1,0:T(8,128)(2,1)S(1)}, bf16[4,4,2,2,32,512]{5,4,3,2,1,0:T(8,128)(2,1)}, u32[]{:S(2)}, u32[]{:S(2)}) collective-permute-start(bf16[4,4,2,2,32,512]{5,4,3,2,1,0:T(8,128)(2,1)S(1)} %bitcast.25), channel_id=1, source_target_pairs={{0,1},{1,0},{2,3},{3,2},{4,5},{5,4},{6,7},{7,6},{8,9},{9,8},{10,11... | collective-permute-start | bytes 6291464 | tf_op jit(solution)/shard_map/ppermute | solution.py:169
  61.4 3.8 %collective-permute-done.1.other = bf16[4,4,2,2,32,512]{5,4,3,2,1,0:T(8,128)(2,1)} collective-permute-done((bf16[4,4,2,2,32,512]{5,4,3,2,1,0:T(8,128)(2,1)S(1)}, bf16[4,4,2,2,32,512]{5,4,3,2,1,0:T(8,128)(2,1)}, u32[]{:S(2)}, u32[]{:S(2)}) %collective-permute-start.1) | collective-permute-done | bytes 2097184 | tf_op jit(solution)/shard_map/ppermute | solution.py:169
  65.2 3.3 %shard_map.67 = (bf16[4,2,512,512]{3,2,1,0:T(8,128)(2,1)S(1)}, f32[4,288,512]{2,1,0:T(8,128)S(1)}) custom-call(s32[4]{0:T(128)S(1)} %pad_add_fusion.place.refs_0_, bf16[4,4,2,2,32,512]{5,4,3,2,1,0:T(8,128)(2,1)S(1)} %bitcast.26, bf16[4,4,2,2,32,512]{5,4,3,2,1,0:T(8,128)(2,1)} %collective-permute-done.1.other, bf16[4,288,512]{2,1,0:T(8,128)(2,1)S(1)} %all-to-all-done.inputs), custom_call_target="tpu_custom_call" | custom-call | flops 603979776 | tf_op jit(solution)/shard_map/pallas_call | solution.py:49
  91.7 2.0 %shard_map.86 = (f32[1152,512]{1,0:T(8,128)S(1)}, bf16[512,1152]{1,0:T(8,128)(2,1)S(1)}, bf16[512,1152]{1,0:T(8,128)(2,1)S(1)}) custom-call(bf16[96,512]{1,0:T(8,128)(2,1)S(1)} %get-tuple-element.101._, s32[4]{0:T(128)S(1)} %pad_add_fusion.place.refs_0_, bf16[1152,512]{1,0:T(8,128)(2,1)S(1)} %bitcast.28, ...), custom_call_target="tpu_custom_call" | custom-call | flops 603979776 | tf_op jit(solution)/shard_map/pallas_call | solution.py:49
  99.4 18.4 %collective-permute-done.20.refs_1_ = bf16[96,512]{1,0:T(8,128)(2,1)S(1)} collective-permute-done((bf16[96,512]{1,0:T(8,128)(2,1)S(1)}, bf16[96,512]{1,0:T(8,128)(2,1)S(1)}, u32[]{:S(2)}, u32[]{:S(2)}) %collective-permute-start.20) | collective-permute-done | bytes 98336 | tf_op jit(solution)/shard_map/ppermute | solution.py:203
  117.8 1.6 shard_map.90._.refs_5_
  119.4 3.7 %collective-permute-done.21.refs_1_ = bf16[96,512]{1,0:T(8,128)(2,1)S(1)} collective-permute-done((bf16[96,512]{1,0:T(8,128)(2,1)S(1)}, bf16[96,512]{1,0:T(8,128)(2,1)S(1)}, u32[]{:S(2)}, u32[]{:S(2)}) %collective-permute-start.21) | collective-permute-done | bytes 98336 | tf_op jit(solution)/shard_map/ppermute | solution.py:203
  123.1 1.6 shard_map.91._.refs_6_
  124.7 2.5 %collective-permute-done.22.refs_1_ = bf16[96,512]{1,0:T(8,128)(2,1)S(1)} collective-permute-done((bf16[96,512]{1,0:T(8,128)(2,1)S(1)}, bf16[96,512]{1,0:T(8,128)(2,1)S(1)}, u32[]{:S(2)}, u32[]{:S(2)}) %collective-permute-start.22) | collective-permute-done | bytes 98336 | tf_op jit(solution)/shard_map/ppermute | solution.py:203
  127.2 1.6 shard_map.92
  128.8 13.6 %all_to_all.21 = bf16[4,288,512]{2,1,0:T(8,128)(2,1)S(1)} all-to-all(bf16[4,288,512]{2,1,0:T(8,128)(2,1)S(1)} %shard_map.92), channel_id=1, replica_groups=mesh['z_lo'=8,'y'=4,'z_hi'=2,'x'=4,'core'=2] {'y'}, dimensions={0} | all-to-all | bytes 2359296 | tf_op jit(solution)/shard_map/all_to_all | solution.py:217
  142.4 2.8 %shard_map.93 = (bf16[1152,512]{1,0:T(8,128)(2,1)S(1)}, bf16[4,2,2,32,512]{4,3,2,1,0:T(8,128)(2,1)S(1)}, f32[4,2,2,32,512]{4,3,2,1,0:T(8,128)S(1)}) custom-call(s32[4]{0:T(128)S(1)} %pad_add_fusion.place.refs_0_, bf16[1152,512]{1,0:T(8,128)(2,1)S(1)} %bitcast.23, bf16[4,2,512,512]{3,2,1,0:T(8,128)(2,1)S(1)} %get-tuple-element.65.weights.refs_2_.refs_3_, ...), custom_call_target="tpu_custom_call" | custom-call | flops 1811939328 | tf_op jit(solution)/shard_map/pallas_call | solution.py:49
  145.2 8.2 %collective-permute-start.23 = (bf16[4,2,2,32,512]{4,3,2,1,0:T(8,128)(2,1)S(1)}, bf16[4,2,2,32,512]{4,3,2,1,0:T(8,128)(2,1)S(1)}, u32[]{:S(2)}, u32[]{:S(2)}) collective-permute-start(bf16[4,2,2,32,512]{4,3,2,1,0:T(8,128)(2,1)S(1)} %get-tuple-element.119), channel_id=1, source_target_pairs={{0,1},{1,0},{2,3},{3,2},{4,5},{5,4},{6,7},{7,6},{8,9},{9,8},{10,11... | collective-permute-start | bytes 1572872 | tf_op jit(solution)/shard_map/ppermute | solution.py:229
  153.5 1.5 collective-permute-done.23.arrived
  155.9 3.5 %all-to-all-start.3 = ((bf16[4,2,2,32,512]{4,3,2,1,0:T(8,128)(2,1)}), bf16[4,2,2,32,512]{4,3,2,1,0:T(8,128)(2,1)S(1)}, u32[]{:S(2)}, u32[]{:S(2)}) async-start(bf16[4,2,2,32,512]{4,3,2,1,0:T(8,128)(2,1)} %shard_map.94), calls=%async_computation.3 | async-start | bytes 1048576 | tf_op jit(solution)/shard_map/all_to_all | solution.py:230
  159.3 9.2 %all-to-all-done.3._ = bf16[4,2,2,32,512]{4,3,2,1,0:T(8,128)(2,1)S(1)} async-done(((bf16[4,2,2,32,512]{4,3,2,1,0:T(8,128)(2,1)}), bf16[4,2,2,32,512]{4,3,2,1,0:T(8,128)(2,1)S(1)}, u32[]{:S(2)}, u32[]{:S(2)}) %all-to-all-start.3) | async-done | bytes 524320 | tf_op jit(solution)/shard_map/all_to_all | solution.py:230
  168.6 4.7 %collective-permute-start.24 = (bf16[2,32,512]{2,1,0:T(8,128)(2,1)S(1)}, bf16[2,32,512]{2,1,0:T(8,128)(2,1)S(1)}, u32[]{:S(2)}, u32[]{:S(2)}) collective-permute-start(bf16[2,32,512]{2,1,0:T(8,128)(2,1)S(1)} %fusion.1), channel_id=1, source_target_pairs={{0,8},{8,0},{1,9},{9,1},{2,10},{10,2},{3,11},{11,3},{4,12},{12,4},... | collective-permute-start | bytes 196616 | tf_op jit(solution)/shard_map/ppermute | solution.py:245
  173.4 2.2 %copy-done.1 = bf16[4,2,512,512]{3,2,1,0:T(8,128)(2,1)S(1)} copy-done((bf16[4,2,512,512]{3,2,1,0:T(8,128)(2,1)S(1)}, bf16[4,2,512,512]{3,2,1,0:T(8,128)(2,1)}, u32[]{:S(2)}) %copy-start.1) | copy-done | bytes 4194328
  175.6 2.3 %shard_map.95 = bf16[1152,512]{1,0:T(8,128)(2,1)} custom-call(bf16[4,2,2,32,512]{4,3,2,1,0:T(8,128)(2,1)S(1)} %all-to-all-done.3._, s32[4]{0:T(128)S(1)} %pad_add_fusion.place.refs_0_, bf16[1152,512]{1,0:T(8,128)(2,1)S(1)} %bitcast.24, bf16[1152,512]{1,0:T(8,128)(2,1)S(1)} %get-tuple-element.120.refs_2_, bf16[4,2,512,512]{3,2,1,0:T(8,128)(2,1)S(1)} %copy-done.1), custom_call_target="tpu_custom_call" | custom-call | flops 603979776 | tf_op jit(solution)/shard_map/pallas_call | solution.py:49
  177.9 5.2 %collective-permute-done.24 = bf16[2,32,512]{2,1,0:T(8,128)(2,1)S(1)} collective-permute-done((bf16[2,32,512]{2,1,0:T(8,128)(2,1)S(1)}, bf16[2,32,512]{2,1,0:T(8,128)(2,1)S(1)}, u32[]{:S(2)}, u32[]{:S(2)}) %collective-permute-start.24) | collective-permute-done | bytes 65568 | tf_op jit(solution)/shard_map/ppermute | solution.py:245
  (83 shorter events, 30.4 us)
Async XLA Ops:
  0.7 22.4 %all-to-all-start = ((bf16[4,288,512]{2,1,0:T(8,128)(2,1)}), bf16[4,288,512]{2,1,0:T(8,128)(2,1)S(1)}, u32[]{:S(2)}, u32[]{:S(2)}) async-start(bf16[4,288,512]{2,1,0:T(8,128)(2,1)} %bitcast.27), calls=%async_computation | async-start | bytes 2359296 | tf_op jit(solution)/shard_map/all_to_all | solution.py:160
  5.8 17.2 %collective-permute-start = (bf16[2,32,512]{2,1,0:T(8,128)(2,1)S(1)}, bf16[2,32,512]{2,1,0:T(8,128)(2,1)S(1)}, u32[]{:S(2)}, u32[]{:S(2)}) collective-permute-start(bf16[2,32,512]{2,1,0:T(8,128)(2,1)S(1)} %pad_maximum_fusion.1), channel_id=1, source_target_pairs={{0,8},{8,0},{1,9},{9,1},{2,10},{10,2},{3,11},{11,3},{4,12},{12,4},... | collective-permute-start | bytes 196616 | tf_op jit(solution)/shard_map/ppermute | solution.py:162
  54.8 10.5 %collective-permute-start.1 = (bf16[4,4,2,2,32,512]{5,4,3,2,1,0:T(8,128)(2,1)S(1)}, bf16[4,4,2,2,32,512]{5,4,3,2,1,0:T(8,128)(2,1)}, u32[]{:S(2)}, u32[]{:S(2)}) collective-permute-start(bf16[4,4,2,2,32,512]{5,4,3,2,1,0:T(8,128)(2,1)S(1)} %bitcast.25), channel_id=1, source_target_pairs={{0,1},{1,0},{2,3},{3,2},{4,5},{5,4},{6,7},{7,6},{8,9},{9,8},{10,11... | collective-permute-start | bytes 6291464 | tf_op jit(solution)/shard_map/ppermute | solution.py:169
  71.8 3.2 %collective-permute-start.4 = (bf16[96,512]{1,0:T(8,128)(2,1)S(1)}, bf16[96,512]{1,0:T(8,128)(2,1)S(1)}, u32[]{:S(2)}, u32[]{:S(2)}) collective-permute-start(bf16[96,512]{1,0:T(8,128)(2,1)S(1)} %get-tuple-element.71._), channel_id=1, source_target_pairs={{448,384},{449,385},{450,386},{451,387},{452,388},{453,389},{454,3... | collective-permute-start | bytes 294920 | tf_op jit(solution)/shard_map/ppermute | solution.py:203
  73.0 3.2 %collective-permute-start.5 = (bf16[96,512]{1,0:T(8,128)(2,1)S(1)}, bf16[96,512]{1,0:T(8,128)(2,1)S(1)}, u32[]{:S(2)}, u32[]{:S(2)}) collective-permute-start(bf16[96,512]{1,0:T(8,128)(2,1)S(1)} %get-tuple-element.73._), channel_id=1, source_target_pairs={{384,320},{385,321},{386,322},{387,323},{388,324},{389,325},{390,3... | collective-permute-start | bytes 294920 | tf_op jit(solution)/shard_map/ppermute | solution.py:203
  74.3 3.2 %collective-permute-start.6 = (bf16[96,512]{1,0:T(8,128)(2,1)S(1)}, bf16[96,512]{1,0:T(8,128)(2,1)S(1)}, u32[]{:S(2)}, u32[]{:S(2)}) collective-permute-start(bf16[96,512]{1,0:T(8,128)(2,1)S(1)} %get-tuple-element.75._), channel_id=1, source_target_pairs={{384,320},{385,321},{386,322},{387,323},{388,324},{389,325},{390,3... | collective-permute-start | bytes 294920 | tf_op jit(solution)/shard_map/ppermute | solution.py:203
  75.6 3.2 %collective-permute-start.7 = (bf16[96,512]{1,0:T(8,128)(2,1)S(1)}, bf16[96,512]{1,0:T(8,128)(2,1)S(1)}, u32[]{:S(2)}, u32[]{:S(2)}) collective-permute-start(bf16[96,512]{1,0:T(8,128)(2,1)S(1)} %get-tuple-element.77._), channel_id=1, source_target_pairs={{384,320},{385,321},{386,322},{387,323},{388,324},{389,325},{390,3... | collective-permute-start | bytes 294920 | tf_op jit(solution)/shard_map/ppermute | solution.py:203
  76.8 3.2 %collective-permute-start.8 = (bf16[96,512]{1,0:T(8,128)(2,1)S(1)}, bf16[96,512]{1,0:T(8,128)(2,1)S(1)}, u32[]{:S(2)}, u32[]{:S(2)}) collective-permute-start(bf16[96,512]{1,0:T(8,128)(2,1)S(1)} %get-tuple-element.79._), channel_id=1, source_target_pairs={{320,256},{321,257},{322,258},{323,259},{324,260},{325,261},{326,2... | collective-permute-start | bytes 294920 | tf_op jit(solution)/shard_map/ppermute | solution.py:203
  78.1 3.2 %collective-permute-start.9 = (bf16[96,512]{1,0:T(8,128)(2,1)S(1)}, bf16[96,512]{1,0:T(8,128)(2,1)S(1)}, u32[]{:S(2)}, u32[]{:S(2)}) collective-permute-start(bf16[96,512]{1,0:T(8,128)(2,1)S(1)} %get-tuple-element.81._), channel_id=1, source_target_pairs={{320,256},{321,257},{322,258},{323,259},{324,260},{325,261},{326,2... | collective-permute-start | bytes 294920 | tf_op jit(solution)/shard_map/ppermute | solution.py:203
  79.4 3.2 %collective-permute-start.10 = (bf16[96,512]{1,0:T(8,128)(2,1)S(1)}, bf16[96,512]{1,0:T(8,128)(2,1)S(1)}, u32[]{:S(2)}, u32[]{:S(2)}) collective-permute-start(bf16[96,512]{1,0:T(8,128)(2,1)S(1)} %get-tuple-element.83._), channel_id=1, source_target_pairs={{320,256},{321,257},{322,258},{323,259},{324,260},{325,261},{326,2... | collective-permute-start | bytes 294920 | tf_op jit(solution)/shard_map/ppermute | solution.py:203
  80.7 3.2 %collective-permute-start.11 = (bf16[96,512]{1,0:T(8,128)(2,1)S(1)}, bf16[96,512]{1,0:T(8,128)(2,1)S(1)}, u32[]{:S(2)}, u32[]{:S(2)}) collective-permute-start(bf16[96,512]{1,0:T(8,128)(2,1)S(1)} %get-tuple-element.85._), channel_id=1, source_target_pairs={{256,192},{257,193},{258,194},{259,195},{260,196},{261,197},{262,1... | collective-permute-start | bytes 294920 | tf_op jit(solution)/shard_map/ppermute | solution.py:203
  81.9 3.2 %collective-permute-start.12 = (bf16[96,512]{1,0:T(8,128)(2,1)S(1)}, bf16[96,512]{1,0:T(8,128)(2,1)S(1)}, u32[]{:S(2)}, u32[]{:S(2)}) collective-permute-start(bf16[96,512]{1,0:T(8,128)(2,1)S(1)} %get-tuple-element.87._), channel_id=1, source_target_pairs={{256,192},{257,193},{258,194},{259,195},{260,196},{261,197},{262,1... | collective-permute-start | bytes 294920 | tf_op jit(solution)/shard_map/ppermute | solution.py:203
  83.2 3.2 %collective-permute-start.13 = (bf16[96,512]{1,0:T(8,128)(2,1)S(1)}, bf16[96,512]{1,0:T(8,128)(2,1)S(1)}, u32[]{:S(2)}, u32[]{:S(2)}) collective-permute-start(bf16[96,512]{1,0:T(8,128)(2,1)S(1)} %get-tuple-element.89._), channel_id=1, source_target_pairs={{256,192},{257,193},{258,194},{259,195},{260,196},{261,197},{262,1... | collective-permute-start | bytes 294920 | tf_op jit(solution)/shard_map/ppermute | solution.py:203
  84.5 3.4 %collective-permute-start.14 = (bf16[96,512]{1,0:T(8,128)(2,1)S(1)}, bf16[96,512]{1,0:T(8,128)(2,1)S(1)}, u32[]{:S(2)}, u32[]{:S(2)}) collective-permute-start(bf16[96,512]{1,0:T(8,128)(2,1)S(1)} %get-tuple-element.91._), channel_id=1, source_target_pairs={{192,128},{193,129},{194,130},{195,131},{196,132},{197,133},{198,1... | collective-permute-start | bytes 294920 | tf_op jit(solution)/shard_map/ppermute | solution.py:203
  85.8 3.4 %collective-permute-start.15 = (bf16[96,512]{1,0:T(8,128)(2,1)S(1)}, bf16[96,512]{1,0:T(8,128)(2,1)S(1)}, u32[]{:S(2)}, u32[]{:S(2)}) collective-permute-start(bf16[96,512]{1,0:T(8,128)(2,1)S(1)} %get-tuple-element.93._), channel_id=1, source_target_pairs={{192,128},{193,129},{194,130},{195,131},{196,132},{197,133},{198,1... | collective-permute-start | bytes 294920 | tf_op jit(solution)/shard_map/ppermute | solution.py:203
  88.5 5.2 %collective-permute-start.17 = (bf16[96,512]{1,0:T(8,128)(2,1)S(1)}, bf16[96,512]{1,0:T(8,128)(2,1)S(1)}, u32[]{:S(2)}, u32[]{:S(2)}) collective-permute-start(bf16[96,512]{1,0:T(8,128)(2,1)S(1)} %get-tuple-element.97._), channel_id=1, source_target_pairs={{128,64},{129,65},{130,66},{131,67},{132,68},{133,69},{134,70},{13... | collective-permute-start | bytes 294920 | tf_op jit(solution)/shard_map/ppermute | solution.py:203
  89.8 5.9 %collective-permute-start.18 = (bf16[96,512]{1,0:T(8,128)(2,1)S(1)}, bf16[96,512]{1,0:T(8,128)(2,1)S(1)}, u32[]{:S(2)}, u32[]{:S(2)}) collective-permute-start(bf16[96,512]{1,0:T(8,128)(2,1)S(1)} %get-tuple-element.99._), channel_id=1, source_target_pairs={{128,64},{129,65},{130,66},{131,67},{132,68},{133,69},{134,70},{13... | collective-permute-start | bytes 294920 | tf_op jit(solution)/shard_map/ppermute | solution.py:203
  91.0 6.5 %collective-permute-start.19 = (bf16[96,512]{1,0:T(8,128)(2,1)S(1)}, bf16[96,512]{1,0:T(8,128)(2,1)S(1)}, u32[]{:S(2)}, u32[]{:S(2)}) collective-permute-start(bf16[96,512]{1,0:T(8,128)(2,1)S(1)} %get-tuple-element.101._), channel_id=1, source_target_pairs={{128,64},{129,65},{130,66},{131,67},{132,68},{133,69},{134,70},{13... | collective-permute-start | bytes 294920 | tf_op jit(solution)/shard_map/ppermute | solution.py:203
  94.3 23.5 %collective-permute-start.20 = (bf16[96,512]{1,0:T(8,128)(2,1)S(1)}, bf16[96,512]{1,0:T(8,128)(2,1)S(1)}, u32[]{:S(2)}, u32[]{:S(2)}) collective-permute-start(bf16[96,512]{1,0:T(8,128)(2,1)S(1)} %get-tuple-element.107._), channel_id=1, source_target_pairs={{64,0},{65,1},{66,2},{67,3},{68,4},{69,5},{70,6},{71,7},{72,8},{73... | collective-permute-start | bytes 294920 | tf_op jit(solution)/shard_map/ppermute | solution.py:203
  96.2 26.9 %collective-permute-start.21 = (bf16[96,512]{1,0:T(8,128)(2,1)S(1)}, bf16[96,512]{1,0:T(8,128)(2,1)S(1)}, u32[]{:S(2)}, u32[]{:S(2)}) collective-permute-start(bf16[96,512]{1,0:T(8,128)(2,1)S(1)} %get-tuple-element.109._), channel_id=1, source_target_pairs={{64,0},{65,1},{66,2},{67,3},{68,4},{69,5},{70,6},{71,7},{72,8},{73... | collective-permute-start | bytes 294920 | tf_op jit(solution)/shard_map/ppermute | solution.py:203
  98.1 29.1 %collective-permute-start.22 = (bf16[96,512]{1,0:T(8,128)(2,1)S(1)}, bf16[96,512]{1,0:T(8,128)(2,1)S(1)}, u32[]{:S(2)}, u32[]{:S(2)}) collective-permute-start(bf16[96,512]{1,0:T(8,128)(2,1)S(1)} %get-tuple-element.111._), channel_id=1, source_target_pairs={{64,0},{65,1},{66,2},{67,3},{68,4},{69,5},{70,6},{71,7},{72,8},{73... | collective-permute-start | bytes 294920 | tf_op jit(solution)/shard_map/ppermute | solution.py:203
  145.2 9.7 %collective-permute-start.23 = (bf16[4,2,2,32,512]{4,3,2,1,0:T(8,128)(2,1)S(1)}, bf16[4,2,2,32,512]{4,3,2,1,0:T(8,128)(2,1)S(1)}, u32[]{:S(2)}, u32[]{:S(2)}) collective-permute-start(bf16[4,2,2,32,512]{4,3,2,1,0:T(8,128)(2,1)S(1)} %get-tuple-element.119), channel_id=1, source_target_pairs={{0,1},{1,0},{2,3},{3,2},{4,5},{5,4},{6,7},{7,6},{8,9},{9,8},{10,11... | collective-permute-start | bytes 1572872 | tf_op jit(solution)/shard_map/ppermute | solution.py:229
  155.9 12.7 %all-to-all-start.3 = ((bf16[4,2,2,32,512]{4,3,2,1,0:T(8,128)(2,1)}), bf16[4,2,2,32,512]{4,3,2,1,0:T(8,128)(2,1)S(1)}, u32[]{:S(2)}, u32[]{:S(2)}) async-start(bf16[4,2,2,32,512]{4,3,2,1,0:T(8,128)(2,1)} %shard_map.94), calls=%async_computation.3 | async-start | bytes 1048576 | tf_op jit(solution)/shard_map/all_to_all | solution.py:230
  168.6 14.4 %collective-permute-start.24 = (bf16[2,32,512]{2,1,0:T(8,128)(2,1)S(1)}, bf16[2,32,512]{2,1,0:T(8,128)(2,1)S(1)}, u32[]{:S(2)}, u32[]{:S(2)}) collective-permute-start(bf16[2,32,512]{2,1,0:T(8,128)(2,1)S(1)} %fusion.1), channel_id=1, source_target_pairs={{0,8},{8,0},{1,9},{9,1},{2,10},{10,2},{3,11},{11,3},{4,12},{12,4},... | collective-permute-start | bytes 196616 | tf_op jit(solution)/shard_map/ppermute | solution.py:245
  (9 other events, 104.5 us)

commit v5 on v4

--- a/solution.py
+++ b/solution.py
@@ -1,4 +1,5 @@
 import functools
+import math
 
 import jax
 import jax.numpy as jnp
@@ -119,6 +120,12 @@
 
 def add_kernel(own, arrived, total):
     total[...] = (own[...] + arrived[...].astype(F32)).astype(BF16)
+
+
+def split_kernel(factor, place, parts, sent, own):
+    zh = place[2]
+    own[...] = sum(parts[x, zh].astype(F32) for x in range(NX)) * factor
+    sent[...] = (sum(parts[x, 1 - zh].astype(F32) for x in range(NX)) * factor).astype(BF16)
 
 
 def input_kernel(place, home_g, dz, weights, dx):
@@ -228,6 +235,13 @@
     )
     (total,) = call(add_kernel, (struct(half, BF16),), own, lax.ppermute(sent, "core", SWAP))
     parts = lax.all_to_all(total, "x", 0, 0)
+    factor = 4.0 / math.sqrt(micro * rows * NH * NX * NC)
+    sent, own = call(
+        functools.partial(split_kernel, factor),
+        (struct((2, shard, width), BF16), struct((2, shard, width), F32)),
+        place,
+        parts,
+    )
     (dx,) = call(
         input_kernel,
         (struct(home_g.shape, BF16),),
@@ -235,14 +249,10 @@
         home_g,
         dz,
         weights,
-        after=parts,
+        after=sent,
         flops=2 * micro * rows * width * width,
     )
-    total = parts.astype(F32).sum(axis=0)
-    sent = lax.dynamic_index_in_dim(total, 1 - zh, 0, keepdims=False).astype(BF16)
-    own = lax.dynamic_index_in_dim(total, zh, 0, keepdims=False)
-    factor = 4.0 / jnp.sqrt(F32(micro * rows * NH * NX * NC))
-    reduced = (own + lax.ppermute(sent, "z_hi", SWAP)) * factor
+    reduced = own + lax.ppermute(sent, "z_hi", SWAP)
     return (reduced[0:1], reduced[1:2], dx.reshape(1, micro, rows, width))
 
 

time: 185 us -> 183 us (0.989)
  blocking collectives: 45.1 us -> 56.7 us
  waiting for transfers between devices: 44.5 us -> 37.4 us
  starting transfers between devices: 59.5 us -> 56 us
  local copies, waits for them, and re-layouts: 4.76 us -> 2.56 us
    all_to_all x0 -> x1, blocking collectives: none -> 11.6 us  [body(): parts = lax.all_to_all(total, 'x', 0, 0)]
    all_to_all x1 -> x0, waiting for transfers between devices: 9.2 us -> none  [body(): parts = lax.all_to_all(total, 'x', 0, 0)]
    all_to_all x1 -> x0, starting transfers between devices: 3.47 us -> none  [body(): parts = lax.all_to_all(total, 'x', 0, 0)]
    unnamed x12 -> x8, local copies, waits for them, and re-layouts: 2.2 us -> 0.02 us
    ppermute x1, waiting for transfers between devices: 5.17 us -> 7.32 us  [body(): reduced = own + lax.ppermute(sent, 'z_hi', SWAP)]
    pallas_call x29 -> x30, Pallas kernels: 28.5 us -> 28.3 us  [call(): pl.pallas_call(kernel, out_shape=out_shape, in_specs=specs, out_specs=jax...]
  transfers between devices with their start and end apart: 27 -> 26, of which waited for: 8 -> 7; matrix products, arithmetic and copies ran while one was open for 1% -> 1% of each run, Pallas kernels for 10% -> 11%
where the time goes in v5:
time: 183 us; the launch traced here: 182 us
  blocking collectives  56.7 us (31%)
  starting transfers between devices  56 us (31%)
  waiting for transfers between devices  37.4 us (20%)
  Pallas kernels  28.3 us (15%)
  local copies, waits for them, and re-layouts  2.56 us (1%)
    all_to_all x1, blocking collectives, body(): lax.all_to_all(block, PLANE, 0, 0).reshape(NY, NX, 2, 2, shard, width)  31.5 us
    pallas_call x30, Pallas kernels, call(): pl.pallas_call(kernel, out_shape=out_shape, in_specs=specs, out_specs=jax...  28.3 us
    ppermute x21, waiting for transfers between devices, body(): lax.ppermute(sending, 'z_lo', [(NZ - 1 - stage, NZ - 2 - stage)])  24.6 us
    ppermute x21, starting transfers between devices, body(): lax.ppermute(sending, 'z_lo', [(NZ - 1 - stage, NZ - 2 - stage)])  15.9 us
    ppermute x1, starting transfers between devices, body(): far = lax.ppermute(own, 'z_hi', SWAP)  15.4 us
    all_to_all x1, blocking collectives, body(): home_g = lax.all_to_all(kept[-1], 'y', 0, 0).reshape(micro * rows, width)  13.6 us
    all_to_all x1, blocking collectives, body(): parts = lax.all_to_all(total, 'x', 0, 0)  11.6 us
    ppermute x1, starting transfers between devices, body(): lax.ppermute(sent, 'core', SWAP)  8.21 us
  transfers between devices with their start and end apart: 26, of which 7 were waited for; matrix products, arithmetic and copies ran while one was open for 1% of the time, Pallas kernels for 11%

profile of v5, /device:TPU:1, one launch (start us, length us, event | category | flops | bytes accessed | tf_op | source)
XLA Modules:
  0.0 182.4 jit_solution(12269511711057616612)
XLA Ops:
  0.7 5.2 %all-to-all-start = ((bf16[4,288,512]{2,1,0:T(8,128)(2,1)}), bf16[4,288,512]{2,1,0:T(8,128)(2,1)S(1)}, u32[]{:S(2)}, u32[]{:S(2)}) async-start(bf16[4,288,512]{2,1,0:T(8,128)(2,1)} %bitcast.21), calls=%async_computation | async-start | bytes 2359296 | tf_op jit(solution)/shard_map/all_to_all | solution.py:167
  5.8 15.4 %collective-permute-start = (bf16[2,32,512]{2,1,0:T(8,128)(2,1)S(1)}, bf16[2,32,512]{2,1,0:T(8,128)(2,1)S(1)}, u32[]{:S(2)}, u32[]{:S(2)}) collective-permute-start(bf16[2,32,512]{2,1,0:T(8,128)(2,1)S(1)} %pad_maximum_fusion.1), channel_id=1, source_target_pairs={{0,8},{8,0},{1,9},{9,1},{2,10},{10,2},{3,11},{11,3},{4,12},{12,4},... | collective-permute-start | bytes 196616 | tf_op jit(solution)/shard_map/ppermute | solution.py:169
  21.3 1.7 dynamic-slice_bitcast_fusion
  23.3 31.5 %all_to_all.20 = bf16[16,128,512]{2,1,0:T(8,128)(2,1)S(1)} all-to-all(bf16[16,128,512]{2,1,0:T(8,128)(2,1)S(1)} %broadcast_in_dim.8), channel_id=1, replica_groups=mesh['z_lo'=8,'y'=4,'z_hi'=2,'x'=4,'core'=2] {'y','x'}, dimensions={0} | all-to-all | bytes 4194304 | tf_op jit(solution)/shard_map/all_to_all | solution.py:175
  54.8 6.6 %collective-permute-start.1 = (bf16[4,4,2,2,32,512]{5,4,3,2,1,0:T(8,128)(2,1)S(1)}, bf16[4,4,2,2,32,512]{5,4,3,2,1,0:T(8,128)(2,1)}, u32[]{:S(2)}, u32[]{:S(2)}) collective-permute-start(bf16[4,4,2,2,32,512]{5,4,3,2,1,0:T(8,128)(2,1)S(1)} %bitcast.19), channel_id=1, source_target_pairs={{0,1},{1,0},{2,3},{3,2},{4,5},{5,4},{6,7},{7,6},{8,9},{9,8},{10,11... | collective-permute-start | bytes 6291464 | tf_op jit(solution)/shard_map/ppermute | solution.py:176
  61.4 3.8 %collective-permute-done.1.other = bf16[4,4,2,2,32,512]{5,4,3,2,1,0:T(8,128)(2,1)} collective-permute-done((bf16[4,4,2,2,32,512]{5,4,3,2,1,0:T(8,128)(2,1)S(1)}, bf16[4,4,2,2,32,512]{5,4,3,2,1,0:T(8,128)(2,1)}, u32[]{:S(2)}, u32[]{:S(2)}) %collective-permute-start.1) | collective-permute-done | bytes 2097184 | tf_op jit(solution)/shard_map/ppermute | solution.py:176
  65.2 3.3 %shard_map.67 = (bf16[4,2,512,512]{3,2,1,0:T(8,128)(2,1)S(1)}, f32[4,288,512]{2,1,0:T(8,128)S(1)}) custom-call(s32[4]{0:T(128)S(1)} %pad_add_fusion.place.refs_0_, bf16[4,4,2,2,32,512]{5,4,3,2,1,0:T(8,128)(2,1)S(1)} %bitcast.20, bf16[4,4,2,2,32,512]{5,4,3,2,1,0:T(8,128)(2,1)} %collective-permute-done.1.other, bf16[4,288,512]{2,1,0:T(8,128)(2,1)S(1)} %all-to-all-done.inputs), custom_call_target="tpu_custom_call" | custom-call | flops 603979776 | tf_op jit(solution)/shard_map/pallas_call | solution.py:50
  91.7 2.0 %shard_map.86 = (f32[1152,512]{1,0:T(8,128)S(1)}, bf16[512,1152]{1,0:T(8,128)(2,1)S(1)}, bf16[512,1152]{1,0:T(8,128)(2,1)S(1)}) custom-call(bf16[96,512]{1,0:T(8,128)(2,1)S(1)} %get-tuple-element.103._, s32[4]{0:T(128)S(1)} %pad_add_fusion.place.refs_0_, bf16[1152,512]{1,0:T(8,128)(2,1)S(1)} %bitcast.22, ...), custom_call_target="tpu_custom_call" | custom-call | flops 603979776 | tf_op jit(solution)/shard_map/pallas_call | solution.py:50
  94.3 1.3 collective-permute-start.20
  96.2 1.3 collective-permute-start.21
  99.4 18.4 %collective-permute-done.20.refs_1_ = bf16[96,512]{1,0:T(8,128)(2,1)S(1)} collective-permute-done((bf16[96,512]{1,0:T(8,128)(2,1)S(1)}, bf16[96,512]{1,0:T(8,128)(2,1)S(1)}, u32[]{:S(2)}, u32[]{:S(2)}) %collective-permute-start.20) | collective-permute-done | bytes 98336 | tf_op jit(solution)/shard_map/ppermute | solution.py:210
  117.8 1.6 shard_map.90._.refs_5_
  119.4 3.6 %collective-permute-done.21.refs_1_ = bf16[96,512]{1,0:T(8,128)(2,1)S(1)} collective-permute-done((bf16[96,512]{1,0:T(8,128)(2,1)S(1)}, bf16[96,512]{1,0:T(8,128)(2,1)S(1)}, u32[]{:S(2)}, u32[]{:S(2)}) %collective-permute-start.21) | collective-permute-done | bytes 98336 | tf_op jit(solution)/shard_map/ppermute | solution.py:210
  123.1 1.6 shard_map.91._.refs_6_
  124.7 2.5 %collective-permute-done.22.refs_1_ = bf16[96,512]{1,0:T(8,128)(2,1)S(1)} collective-permute-done((bf16[96,512]{1,0:T(8,128)(2,1)S(1)}, bf16[96,512]{1,0:T(8,128)(2,1)S(1)}, u32[]{:S(2)}, u32[]{:S(2)}) %collective-permute-start.22) | collective-permute-done | bytes 98336 | tf_op jit(solution)/shard_map/ppermute | solution.py:210
  127.2 1.6 shard_map.92
  128.8 13.6 %all_to_all.21 = bf16[4,288,512]{2,1,0:T(8,128)(2,1)S(1)} all-to-all(bf16[4,288,512]{2,1,0:T(8,128)(2,1)S(1)} %shard_map.92), channel_id=1, replica_groups=mesh['z_lo'=8,'y'=4,'z_hi'=2,'x'=4,'core'=2] {'y'}, dimensions={0} | all-to-all | bytes 2359296 | tf_op jit(solution)/shard_map/all_to_all | solution.py:224
  142.4 2.8 %shard_map.93 = (bf16[1152,512]{1,0:T(8,128)(2,1)S(1)}, bf16[4,2,2,32,512]{4,3,2,1,0:T(8,128)(2,1)S(1)}, f32[4,2,2,32,512]{4,3,2,1,0:T(8,128)S(1)}) custom-call(s32[4]{0:T(128)S(1)} %pad_add_fusion.place.refs_0_, bf16[1152,512]{1,0:T(8,128)(2,1)S(1)} %bitcast.17, bf16[4,2,512,512]{3,2,1,0:T(8,128)(2,1)S(1)} %get-tuple-element.67.weights.refs_2_.refs_3_, ...), custom_call_target="tpu_custom_call" | custom-call | flops 1811939328 | tf_op jit(solution)/shard_map/pallas_call | solution.py:50
  145.2 8.2 %collective-permute-start.23 = (bf16[4,2,2,32,512]{4,3,2,1,0:T(8,128)(2,1)S(1)}, bf16[4,2,2,32,512]{4,3,2,1,0:T(8,128)(2,1)S(1)}, u32[]{:S(2)}, u32[]{:S(2)}) collective-permute-start(bf16[4,2,2,32,512]{4,3,2,1,0:T(8,128)(2,1)S(1)} %get-tuple-element.121), channel_id=1, source_target_pairs={{0,1},{1,0},{2,3},{3,2},{4,5},{5,4},{6,7},{7,6},{8,9},{9,8},{10,11... | collective-permute-start | bytes 1572872 | tf_op jit(solution)/shard_map/ppermute | solution.py:236
  153.4 1.5 collective-permute-done.23.arrived
  155.0 11.6 %all_to_all.22.parts = bf16[4,2,2,32,512]{4,3,2,1,0:T(8,128)(2,1)S(1)} all-to-all(bf16[4,2,2,32,512]{4,3,2,1,0:T(8,128)(2,1)S(1)} %shard_map.94), channel_id=1, replica_groups=mesh['z_lo'=8,'y'=4,'z_hi'=2,'x'=4,'core'=2] {'x'}, dimensions={0} | all-to-all | bytes 1048576 | tf_op jit(solution)/shard_map/all_to_all | solution.py:237
  167.3 4.8 %collective-permute-start.24 = (bf16[2,32,512]{2,1,0:T(8,128)(2,1)S(1)}, bf16[2,32,512]{2,1,0:T(8,128)(2,1)S(1)}, u32[]{:S(2)}, u32[]{:S(2)}) collective-permute-start(bf16[2,32,512]{2,1,0:T(8,128)(2,1)S(1)} %get-tuple-element.123._), channel_id=1, source_target_pairs={{0,8},{8,0},{1,9},{9,1},{2,10},{10,2},{3,11},{11,3},{4,12},{12,4},... | collective-permute-start | bytes 196616 | tf_op jit(solution)/shard_map/ppermute | solution.py:255
  172.1 2.3 %shard_map.96 = bf16[1152,512]{1,0:T(8,128)(2,1)} custom-call(bf16[2,32,512]{2,1,0:T(8,128)(2,1)S(1)} %get-tuple-element.123._, s32[4]{0:T(128)S(1)} %pad_add_fusion.place.refs_0_, bf16[1152,512]{1,0:T(8,128)(2,1)S(1)} %bitcast.18, bf16[1152,512]{1,0:T(8,128)(2,1)S(1)} %get-tuple-element.124.refs_2_, ...), custom_call_target="tpu_custom_call" | custom-call | flops 603979776 | tf_op jit(solution)/shard_map/pallas_call | solution.py:50
  174.4 7.3 %collective-permute-done.24 = bf16[2,32,512]{2,1,0:T(8,128)(2,1)S(1)} collective-permute-done((bf16[2,32,512]{2,1,0:T(8,128)(2,1)S(1)}, bf16[2,32,512]{2,1,0:T(8,128)(2,1)S(1)}, u32[]{:S(2)}, u32[]{:S(2)}) %collective-permute-start.24) | collective-permute-done | bytes 65568 | tf_op jit(solution)/shard_map/ppermute | solution.py:255
  (77 shorter events, 27.6 us)
Async XLA Ops:
  0.7 22.4 %all-to-all-start = ((bf16[4,288,512]{2,1,0:T(8,128)(2,1)}), bf16[4,288,512]{2,1,0:T(8,128)(2,1)S(1)}, u32[]{:S(2)}, u32[]{:S(2)}) async-start(bf16[4,288,512]{2,1,0:T(8,128)(2,1)} %bitcast.21), calls=%async_computation | async-start | bytes 2359296 | tf_op jit(solution)/shard_map/all_to_all | solution.py:167
  5.8 17.2 %collective-permute-start = (bf16[2,32,512]{2,1,0:T(8,128)(2,1)S(1)}, bf16[2,32,512]{2,1,0:T(8,128)(2,1)S(1)}, u32[]{:S(2)}, u32[]{:S(2)}) collective-permute-start(bf16[2,32,512]{2,1,0:T(8,128)(2,1)S(1)} %pad_maximum_fusion.1), channel_id=1, source_target_pairs={{0,8},{8,0},{1,9},{9,1},{2,10},{10,2},{3,11},{11,3},{4,12},{12,4},... | collective-permute-start | bytes 196616 | tf_op jit(solution)/shard_map/ppermute | solution.py:169
  54.8 10.5 %collective-permute-start.1 = (bf16[4,4,2,2,32,512]{5,4,3,2,1,0:T(8,128)(2,1)S(1)}, bf16[4,4,2,2,32,512]{5,4,3,2,1,0:T(8,128)(2,1)}, u32[]{:S(2)}, u32[]{:S(2)}) collective-permute-start(bf16[4,4,2,2,32,512]{5,4,3,2,1,0:T(8,128)(2,1)S(1)} %bitcast.19), channel_id=1, source_target_pairs={{0,1},{1,0},{2,3},{3,2},{4,5},{5,4},{6,7},{7,6},{8,9},{9,8},{10,11... | collective-permute-start | bytes 6291464 | tf_op jit(solution)/shard_map/ppermute | solution.py:176
  71.7 3.2 %collective-permute-start.4 = (bf16[96,512]{1,0:T(8,128)(2,1)S(1)}, bf16[96,512]{1,0:T(8,128)(2,1)S(1)}, u32[]{:S(2)}, u32[]{:S(2)}) collective-permute-start(bf16[96,512]{1,0:T(8,128)(2,1)S(1)} %get-tuple-element.73._), channel_id=1, source_target_pairs={{448,384},{449,385},{450,386},{451,387},{452,388},{453,389},{454,3... | collective-permute-start | bytes 294920 | tf_op jit(solution)/shard_map/ppermute | solution.py:210
  73.0 3.2 %collective-permute-start.5 = (bf16[96,512]{1,0:T(8,128)(2,1)S(1)}, bf16[96,512]{1,0:T(8,128)(2,1)S(1)}, u32[]{:S(2)}, u32[]{:S(2)}) collective-permute-start(bf16[96,512]{1,0:T(8,128)(2,1)S(1)} %get-tuple-element.75._), channel_id=1, source_target_pairs={{384,320},{385,321},{386,322},{387,323},{388,324},{389,325},{390,3... | collective-permute-start | bytes 294920 | tf_op jit(solution)/shard_map/ppermute | solution.py:210
  74.3 3.2 %collective-permute-start.6 = (bf16[96,512]{1,0:T(8,128)(2,1)S(1)}, bf16[96,512]{1,0:T(8,128)(2,1)S(1)}, u32[]{:S(2)}, u32[]{:S(2)}) collective-permute-start(bf16[96,512]{1,0:T(8,128)(2,1)S(1)} %get-tuple-element.77._), channel_id=1, source_target_pairs={{384,320},{385,321},{386,322},{387,323},{388,324},{389,325},{390,3... | collective-permute-start | bytes 294920 | tf_op jit(solution)/shard_map/ppermute | solution.py:210
  75.6 3.2 %collective-permute-start.7 = (bf16[96,512]{1,0:T(8,128)(2,1)S(1)}, bf16[96,512]{1,0:T(8,128)(2,1)S(1)}, u32[]{:S(2)}, u32[]{:S(2)}) collective-permute-start(bf16[96,512]{1,0:T(8,128)(2,1)S(1)} %get-tuple-element.79._), channel_id=1, source_target_pairs={{384,320},{385,321},{386,322},{387,323},{388,324},{389,325},{390,3... | collective-permute-start | bytes 294920 | tf_op jit(solution)/shard_map/ppermute | solution.py:210
  76.8 3.2 %collective-permute-start.8 = (bf16[96,512]{1,0:T(8,128)(2,1)S(1)}, bf16[96,512]{1,0:T(8,128)(2,1)S(1)}, u32[]{:S(2)}, u32[]{:S(2)}) collective-permute-start(bf16[96,512]{1,0:T(8,128)(2,1)S(1)} %get-tuple-element.81._), channel_id=1, source_target_pairs={{320,256},{321,257},{322,258},{323,259},{324,260},{325,261},{326,2... | collective-permute-start | bytes 294920 | tf_op jit(solution)/shard_map/ppermute | solution.py:210
  78.1 3.2 %collective-permute-start.9 = (bf16[96,512]{1,0:T(8,128)(2,1)S(1)}, bf16[96,512]{1,0:T(8,128)(2,1)S(1)}, u32[]{:S(2)}, u32[]{:S(2)}) collective-permute-start(bf16[96,512]{1,0:T(8,128)(2,1)S(1)} %get-tuple-element.83._), channel_id=1, source_target_pairs={{320,256},{321,257},{322,258},{323,259},{324,260},{325,261},{326,2... | collective-permute-start | bytes 294920 | tf_op jit(solution)/shard_map/ppermute | solution.py:210
  79.4 3.2 %collective-permute-start.10 = (bf16[96,512]{1,0:T(8,128)(2,1)S(1)}, bf16[96,512]{1,0:T(8,128)(2,1)S(1)}, u32[]{:S(2)}, u32[]{:S(2)}) collective-permute-start(bf16[96,512]{1,0:T(8,128)(2,1)S(1)} %get-tuple-element.85._), channel_id=1, source_target_pairs={{320,256},{321,257},{322,258},{323,259},{324,260},{325,261},{326,2... | collective-permute-start | bytes 294920 | tf_op jit(solution)/shard_map/ppermute | solution.py:210
  80.7 3.2 %collective-permute-start.11 = (bf16[96,512]{1,0:T(8,128)(2,1)S(1)}, bf16[96,512]{1,0:T(8,128)(2,1)S(1)}, u32[]{:S(2)}, u32[]{:S(2)}) collective-permute-start(bf16[96,512]{1,0:T(8,128)(2,1)S(1)} %get-tuple-element.87._), channel_id=1, source_target_pairs={{256,192},{257,193},{258,194},{259,195},{260,196},{261,197},{262,1... | collective-permute-start | bytes 294920 | tf_op jit(solution)/shard_map/ppermute | solution.py:210
  81.9 3.2 %collective-permute-start.12 = (bf16[96,512]{1,0:T(8,128)(2,1)S(1)}, bf16[96,512]{1,0:T(8,128)(2,1)S(1)}, u32[]{:S(2)}, u32[]{:S(2)}) collective-permute-start(bf16[96,512]{1,0:T(8,128)(2,1)S(1)} %get-tuple-element.89._), channel_id=1, source_target_pairs={{256,192},{257,193},{258,194},{259,195},{260,196},{261,197},{262,1... | collective-permute-start | bytes 294920 | tf_op jit(solution)/shard_map/ppermute | solution.py:210
  83.2 3.2 %collective-permute-start.13 = (bf16[96,512]{1,0:T(8,128)(2,1)S(1)}, bf16[96,512]{1,0:T(8,128)(2,1)S(1)}, u32[]{:S(2)}, u32[]{:S(2)}) collective-permute-start(bf16[96,512]{1,0:T(8,128)(2,1)S(1)} %get-tuple-element.91._), channel_id=1, source_target_pairs={{256,192},{257,193},{258,194},{259,195},{260,196},{261,197},{262,1... | collective-permute-start | bytes 294920 | tf_op jit(solution)/shard_map/ppermute | solution.py:210
  84.5 3.4 %collective-permute-start.14 = (bf16[96,512]{1,0:T(8,128)(2,1)S(1)}, bf16[96,512]{1,0:T(8,128)(2,1)S(1)}, u32[]{:S(2)}, u32[]{:S(2)}) collective-permute-start(bf16[96,512]{1,0:T(8,128)(2,1)S(1)} %get-tuple-element.93._), channel_id=1, source_target_pairs={{192,128},{193,129},{194,130},{195,131},{196,132},{197,133},{198,1... | collective-permute-start | bytes 294920 | tf_op jit(solution)/shard_map/ppermute | solution.py:210
  85.7 3.4 %collective-permute-start.15 = (bf16[96,512]{1,0:T(8,128)(2,1)S(1)}, bf16[96,512]{1,0:T(8,128)(2,1)S(1)}, u32[]{:S(2)}, u32[]{:S(2)}) collective-permute-start(bf16[96,512]{1,0:T(8,128)(2,1)S(1)} %get-tuple-element.95._), channel_id=1, source_target_pairs={{192,128},{193,129},{194,130},{195,131},{196,132},{197,133},{198,1... | collective-permute-start | bytes 294920 | tf_op jit(solution)/shard_map/ppermute | solution.py:210
  87.2 3.2 %collective-permute-start.16 = (bf16[96,512]{1,0:T(8,128)(2,1)S(1)}, bf16[96,512]{1,0:T(8,128)(2,1)S(1)}, u32[]{:S(2)}, u32[]{:S(2)}) collective-permute-start(bf16[96,512]{1,0:T(8,128)(2,1)S(1)} %get-tuple-element.97._), channel_id=1, source_target_pairs={{192,128},{193,129},{194,130},{195,131},{196,132},{197,133},{198,1... | collective-permute-start | bytes 294920 | tf_op jit(solution)/shard_map/ppermute | solution.py:210
  88.5 5.2 %collective-permute-start.17 = (bf16[96,512]{1,0:T(8,128)(2,1)S(1)}, bf16[96,512]{1,0:T(8,128)(2,1)S(1)}, u32[]{:S(2)}, u32[]{:S(2)}) collective-permute-start(bf16[96,512]{1,0:T(8,128)(2,1)S(1)} %get-tuple-element.99._), channel_id=1, source_target_pairs={{128,64},{129,65},{130,66},{131,67},{132,68},{133,69},{134,70},{13... | collective-permute-start | bytes 294920 | tf_op jit(solution)/shard_map/ppermute | solution.py:210
  89.7 5.9 %collective-permute-start.18 = (bf16[96,512]{1,0:T(8,128)(2,1)S(1)}, bf16[96,512]{1,0:T(8,128)(2,1)S(1)}, u32[]{:S(2)}, u32[]{:S(2)}) collective-permute-start(bf16[96,512]{1,0:T(8,128)(2,1)S(1)} %get-tuple-element.101._), channel_id=1, source_target_pairs={{128,64},{129,65},{130,66},{131,67},{132,68},{133,69},{134,70},{13... | collective-permute-start | bytes 294920 | tf_op jit(solution)/shard_map/ppermute | solution.py:210
  91.0 6.5 %collective-permute-start.19 = (bf16[96,512]{1,0:T(8,128)(2,1)S(1)}, bf16[96,512]{1,0:T(8,128)(2,1)S(1)}, u32[]{:S(2)}, u32[]{:S(2)}) collective-permute-start(bf16[96,512]{1,0:T(8,128)(2,1)S(1)} %get-tuple-element.103._), channel_id=1, source_target_pairs={{128,64},{129,65},{130,66},{131,67},{132,68},{133,69},{134,70},{13... | collective-permute-start | bytes 294920 | tf_op jit(solution)/shard_map/ppermute | solution.py:210
  94.3 23.5 %collective-permute-start.20 = (bf16[96,512]{1,0:T(8,128)(2,1)S(1)}, bf16[96,512]{1,0:T(8,128)(2,1)S(1)}, u32[]{:S(2)}, u32[]{:S(2)}) collective-permute-start(bf16[96,512]{1,0:T(8,128)(2,1)S(1)} %get-tuple-element.109._), channel_id=1, source_target_pairs={{64,0},{65,1},{66,2},{67,3},{68,4},{69,5},{70,6},{71,7},{72,8},{73... | collective-permute-start | bytes 294920 | tf_op jit(solution)/shard_map/ppermute | solution.py:210
  96.2 26.9 %collective-permute-start.21 = (bf16[96,512]{1,0:T(8,128)(2,1)S(1)}, bf16[96,512]{1,0:T(8,128)(2,1)S(1)}, u32[]{:S(2)}, u32[]{:S(2)}) collective-permute-start(bf16[96,512]{1,0:T(8,128)(2,1)S(1)} %get-tuple-element.111._), channel_id=1, source_target_pairs={{64,0},{65,1},{66,2},{67,3},{68,4},{69,5},{70,6},{71,7},{72,8},{73... | collective-permute-start | bytes 294920 | tf_op jit(solution)/shard_map/ppermute | solution.py:210
  98.1 29.1 %collective-permute-start.22 = (bf16[96,512]{1,0:T(8,128)(2,1)S(1)}, bf16[96,512]{1,0:T(8,128)(2,1)S(1)}, u32[]{:S(2)}, u32[]{:S(2)}) collective-permute-start(bf16[96,512]{1,0:T(8,128)(2,1)S(1)} %get-tuple-element.113._), channel_id=1, source_target_pairs={{64,0},{65,1},{66,2},{67,3},{68,4},{69,5},{70,6},{71,7},{72,8},{73... | collective-permute-start | bytes 294920 | tf_op jit(solution)/shard_map/ppermute | solution.py:210
  145.2 9.7 %collective-permute-start.23 = (bf16[4,2,2,32,512]{4,3,2,1,0:T(8,128)(2,1)S(1)}, bf16[4,2,2,32,512]{4,3,2,1,0:T(8,128)(2,1)S(1)}, u32[]{:S(2)}, u32[]{:S(2)}) collective-permute-start(bf16[4,2,2,32,512]{4,3,2,1,0:T(8,128)(2,1)S(1)} %get-tuple-element.121), channel_id=1, source_target_pairs={{0,1},{1,0},{2,3},{3,2},{4,5},{5,4},{6,7},{7,6},{8,9},{9,8},{10,11... | collective-permute-start | bytes 1572872 | tf_op jit(solution)/shard_map/ppermute | solution.py:236
  167.3 14.4 %collective-permute-start.24 = (bf16[2,32,512]{2,1,0:T(8,128)(2,1)S(1)}, bf16[2,32,512]{2,1,0:T(8,128)(2,1)S(1)}, u32[]{:S(2)}, u32[]{:S(2)}) collective-permute-start(bf16[2,32,512]{2,1,0:T(8,128)(2,1)S(1)} %get-tuple-element.123._), channel_id=1, source_target_pairs={{0,8},{8,0},{1,9},{9,1},{2,10},{10,2},{3,11},{11,3},{4,12},{12,4},... | collective-permute-start | bytes 196616 | tf_op jit(solution)/shard_map/ppermute | solution.py:255
  (6 other events, 25.2 us)

commit v6 on v5

--- a/solution.py
+++ b/solution.py
@@ -12,12 +12,30 @@
 RHO = 0.25
 NZ, NY, NH, NX, NC = 8, 4, 2, 4, 2
 AXES = ("z_lo", "y", "z_hi", "x", "core")
-PLANE = ("y", "x")
+PLANE = ("y", "x", "core")
 CHUNKS = 3
 HOME_AT = NZ - 3
 MIB = 1024 * 1024
 BF16, F32 = jnp.bfloat16, jnp.float32
 SWAP = [(0, 1), (1, 0)]
+
+
+def plane_groups(first):
+    def at(y, x, core):
+        return (y * NX + x) * NC + core
+
+    groups = []
+    for core in range(NC):
+        if (core == 0) == first:
+            groups += [[at(y, x, core) for y in range(NY)] for x in range(NX)]
+        else:
+            groups += [[at(y, x, core) for x in range(NX)] for y in range(NY)]
+    return groups
+
+
+def gather_step(rows, first):
+    pieces = jnp.broadcast_to(rows[None], (NY, *rows.shape))
+    return lax.all_to_all(pieces, PLANE, 0, 0, axis_index_groups=plane_groups(first))
 
 
 def struct(shape, dtype):
@@ -59,18 +77,20 @@
 
 
 def prepare_kernel(place, mine, other, inputs, weights, slopes, natural):
-    rows = mine.shape[4]
+    rows = mine.shape[3]
+    core = place[1]
     near_at = place[2] * (NX * NC * rows)
     far_at = NX * NC * rows - near_at
     mine_at = place[1] * rows
     other_at = rows - mine_at
     for s in reversed(range(NY)):
-        for source, core_at in ((mine, mine_at), (other, other_at)):
+        for source, core_at, c in ((mine, mine_at, core), (other, other_at, 1 - core)):
             for half, half_at in enumerate((near_at, far_at)):
                 for x in range(NX):
                     at = pl.multiple_of(half_at + x * NC * rows + core_at, rows)
+                    entry = (1 - c) * (x * NY + s) + c * (s * NX + x)
                     for w in range(2):
-                        natural[s, w, pl.ds(at, rows)] = source[s, x, half, w]
+                        natural[s, w, pl.ds(at, rows)] = source[entry, half, w]
         slopes[s] = slope(dot(inputs[s], natural[s, 0], 1, 0))
         for w in range(2):
             weights[s, w] = natural[s, w].T
@@ -170,9 +190,9 @@
     given = lax.dynamic_index_in_dim(cotangent.reshape(NY, share, width), y, 0, keepdims=False)
     arriving = [given[m * part : (m + 1) * part] for m in range(CHUNKS)]
     far, stage_x, *arriving = lax.optimization_barrier((far, stage_x, *arriving))
-    block = jnp.concatenate([own, far], axis=0).reshape(1, 4 * shard, width)
-    block = jnp.broadcast_to(block, (NY * NX, 4 * shard, width))
-    mine = lax.all_to_all(block, PLANE, 0, 0).reshape(NY, NX, 2, 2, shard, width)
+    block = jnp.concatenate([own, far], axis=0).reshape(4 * shard, width)
+    block = gather_step(block, True).reshape(NY * 4 * shard, width)
+    mine = gather_step(block, False).reshape(NY * NX, 2, 2, shard, width)
     other = lax.ppermute(mine, "core", SWAP)
     weights, slopes = call(
         prepare_kernel,

time: 183 us -> 181 us (0.989)
  waiting for transfers between devices: 37.4 us -> 32.9 us
  starting transfers between devices: 56 us -> 59.2 us
    ppermute x21, waiting for transfers between devices: 24.6 us -> 22 us  [body(): lax.ppermute(sending, 'z_lo', [(NZ - 1 - stage, NZ - 2 - stage)])]
    ppermute x1, starting transfers between devices: 4.76 us -> 6.59 us  [body(): reduced = own + lax.ppermute(sent, 'z_hi', SWAP)]
    all_to_all x1 -> x2, blocking collectives: 31.5 us -> 30.4 us  [gather_step(): lax.all_to_all(pieces, PLANE, 0, 0, axis_index_groups=plane_groups(first))]
where the time goes in v6:
time: 181 us; the launch traced here: 180 us
  starting transfers between devices  59.2 us (33%)
  blocking collectives  55.6 us (31%)
  waiting for transfers between devices  32.9 us (18%)
  Pallas kernels  28.4 us (16%)
  local copies, waits for them, and re-layouts  2.56 us (1%)
    all_to_all x2, blocking collectives, gather_step(): lax.all_to_all(pieces, PLANE, 0, 0, axis_index_groups=plane_groups(first))  30.4 us
    pallas_call x30, Pallas kernels, call(): pl.pallas_call(kernel, out_shape=out_shape, in_specs=specs, out_specs=jax...  28.4 us
    ppermute x21, waiting for transfers between devices, body(): lax.ppermute(sending, 'z_lo', [(NZ - 1 - stage, NZ - 2 - stage)])  22 us
    ppermute x21, starting transfers between devices, body(): lax.ppermute(sending, 'z_lo', [(NZ - 1 - stage, NZ - 2 - stage)])  15.9 us
    ppermute x1, starting transfers between devices, body(): far = lax.ppermute(own, 'z_hi', SWAP)  15.4 us
    all_to_all x1, blocking collectives, body(): home_g = lax.all_to_all(kept[-1], 'y', 0, 0).reshape(micro * rows, width)  13.6 us
    all_to_all x1, blocking collectives, body(): parts = lax.all_to_all(total, 'x', 0, 0)  11.6 us
    ppermute x1, starting transfers between devices, body(): lax.ppermute(sent, 'core', SWAP)  8.21 us
  transfers between devices with their start and end apart: 26, of which 7 were waited for; matrix products, arithmetic and copies ran while one was open for 1% of the time, Pallas kernels for 11%

profile of v6, /device:TPU:1, one launch (start us, length us, event | category | flops | bytes accessed | tf_op | source)
XLA Modules:
  0.0 180.1 jit_solution(31154632406774535)
XLA Ops:
  0.7 5.2 %all-to-all-start = ((bf16[4,288,512]{2,1,0:T(8,128)(2,1)}), bf16[4,288,512]{2,1,0:T(8,128)(2,1)S(1)}, u32[]{:S(2)}, u32[]{:S(2)}) async-start(bf16[4,288,512]{2,1,0:T(8,128)(2,1)} %bitcast.22), calls=%async_computation | async-start | bytes 2359296 | tf_op jit(solution)/shard_map/all_to_all | solution.py:187
  5.8 15.4 %collective-permute-start = (bf16[2,32,512]{2,1,0:T(8,128)(2,1)S(1)}, bf16[2,32,512]{2,1,0:T(8,128)(2,1)S(1)}, u32[]{:S(2)}, u32[]{:S(2)}) collective-permute-start(bf16[2,32,512]{2,1,0:T(8,128)(2,1)S(1)} %pad_maximum_fusion.1), channel_id=1, source_target_pairs={{0,8},{8,0},{1,9},{9,1},{2,10},{10,2},{3,11},{11,3},{4,12},{12,4},... | collective-permute-start | bytes 196616 | tf_op jit(solution)/shard_map/ppermute | solution.py:189
  21.3 1.7 dynamic-slice_bitcast_fusion
  23.1 10.7 %all_to_all.25 = bf16[4,128,512]{2,1,0:T(8,128)(2,1)S(1)} all-to-all(bf16[4,128,512]{2,1,0:T(8,128)(2,1)S(1)} %broadcast_in_dim.15), channel_id=1, replica_groups={{0,16,32,48},{2,18,34,50},{4,20,36,52},{6,22,38,54},{1,3,5,7},{17,19,21..., dimensions={0} | all-to-all | bytes 1048576 | tf_op jit(solution)/shard_map/all_to_all | solution.py:38
  34.0 19.7 %all_to_all.26 = bf16[4,512,512]{2,1,0:T(8,128)(2,1)S(1)} all-to-all(bf16[4,512,512]{2,1,0:T(8,128)(2,1)S(1)} %broadcast_in_dim.17), channel_id=1, replica_groups={{0,2,4,6},{16,18,20,22},{32,34,36,38},{48,50,52,54},{1,17,33,49},{3,19,..., dimensions={0} | all-to-all | bytes 4194304 | tf_op jit(solution)/shard_map/all_to_all | solution.py:38
  53.7 7.9 %collective-permute-start.1 = (bf16[16,2,2,32,512]{4,3,2,1,0:T(8,128)(2,1)S(1)}, bf16[16,2,2,32,512]{4,3,2,1,0:T(8,128)(2,1)}, u32[]{:S(2)}, u32[]{:S(2)}) collective-permute-start(bf16[16,2,2,32,512]{4,3,2,1,0:T(8,128)(2,1)S(1)} %bitcast.20), channel_id=1, source_target_pairs={{0,1},{1,0},{2,3},{3,2},{4,5},{5,4},{6,7},{7,6},{8,9},{9,8},{10,11... | collective-permute-start | bytes 6291464 | tf_op jit(solution)/shard_map/ppermute | solution.py:196
  61.7 3.8 %collective-permute-done.1.other = bf16[16,2,2,32,512]{4,3,2,1,0:T(8,128)(2,1)} collective-permute-done((bf16[16,2,2,32,512]{4,3,2,1,0:T(8,128)(2,1)S(1)}, bf16[16,2,2,32,512]{4,3,2,1,0:T(8,128)(2,1)}, u32[]{:S(2)}, u32[]{:S(2)}) %collective-permute-start.1) | collective-permute-done | bytes 2097184 | tf_op jit(solution)/shard_map/ppermute | solution.py:196
  65.5 3.4 %shard_map.67 = (bf16[4,2,512,512]{3,2,1,0:T(8,128)(2,1)S(1)}, f32[4,288,512]{2,1,0:T(8,128)S(1)}) custom-call(s32[4]{0:T(128)S(1)} %pad_add_fusion.place.refs_0_, bf16[16,2,2,32,512]{4,3,2,1,0:T(8,128)(2,1)S(1)} %bitcast.21, bf16[16,2,2,32,512]{4,3,2,1,0:T(8,128)(2,1)} %collective-permute-done.1.other, bf16[4,288,512]{2,1,0:T(8,128)(2,1)S(1)} %all-to-all-done.inputs), custom_call_target="tpu_custom_call" | custom-call | flops 603979776 | tf_op jit(solution)/shard_map/pallas_call | solution.py:68
  92.0 2.0 %shard_map.86 = (f32[1152,512]{1,0:T(8,128)S(1)}, bf16[512,1152]{1,0:T(8,128)(2,1)S(1)}, bf16[512,1152]{1,0:T(8,128)(2,1)S(1)}) custom-call(bf16[96,512]{1,0:T(8,128)(2,1)S(1)} %get-tuple-element.103._, s32[4]{0:T(128)S(1)} %pad_add_fusion.place.refs_0_, bf16[1152,512]{1,0:T(8,128)(2,1)S(1)} %bitcast.23, ...), custom_call_target="tpu_custom_call" | custom-call | flops 603979776 | tf_op jit(solution)/shard_map/pallas_call | solution.py:68
  94.7 1.3 collective-permute-start.20
  99.8 15.8 %collective-permute-done.20.refs_1_ = bf16[96,512]{1,0:T(8,128)(2,1)S(1)} collective-permute-done((bf16[96,512]{1,0:T(8,128)(2,1)S(1)}, bf16[96,512]{1,0:T(8,128)(2,1)S(1)}, u32[]{:S(2)}, u32[]{:S(2)}) %collective-permute-start.20) | collective-permute-done | bytes 98336 | tf_op jit(solution)/shard_map/ppermute | solution.py:230
  115.6 1.6 shard_map.90._.refs_5_
  117.2 3.6 %collective-permute-done.21.refs_1_ = bf16[96,512]{1,0:T(8,128)(2,1)S(1)} collective-permute-done((bf16[96,512]{1,0:T(8,128)(2,1)S(1)}, bf16[96,512]{1,0:T(8,128)(2,1)S(1)}, u32[]{:S(2)}, u32[]{:S(2)}) %collective-permute-start.21) | collective-permute-done | bytes 98336 | tf_op jit(solution)/shard_map/ppermute | solution.py:230
  120.8 1.6 shard_map.91._.refs_6_
  122.4 2.5 %collective-permute-done.22.refs_1_ = bf16[96,512]{1,0:T(8,128)(2,1)S(1)} collective-permute-done((bf16[96,512]{1,0:T(8,128)(2,1)S(1)}, bf16[96,512]{1,0:T(8,128)(2,1)S(1)}, u32[]{:S(2)}, u32[]{:S(2)}) %collective-permute-start.22) | collective-permute-done | bytes 98336 | tf_op jit(solution)/shard_map/ppermute | solution.py:230
  124.9 1.6 shard_map.92
  126.5 13.6 %all_to_all.27 = bf16[4,288,512]{2,1,0:T(8,128)(2,1)S(1)} all-to-all(bf16[4,288,512]{2,1,0:T(8,128)(2,1)S(1)} %shard_map.92), channel_id=1, replica_groups=mesh['z_lo'=8,'y'=4,'z_hi'=2,'x'=4,'core'=2] {'y'}, dimensions={0} | all-to-all | bytes 2359296 | tf_op jit(solution)/shard_map/all_to_all | solution.py:244
  140.1 2.8 %shard_map.93 = (bf16[1152,512]{1,0:T(8,128)(2,1)S(1)}, bf16[4,2,2,32,512]{4,3,2,1,0:T(8,128)(2,1)S(1)}, f32[4,2,2,32,512]{4,3,2,1,0:T(8,128)S(1)}) custom-call(s32[4]{0:T(128)S(1)} %pad_add_fusion.place.refs_0_, bf16[1152,512]{1,0:T(8,128)(2,1)S(1)} %bitcast.18, bf16[4,2,512,512]{3,2,1,0:T(8,128)(2,1)S(1)} %get-tuple-element.67.weights.refs_2_.refs_3_, ...), custom_call_target="tpu_custom_call" | custom-call | flops 1811939328 | tf_op jit(solution)/shard_map/pallas_call | solution.py:68
  142.9 8.2 %collective-permute-start.23 = (bf16[4,2,2,32,512]{4,3,2,1,0:T(8,128)(2,1)S(1)}, bf16[4,2,2,32,512]{4,3,2,1,0:T(8,128)(2,1)S(1)}, u32[]{:S(2)}, u32[]{:S(2)}) collective-permute-start(bf16[4,2,2,32,512]{4,3,2,1,0:T(8,128)(2,1)S(1)} %get-tuple-element.121), channel_id=1, source_target_pairs={{0,1},{1,0},{2,3},{3,2},{4,5},{5,4},{6,7},{7,6},{8,9},{9,8},{10,11... | collective-permute-start | bytes 1572872 | tf_op jit(solution)/shard_map/ppermute | solution.py:256
  151.1 1.5 collective-permute-done.23.arrived
  152.7 11.6 %all_to_all.28.parts = bf16[4,2,2,32,512]{4,3,2,1,0:T(8,128)(2,1)S(1)} all-to-all(bf16[4,2,2,32,512]{4,3,2,1,0:T(8,128)(2,1)S(1)} %shard_map.94), channel_id=1, replica_groups=mesh['z_lo'=8,'y'=4,'z_hi'=2,'x'=4,'core'=2] {'x'}, dimensions={0} | all-to-all | bytes 1048576 | tf_op jit(solution)/shard_map/all_to_all | solution.py:257
  165.0 6.6 %collective-permute-start.24 = (bf16[2,32,512]{2,1,0:T(8,128)(2,1)S(1)}, bf16[2,32,512]{2,1,0:T(8,128)(2,1)S(1)}, u32[]{:S(2)}, u32[]{:S(2)}) collective-permute-start(bf16[2,32,512]{2,1,0:T(8,128)(2,1)S(1)} %get-tuple-element.123._), channel_id=1, source_target_pairs={{0,8},{8,0},{1,9},{9,1},{2,10},{10,2},{3,11},{11,3},{4,12},{12,4},... | collective-permute-start | bytes 196616 | tf_op jit(solution)/shard_map/ppermute | solution.py:275
  171.6 2.3 %shard_map.96 = bf16[1152,512]{1,0:T(8,128)(2,1)} custom-call(bf16[2,32,512]{2,1,0:T(8,128)(2,1)S(1)} %get-tuple-element.123._, s32[4]{0:T(128)S(1)} %pad_add_fusion.place.refs_0_, bf16[1152,512]{1,0:T(8,128)(2,1)S(1)} %bitcast.19, bf16[1152,512]{1,0:T(8,128)(2,1)S(1)} %get-tuple-element.124.refs_2_, ...), custom_call_target="tpu_custom_call" | custom-call | flops 603979776 | tf_op jit(solution)/shard_map/pallas_call | solution.py:68
  173.9 5.5 %collective-permute-done.24 = bf16[2,32,512]{2,1,0:T(8,128)(2,1)S(1)} collective-permute-done((bf16[2,32,512]{2,1,0:T(8,128)(2,1)S(1)}, bf16[2,32,512]{2,1,0:T(8,128)(2,1)S(1)}, u32[]{:S(2)}, u32[]{:S(2)}) %collective-permute-start.24) | collective-permute-done | bytes 65568 | tf_op jit(solution)/shard_map/ppermute | solution.py:275
  (79 shorter events, 28.9 us)
Async XLA Ops:
  0.7 22.4 %all-to-all-start = ((bf16[4,288,512]{2,1,0:T(8,128)(2,1)}), bf16[4,288,512]{2,1,0:T(8,128)(2,1)S(1)}, u32[]{:S(2)}, u32[]{:S(2)}) async-start(bf16[4,288,512]{2,1,0:T(8,128)(2,1)} %bitcast.22), calls=%async_computation | async-start | bytes 2359296 | tf_op jit(solution)/shard_map/all_to_all | solution.py:187
  5.8 17.2 %collective-permute-start = (bf16[2,32,512]{2,1,0:T(8,128)(2,1)S(1)}, bf16[2,32,512]{2,1,0:T(8,128)(2,1)S(1)}, u32[]{:S(2)}, u32[]{:S(2)}) collective-permute-start(bf16[2,32,512]{2,1,0:T(8,128)(2,1)S(1)} %pad_maximum_fusion.1), channel_id=1, source_target_pairs={{0,8},{8,0},{1,9},{9,1},{2,10},{10,2},{3,11},{11,3},{4,12},{12,4},... | collective-permute-start | bytes 196616 | tf_op jit(solution)/shard_map/ppermute | solution.py:189
  53.7 11.8 %collective-permute-start.1 = (bf16[16,2,2,32,512]{4,3,2,1,0:T(8,128)(2,1)S(1)}, bf16[16,2,2,32,512]{4,3,2,1,0:T(8,128)(2,1)}, u32[]{:S(2)}, u32[]{:S(2)}) collective-permute-start(bf16[16,2,2,32,512]{4,3,2,1,0:T(8,128)(2,1)S(1)} %bitcast.20), channel_id=1, source_target_pairs={{0,1},{1,0},{2,3},{3,2},{4,5},{5,4},{6,7},{7,6},{8,9},{9,8},{10,11... | collective-permute-start | bytes 6291464 | tf_op jit(solution)/shard_map/ppermute | solution.py:196
  72.0 3.2 %collective-permute-start.4 = (bf16[96,512]{1,0:T(8,128)(2,1)S(1)}, bf16[96,512]{1,0:T(8,128)(2,1)S(1)}, u32[]{:S(2)}, u32[]{:S(2)}) collective-permute-start(bf16[96,512]{1,0:T(8,128)(2,1)S(1)} %get-tuple-element.73._), channel_id=1, source_target_pairs={{448,384},{449,385},{450,386},{451,387},{452,388},{453,389},{454,3... | collective-permute-start | bytes 294920 | tf_op jit(solution)/shard_map/ppermute | solution.py:230
  73.3 3.2 %collective-permute-start.5 = (bf16[96,512]{1,0:T(8,128)(2,1)S(1)}, bf16[96,512]{1,0:T(8,128)(2,1)S(1)}, u32[]{:S(2)}, u32[]{:S(2)}) collective-permute-start(bf16[96,512]{1,0:T(8,128)(2,1)S(1)} %get-tuple-element.75._), channel_id=1, source_target_pairs={{384,320},{385,321},{386,322},{387,323},{388,324},{389,325},{390,3... | collective-permute-start | bytes 294920 | tf_op jit(solution)/shard_map/ppermute | solution.py:230
  74.6 3.2 %collective-permute-start.6 = (bf16[96,512]{1,0:T(8,128)(2,1)S(1)}, bf16[96,512]{1,0:T(8,128)(2,1)S(1)}, u32[]{:S(2)}, u32[]{:S(2)}) collective-permute-start(bf16[96,512]{1,0:T(8,128)(2,1)S(1)} %get-tuple-element.77._), channel_id=1, source_target_pairs={{384,320},{385,321},{386,322},{387,323},{388,324},{389,325},{390,3... | collective-permute-start | bytes 294920 | tf_op jit(solution)/shard_map/ppermute | solution.py:230
  75.9 3.2 %collective-permute-start.7 = (bf16[96,512]{1,0:T(8,128)(2,1)S(1)}, bf16[96,512]{1,0:T(8,128)(2,1)S(1)}, u32[]{:S(2)}, u32[]{:S(2)}) collective-permute-start(bf16[96,512]{1,0:T(8,128)(2,1)S(1)} %get-tuple-element.79._), channel_id=1, source_target_pairs={{384,320},{385,321},{386,322},{387,323},{388,324},{389,325},{390,3... | collective-permute-start | bytes 294920 | tf_op jit(solution)/shard_map/ppermute | solution.py:230
  77.1 3.2 %collective-permute-start.8 = (bf16[96,512]{1,0:T(8,128)(2,1)S(1)}, bf16[96,512]{1,0:T(8,128)(2,1)S(1)}, u32[]{:S(2)}, u32[]{:S(2)}) collective-permute-start(bf16[96,512]{1,0:T(8,128)(2,1)S(1)} %get-tuple-element.81._), channel_id=1, source_target_pairs={{320,256},{321,257},{322,258},{323,259},{324,260},{325,261},{326,2... | collective-permute-start | bytes 294920 | tf_op jit(solution)/shard_map/ppermute | solution.py:230
  78.4 3.2 %collective-permute-start.9 = (bf16[96,512]{1,0:T(8,128)(2,1)S(1)}, bf16[96,512]{1,0:T(8,128)(2,1)S(1)}, u32[]{:S(2)}, u32[]{:S(2)}) collective-permute-start(bf16[96,512]{1,0:T(8,128)(2,1)S(1)} %get-tuple-element.83._), channel_id=1, source_target_pairs={{320,256},{321,257},{322,258},{323,259},{324,260},{325,261},{326,2... | collective-permute-start | bytes 294920 | tf_op jit(solution)/shard_map/ppermute | solution.py:230
  79.7 3.2 %collective-permute-start.10 = (bf16[96,512]{1,0:T(8,128)(2,1)S(1)}, bf16[96,512]{1,0:T(8,128)(2,1)S(1)}, u32[]{:S(2)}, u32[]{:S(2)}) collective-permute-start(bf16[96,512]{1,0:T(8,128)(2,1)S(1)} %get-tuple-element.85._), channel_id=1, source_target_pairs={{320,256},{321,257},{322,258},{323,259},{324,260},{325,261},{326,2... | collective-permute-start | bytes 294920 | tf_op jit(solution)/shard_map/ppermute | solution.py:230
  81.0 3.2 %collective-permute-start.11 = (bf16[96,512]{1,0:T(8,128)(2,1)S(1)}, bf16[96,512]{1,0:T(8,128)(2,1)S(1)}, u32[]{:S(2)}, u32[]{:S(2)}) collective-permute-start(bf16[96,512]{1,0:T(8,128)(2,1)S(1)} %get-tuple-element.87._), channel_id=1, source_target_pairs={{256,192},{257,193},{258,194},{259,195},{260,196},{261,197},{262,1... | collective-permute-start | bytes 294920 | tf_op jit(solution)/shard_map/ppermute | solution.py:230
  82.2 3.2 %collective-permute-start.12 = (bf16[96,512]{1,0:T(8,128)(2,1)S(1)}, bf16[96,512]{1,0:T(8,128)(2,1)S(1)}, u32[]{:S(2)}, u32[]{:S(2)}) collective-permute-start(bf16[96,512]{1,0:T(8,128)(2,1)S(1)} %get-tuple-element.89._), channel_id=1, source_target_pairs={{256,192},{257,193},{258,194},{259,195},{260,196},{261,197},{262,1... | collective-permute-start | bytes 294920 | tf_op jit(solution)/shard_map/ppermute | solution.py:230
  83.5 3.2 %collective-permute-start.13 = (bf16[96,512]{1,0:T(8,128)(2,1)S(1)}, bf16[96,512]{1,0:T(8,128)(2,1)S(1)}, u32[]{:S(2)}, u32[]{:S(2)}) collective-permute-start(bf16[96,512]{1,0:T(8,128)(2,1)S(1)} %get-tuple-element.91._), channel_id=1, source_target_pairs={{256,192},{257,193},{258,194},{259,195},{260,196},{261,197},{262,1... | collective-permute-start | bytes 294920 | tf_op jit(solution)/shard_map/ppermute | solution.py:230
  84.8 3.4 %collective-permute-start.14 = (bf16[96,512]{1,0:T(8,128)(2,1)S(1)}, bf16[96,512]{1,0:T(8,128)(2,1)S(1)}, u32[]{:S(2)}, u32[]{:S(2)}) collective-permute-start(bf16[96,512]{1,0:T(8,128)(2,1)S(1)} %get-tuple-element.93._), channel_id=1, source_target_pairs={{192,128},{193,129},{194,130},{195,131},{196,132},{197,133},{198,1... | collective-permute-start | bytes 294920 | tf_op jit(solution)/shard_map/ppermute | solution.py:230
  86.0 3.4 %collective-permute-start.15 = (bf16[96,512]{1,0:T(8,128)(2,1)S(1)}, bf16[96,512]{1,0:T(8,128)(2,1)S(1)}, u32[]{:S(2)}, u32[]{:S(2)}) collective-permute-start(bf16[96,512]{1,0:T(8,128)(2,1)S(1)} %get-tuple-element.95._), channel_id=1, source_target_pairs={{192,128},{193,129},{194,130},{195,131},{196,132},{197,133},{198,1... | collective-permute-start | bytes 294920 | tf_op jit(solution)/shard_map/ppermute | solution.py:230
  87.5 3.2 %collective-permute-start.16 = (bf16[96,512]{1,0:T(8,128)(2,1)S(1)}, bf16[96,512]{1,0:T(8,128)(2,1)S(1)}, u32[]{:S(2)}, u32[]{:S(2)}) collective-permute-start(bf16[96,512]{1,0:T(8,128)(2,1)S(1)} %get-tuple-element.97._), channel_id=1, source_target_pairs={{192,128},{193,129},{194,130},{195,131},{196,132},{197,133},{198,1... | collective-permute-start | bytes 294920 | tf_op jit(solution)/shard_map/ppermute | solution.py:230
  88.8 5.3 %collective-permute-start.17 = (bf16[96,512]{1,0:T(8,128)(2,1)S(1)}, bf16[96,512]{1,0:T(8,128)(2,1)S(1)}, u32[]{:S(2)}, u32[]{:S(2)}) collective-permute-start(bf16[96,512]{1,0:T(8,128)(2,1)S(1)} %get-tuple-element.99._), channel_id=1, source_target_pairs={{128,64},{129,65},{130,66},{131,67},{132,68},{133,69},{134,70},{13... | collective-permute-start | bytes 294920 | tf_op jit(solution)/shard_map/ppermute | solution.py:230
  90.0 5.9 %collective-permute-start.18 = (bf16[96,512]{1,0:T(8,128)(2,1)S(1)}, bf16[96,512]{1,0:T(8,128)(2,1)S(1)}, u32[]{:S(2)}, u32[]{:S(2)}) collective-permute-start(bf16[96,512]{1,0:T(8,128)(2,1)S(1)} %get-tuple-element.101._), channel_id=1, source_target_pairs={{128,64},{129,65},{130,66},{131,67},{132,68},{133,69},{134,70},{13... | collective-permute-start | bytes 294920 | tf_op jit(solution)/shard_map/ppermute | solution.py:230
  91.3 6.5 %collective-permute-start.19 = (bf16[96,512]{1,0:T(8,128)(2,1)S(1)}, bf16[96,512]{1,0:T(8,128)(2,1)S(1)}, u32[]{:S(2)}, u32[]{:S(2)}) collective-permute-start(bf16[96,512]{1,0:T(8,128)(2,1)S(1)} %get-tuple-element.103._), channel_id=1, source_target_pairs={{128,64},{129,65},{130,66},{131,67},{132,68},{133,69},{134,70},{13... | collective-permute-start | bytes 294920 | tf_op jit(solution)/shard_map/ppermute | solution.py:230
  94.7 20.9 %collective-permute-start.20 = (bf16[96,512]{1,0:T(8,128)(2,1)S(1)}, bf16[96,512]{1,0:T(8,128)(2,1)S(1)}, u32[]{:S(2)}, u32[]{:S(2)}) collective-permute-start(bf16[96,512]{1,0:T(8,128)(2,1)S(1)} %get-tuple-element.109._), channel_id=1, source_target_pairs={{64,0},{65,1},{66,2},{67,3},{68,4},{69,5},{70,6},{71,7},{72,8},{73... | collective-permute-start | bytes 294920 | tf_op jit(solution)/shard_map/ppermute | solution.py:230
  96.6 24.2 %collective-permute-start.21 = (bf16[96,512]{1,0:T(8,128)(2,1)S(1)}, bf16[96,512]{1,0:T(8,128)(2,1)S(1)}, u32[]{:S(2)}, u32[]{:S(2)}) collective-permute-start(bf16[96,512]{1,0:T(8,128)(2,1)S(1)} %get-tuple-element.111._), channel_id=1, source_target_pairs={{64,0},{65,1},{66,2},{67,3},{68,4},{69,5},{70,6},{71,7},{72,8},{73... | collective-permute-start | bytes 294920 | tf_op jit(solution)/shard_map/ppermute | solution.py:230
  98.5 26.4 %collective-permute-start.22 = (bf16[96,512]{1,0:T(8,128)(2,1)S(1)}, bf16[96,512]{1,0:T(8,128)(2,1)S(1)}, u32[]{:S(2)}, u32[]{:S(2)}) collective-permute-start(bf16[96,512]{1,0:T(8,128)(2,1)S(1)} %get-tuple-element.113._), channel_id=1, source_target_pairs={{64,0},{65,1},{66,2},{67,3},{68,4},{69,5},{70,6},{71,7},{72,8},{73... | collective-permute-start | bytes 294920 | tf_op jit(solution)/shard_map/ppermute | solution.py:230
  142.9 9.7 %collective-permute-start.23 = (bf16[4,2,2,32,512]{4,3,2,1,0:T(8,128)(2,1)S(1)}, bf16[4,2,2,32,512]{4,3,2,1,0:T(8,128)(2,1)S(1)}, u32[]{:S(2)}, u32[]{:S(2)}) collective-permute-start(bf16[4,2,2,32,512]{4,3,2,1,0:T(8,128)(2,1)S(1)} %get-tuple-element.121), channel_id=1, source_target_pairs={{0,1},{1,0},{2,3},{3,2},{4,5},{5,4},{6,7},{7,6},{8,9},{9,8},{10,11... | collective-permute-start | bytes 1572872 | tf_op jit(solution)/shard_map/ppermute | solution.py:256
  165.0 14.4 %collective-permute-start.24 = (bf16[2,32,512]{2,1,0:T(8,128)(2,1)S(1)}, bf16[2,32,512]{2,1,0:T(8,128)(2,1)S(1)}, u32[]{:S(2)}, u32[]{:S(2)}) collective-permute-start(bf16[2,32,512]{2,1,0:T(8,128)(2,1)S(1)} %get-tuple-element.123._), channel_id=1, source_target_pairs={{0,8},{8,0},{1,9},{9,1},{2,10},{10,2},{3,11},{11,3},{4,12},{12,4},... | collective-permute-start | bytes 196616 | tf_op jit(solution)/shard_map/ppermute | solution.py:275
  (6 other events, 25.3 us)

commit v7 on v6

--- a/solution.py
+++ b/solution.py
@@ -128,14 +128,41 @@
 def forward_kernel(place, inputs, weights, slopes, inputs_t, h_t):
     w_in = weights[place[3], 0]
     part = inputs.shape[0] // 3
+    shard = inputs_t.shape[1] // (NH * NX)
     for block in range(3):
         at = pl.ds(block * part, part)
         x = inputs[at]
         zed = dot(x, w_in, 1, 1)
         sig = 1.0 / (1.0 + jnp.exp(-zed))
         slopes[at] = RHO * sig * (1.0 + zed * (1.0 - sig))
-        h_t[:, at] = (zed * sig).astype(BF16).T
-        inputs_t[:, at] = x.T
+        for target, rows in ((h_t, (zed * sig).astype(BF16).T), (inputs_t, x.T)):
+            for owner in range(NH * NX):
+                for core in range(NC):
+                    start = (owner * NC + core) * shard
+                    target[core, pl.ds(owner * shard, shard), at] = rows[start : start + shard]
+
+
+def write_rows(target, w, product):
+    rows = target.shape[3]
+    for zh in range(NH):
+        for x in range(NX):
+            start = (zh * NX + x) * rows
+            target[x, zh, w] = product[start : start + rows].astype(target.dtype)
+
+
+def sent_kernel(place, home_g, weights, slopes, inputs_t, h_t, dz, sent):
+    w_out = weights[place[3], 1]
+    part = home_g.shape[0] // NY
+    for block in range(NY):
+        at = pl.ds(block * part, part)
+        dz[at] = (dot(home_g[at], w_out, 1, 0) * slopes[at]).astype(BF16)
+    write_rows(sent, 0, dot(inputs_t[1 - place[1]], dz[...], 1, 0))
+    write_rows(sent, 1, RHO * dot(h_t[1 - place[1]], home_g[...], 1, 0))
+
+
+def own_kernel(place, home_g, dz, inputs_t, h_t, own):
+    write_rows(own, 0, dot(inputs_t[place[1]], dz[...], 1, 0))
+    write_rows(own, 1, RHO * dot(h_t[place[1]], home_g[...], 1, 0))
 
 
 def add_kernel(own, arrived, total):
@@ -229,7 +256,7 @@
             if stage < NZ - 1:
                 arriving[m] = lax.ppermute(sending, "z_lo", [(NZ - 1 - stage, NZ - 2 - stage)])
         if stage == HOME_AT:
-            wide = struct((width, micro * rows), BF16)
+            wide = struct((NC, width // NC, micro * rows), BF16)
             home = call(
                 forward_kernel,
                 (struct(flat_x.shape, F32), wide, wide),
@@ -243,15 +270,25 @@
 
     home_g = lax.all_to_all(kept[-1], "y", 0, 0).reshape(micro * rows, width)
     half = (NX, NH, 2, shard, width)
-    dz, sent, own = call(
-        home_kernel,
-        (struct(home_g.shape, BF16), struct(half, BF16), struct(half, F32)),
+    home_slopes, *home_rows = home
+    dz, sent = call(
+        sent_kernel,
+        (struct(home_g.shape, BF16), struct(half, BF16)),
         place,
         home_g,
         weights,
-        *home,
-        scratch=[pltpu.VMEM((width, width), F32)],
-        flops=6 * micro * rows * width * width,
+        home_slopes,
+        *home_rows,
+        flops=4 * micro * rows * width * width,
+    )
+    (own,) = call(
+        own_kernel,
+        (struct(half, F32),),
+        place,
+        home_g,
+        dz,
+        *home_rows,
+        flops=2 * micro * rows * width * width,
     )
     (total,) = call(add_kernel, (struct(half, BF16),), own, lax.ppermute(sent, "core", SWAP))
     parts = lax.all_to_all(total, "x", 0, 0)

time: 181 us -> 180 us (level)
    pallas_call x30 -> x31, Pallas kernels: 28.4 us -> 29 us  [call(): pl.pallas_call(kernel, out_shape=out_shape, in_specs=specs, out_specs=jax...]
  transfers between devices with their start and end apart: 26 -> 26, of which waited for: 7 -> 7; matrix products, arithmetic and copies ran while one was open for 1% -> 1% of each run, Pallas kernels for 11% -> 12%
where the time goes in v7:
time: 180 us; the launch traced here: 179 us
  starting transfers between devices  59 us (33%)
  blocking collectives  55.6 us (31%)
  waiting for transfers between devices  31.8 us (18%)
  Pallas kernels  29 us (16%)
  local copies, waits for them, and re-layouts  2.56 us (1%)
    all_to_all x2, blocking collectives, gather_step(): lax.all_to_all(pieces, PLANE, 0, 0, axis_index_groups=plane_groups(first))  30.4 us
    pallas_call x31, Pallas kernels, call(): pl.pallas_call(kernel, out_shape=out_shape, in_specs=specs, out_specs=jax...  29 us
    ppermute x21, waiting for transfers between devices, body(): lax.ppermute(sending, 'z_lo', [(NZ - 1 - stage, NZ - 2 - stage)])  22 us
    ppermute x21, starting transfers between devices, body(): lax.ppermute(sending, 'z_lo', [(NZ - 1 - stage, NZ - 2 - stage)])  15.9 us
    ppermute x1, starting transfers between devices, body(): far = lax.ppermute(own, 'z_hi', SWAP)  15.4 us
    all_to_all x1, blocking collectives, body(): home_g = lax.all_to_all(kept[-1], 'y', 0, 0).reshape(micro * rows, width)  13.6 us
    all_to_all x1, blocking collectives, body(): parts = lax.all_to_all(total, 'x', 0, 0)  11.6 us
    ppermute x1, starting transfers between devices, body(): lax.ppermute(sent, 'core', SWAP)  8.2 us
  transfers between devices with their start and end apart: 26, of which 7 were waited for; matrix products, arithmetic and copies ran while one was open for 1% of the time, Pallas kernels for 12%

profile of v7, /device:TPU:1, one launch (start us, length us, event | category | flops | bytes accessed | tf_op | source)
XLA Modules:
  0.0 179.3 jit_solution(17137391816681771577)
XLA Ops:
  0.7 5.2 %all-to-all-start = ((bf16[4,288,512]{2,1,0:T(8,128)(2,1)}), bf16[4,288,512]{2,1,0:T(8,128)(2,1)S(1)}, u32[]{:S(2)}, u32[]{:S(2)}) async-start(bf16[4,288,512]{2,1,0:T(8,128)(2,1)} %bitcast.23), calls=%async_computation | async-start | bytes 2359296 | tf_op jit(solution)/shard_map/all_to_all | solution.py:214
  5.8 15.4 %collective-permute-start = (bf16[2,32,512]{2,1,0:T(8,128)(2,1)S(1)}, bf16[2,32,512]{2,1,0:T(8,128)(2,1)S(1)}, u32[]{:S(2)}, u32[]{:S(2)}) collective-permute-start(bf16[2,32,512]{2,1,0:T(8,128)(2,1)S(1)} %pad_maximum_fusion.1), channel_id=1, source_target_pairs={{0,8},{8,0},{1,9},{9,1},{2,10},{10,2},{3,11},{11,3},{4,12},{12,4},... | collective-permute-start | bytes 196616 | tf_op jit(solution)/shard_map/ppermute | solution.py:216
  21.3 1.7 dynamic-slice_bitcast_fusion
  23.1 10.7 %all_to_all.25 = bf16[4,128,512]{2,1,0:T(8,128)(2,1)S(1)} all-to-all(bf16[4,128,512]{2,1,0:T(8,128)(2,1)S(1)} %broadcast_in_dim.15), channel_id=1, replica_groups={{0,16,32,48},{2,18,34,50},{4,20,36,52},{6,22,38,54},{1,3,5,7},{17,19,21..., dimensions={0} | all-to-all | bytes 1048576 | tf_op jit(solution)/shard_map/all_to_all | solution.py:38
  34.0 19.7 %all_to_all.26 = bf16[4,512,512]{2,1,0:T(8,128)(2,1)S(1)} all-to-all(bf16[4,512,512]{2,1,0:T(8,128)(2,1)S(1)} %broadcast_in_dim.17), channel_id=1, replica_groups={{0,2,4,6},{16,18,20,22},{32,34,36,38},{48,50,52,54},{1,17,33,49},{3,19,..., dimensions={0} | all-to-all | bytes 4194304 | tf_op jit(solution)/shard_map/all_to_all | solution.py:38
  53.7 7.9 %collective-permute-start.1 = (bf16[16,2,2,32,512]{4,3,2,1,0:T(8,128)(2,1)S(1)}, bf16[16,2,2,32,512]{4,3,2,1,0:T(8,128)(2,1)}, u32[]{:S(2)}, u32[]{:S(2)}) collective-permute-start(bf16[16,2,2,32,512]{4,3,2,1,0:T(8,128)(2,1)S(1)} %bitcast.21), channel_id=1, source_target_pairs={{0,1},{1,0},{2,3},{3,2},{4,5},{5,4},{6,7},{7,6},{8,9},{9,8},{10,11... | collective-permute-start | bytes 6291464 | tf_op jit(solution)/shard_map/ppermute | solution.py:223
  61.7 3.8 %collective-permute-done.1.other = bf16[16,2,2,32,512]{4,3,2,1,0:T(8,128)(2,1)} collective-permute-done((bf16[16,2,2,32,512]{4,3,2,1,0:T(8,128)(2,1)S(1)}, bf16[16,2,2,32,512]{4,3,2,1,0:T(8,128)(2,1)}, u32[]{:S(2)}, u32[]{:S(2)}) %collective-permute-start.1) | collective-permute-done | bytes 2097184 | tf_op jit(solution)/shard_map/ppermute | solution.py:223
  65.5 3.4 %shard_map.67 = (bf16[4,2,512,512]{3,2,1,0:T(8,128)(2,1)S(1)}, f32[4,288,512]{2,1,0:T(8,128)S(1)}) custom-call(s32[4]{0:T(128)S(1)} %pad_add_fusion.place.refs_0_, bf16[16,2,2,32,512]{4,3,2,1,0:T(8,128)(2,1)S(1)} %bitcast.22, bf16[16,2,2,32,512]{4,3,2,1,0:T(8,128)(2,1)} %collective-permute-done.1.other, bf16[4,288,512]{2,1,0:T(8,128)(2,1)S(1)} %all-to-all-done.inputs), custom_call_target="tpu_custom_call" | custom-call | flops 603979776 | tf_op jit(solution)/shard_map/pallas_call | solution.py:68
  92.0 2.0 %shard_map.86 = (f32[1152,512]{1,0:T(8,128)S(1)}, bf16[2,256,1152]{2,1,0:T(8,128)(2,1)S(1)}, bf16[2,256,1152]{2,1,0:T(8,128)(2,1)S(1)}) custom-call(bf16[96,512]{1,0:T(8,128)(2,1)S(1)} %get-tuple-element.102._, s32[4]{0:T(128)S(1)} %pad_add_fusion.place.refs_0_, bf16[1152,512]{1,0:T(8,128)(2,1)S(1)} %bitcast.24, ...), custom_call_target="tpu_custom_call" | custom-call | flops 603979776 | tf_op jit(solution)/shard_map/pallas_call | solution.py:68
  94.7 1.3 collective-permute-start.20
  99.8 15.8 %collective-permute-done.20.refs_1_ = bf16[96,512]{1,0:T(8,128)(2,1)S(1)} collective-permute-done((bf16[96,512]{1,0:T(8,128)(2,1)S(1)}, bf16[96,512]{1,0:T(8,128)(2,1)S(1)}, u32[]{:S(2)}, u32[]{:S(2)}) %collective-permute-start.20) | collective-permute-done | bytes 98336 | tf_op jit(solution)/shard_map/ppermute | solution.py:257
  115.5 1.6 shard_map.90._.refs_5_
  117.1 3.6 %collective-permute-done.21.refs_1_ = bf16[96,512]{1,0:T(8,128)(2,1)S(1)} collective-permute-done((bf16[96,512]{1,0:T(8,128)(2,1)S(1)}, bf16[96,512]{1,0:T(8,128)(2,1)S(1)}, u32[]{:S(2)}, u32[]{:S(2)}) %collective-permute-start.21) | collective-permute-done | bytes 98336 | tf_op jit(solution)/shard_map/ppermute | solution.py:257
  120.8 1.6 shard_map.91._.refs_6_
  122.4 2.5 %collective-permute-done.22.refs_1_ = bf16[96,512]{1,0:T(8,128)(2,1)S(1)} collective-permute-done((bf16[96,512]{1,0:T(8,128)(2,1)S(1)}, bf16[96,512]{1,0:T(8,128)(2,1)S(1)}, u32[]{:S(2)}, u32[]{:S(2)}) %collective-permute-start.22) | collective-permute-done | bytes 98336 | tf_op jit(solution)/shard_map/ppermute | solution.py:257
  124.9 1.6 shard_map.92
  126.5 13.6 %all_to_all.27 = bf16[4,288,512]{2,1,0:T(8,128)(2,1)S(1)} all-to-all(bf16[4,288,512]{2,1,0:T(8,128)(2,1)S(1)} %shard_map.92), channel_id=1, replica_groups=mesh['z_lo'=8,'y'=4,'z_hi'=2,'x'=4,'core'=2] {'y'}, dimensions={0} | all-to-all | bytes 2359296 | tf_op jit(solution)/shard_map/all_to_all | solution.py:271
  140.1 2.0 %shard_map.93 = (bf16[1152,512]{1,0:T(8,128)(2,1)S(1)}, bf16[4,2,2,32,512]{4,3,2,1,0:T(8,128)(2,1)S(1)}) custom-call(s32[4]{0:T(128)S(1)} %pad_add_fusion.place.refs_0_, bf16[1152,512]{1,0:T(8,128)(2,1)S(1)} %bitcast.18, bf16[4,2,512,512]{3,2,1,0:T(8,128)(2,1)S(1)} %get-tuple-element.66.weights.refs_2_.refs_3_, f32[1152,512]{1,0:T(8,128)S(1)} %get-tuple-element.116.slopes, ...), custom_call_target="tpu_custom_call" | custom-call | flops 1207959552 | tf_op jit(solution)/shard_map/pallas_call | solution.py:68
  142.1 8.2 %collective-permute-start.23 = (bf16[4,2,2,32,512]{4,3,2,1,0:T(8,128)(2,1)S(1)}, bf16[4,2,2,32,512]{4,3,2,1,0:T(8,128)(2,1)S(1)}, u32[]{:S(2)}, u32[]{:S(2)}) collective-permute-start(bf16[4,2,2,32,512]{4,3,2,1,0:T(8,128)(2,1)S(1)} %get-tuple-element.120), channel_id=1, source_target_pairs={{0,1},{1,0},{2,3},{3,2},{4,5},{5,4},{6,7},{7,6},{8,9},{9,8},{10,11... | collective-permute-start | bytes 1572872 | tf_op jit(solution)/shard_map/ppermute | solution.py:293
  150.3 1.4 shard_map.94.own
  152.0 11.6 %all_to_all.28.parts = bf16[4,2,2,32,512]{4,3,2,1,0:T(8,128)(2,1)S(1)} all-to-all(bf16[4,2,2,32,512]{4,3,2,1,0:T(8,128)(2,1)S(1)} %shard_map.95), channel_id=1, replica_groups=mesh['z_lo'=8,'y'=4,'z_hi'=2,'x'=4,'core'=2] {'x'}, dimensions={0} | all-to-all | bytes 1048576 | tf_op jit(solution)/shard_map/all_to_all | solution.py:294
  164.2 6.4 %collective-permute-start.24 = (bf16[2,32,512]{2,1,0:T(8,128)(2,1)S(1)}, bf16[2,32,512]{2,1,0:T(8,128)(2,1)S(1)}, u32[]{:S(2)}, u32[]{:S(2)}) collective-permute-start(bf16[2,32,512]{2,1,0:T(8,128)(2,1)S(1)} %get-tuple-element.122._), channel_id=1, source_target_pairs={{0,8},{8,0},{1,9},{9,1},{2,10},{10,2},{3,11},{11,3},{4,12},{12,4},... | collective-permute-start | bytes 196616 | tf_op jit(solution)/shard_map/ppermute | solution.py:312
  170.6 2.3 %shard_map.97 = bf16[1152,512]{1,0:T(8,128)(2,1)} custom-call(bf16[2,32,512]{2,1,0:T(8,128)(2,1)S(1)} %get-tuple-element.122._, s32[4]{0:T(128)S(1)} %pad_add_fusion.place.refs_0_, bf16[1152,512]{1,0:T(8,128)(2,1)S(1)} %bitcast.20, bf16[1152,512]{1,0:T(8,128)(2,1)S(1)} %get-tuple-element.119.dz.refs_2_, ...), custom_call_target="tpu_custom_call" | custom-call | flops 603979776 | tf_op jit(solution)/shard_map/pallas_call | solution.py:68
  173.0 5.7 %collective-permute-done.24 = bf16[2,32,512]{2,1,0:T(8,128)(2,1)S(1)} collective-permute-done((bf16[2,32,512]{2,1,0:T(8,128)(2,1)S(1)}, bf16[2,32,512]{2,1,0:T(8,128)(2,1)S(1)}, u32[]{:S(2)}, u32[]{:S(2)}) %collective-permute-start.24) | collective-permute-done | bytes 65568 | tf_op jit(solution)/shard_map/ppermute | solution.py:312
  (80 shorter events, 29.0 us)
Async XLA Ops:
  0.7 22.4 %all-to-all-start = ((bf16[4,288,512]{2,1,0:T(8,128)(2,1)}), bf16[4,288,512]{2,1,0:T(8,128)(2,1)S(1)}, u32[]{:S(2)}, u32[]{:S(2)}) async-start(bf16[4,288,512]{2,1,0:T(8,128)(2,1)} %bitcast.23), calls=%async_computation | async-start | bytes 2359296 | tf_op jit(solution)/shard_map/all_to_all | solution.py:214
  5.8 17.2 %collective-permute-start = (bf16[2,32,512]{2,1,0:T(8,128)(2,1)S(1)}, bf16[2,32,512]{2,1,0:T(8,128)(2,1)S(1)}, u32[]{:S(2)}, u32[]{:S(2)}) collective-permute-start(bf16[2,32,512]{2,1,0:T(8,128)(2,1)S(1)} %pad_maximum_fusion.1), channel_id=1, source_target_pairs={{0,8},{8,0},{1,9},{9,1},{2,10},{10,2},{3,11},{11,3},{4,12},{12,4},... | collective-permute-start | bytes 196616 | tf_op jit(solution)/shard_map/ppermute | solution.py:216
  53.7 11.8 %collective-permute-start.1 = (bf16[16,2,2,32,512]{4,3,2,1,0:T(8,128)(2,1)S(1)}, bf16[16,2,2,32,512]{4,3,2,1,0:T(8,128)(2,1)}, u32[]{:S(2)}, u32[]{:S(2)}) collective-permute-start(bf16[16,2,2,32,512]{4,3,2,1,0:T(8,128)(2,1)S(1)} %bitcast.21), channel_id=1, source_target_pairs={{0,1},{1,0},{2,3},{3,2},{4,5},{5,4},{6,7},{7,6},{8,9},{9,8},{10,11... | collective-permute-start | bytes 6291464 | tf_op jit(solution)/shard_map/ppermute | solution.py:223
  72.0 3.2 %collective-permute-start.4 = (bf16[96,512]{1,0:T(8,128)(2,1)S(1)}, bf16[96,512]{1,0:T(8,128)(2,1)S(1)}, u32[]{:S(2)}, u32[]{:S(2)}) collective-permute-start(bf16[96,512]{1,0:T(8,128)(2,1)S(1)} %get-tuple-element.72._), channel_id=1, source_target_pairs={{448,384},{449,385},{450,386},{451,387},{452,388},{453,389},{454,3... | collective-permute-start | bytes 294920 | tf_op jit(solution)/shard_map/ppermute | solution.py:257
  73.3 3.2 %collective-permute-start.5 = (bf16[96,512]{1,0:T(8,128)(2,1)S(1)}, bf16[96,512]{1,0:T(8,128)(2,1)S(1)}, u32[]{:S(2)}, u32[]{:S(2)}) collective-permute-start(bf16[96,512]{1,0:T(8,128)(2,1)S(1)} %get-tuple-element.74._), channel_id=1, source_target_pairs={{384,320},{385,321},{386,322},{387,323},{388,324},{389,325},{390,3... | collective-permute-start | bytes 294920 | tf_op jit(solution)/shard_map/ppermute | solution.py:257
  74.6 3.2 %collective-permute-start.6 = (bf16[96,512]{1,0:T(8,128)(2,1)S(1)}, bf16[96,512]{1,0:T(8,128)(2,1)S(1)}, u32[]{:S(2)}, u32[]{:S(2)}) collective-permute-start(bf16[96,512]{1,0:T(8,128)(2,1)S(1)} %get-tuple-element.76._), channel_id=1, source_target_pairs={{384,320},{385,321},{386,322},{387,323},{388,324},{389,325},{390,3... | collective-permute-start | bytes 294920 | tf_op jit(solution)/shard_map/ppermute | solution.py:257
  75.9 3.2 %collective-permute-start.7 = (bf16[96,512]{1,0:T(8,128)(2,1)S(1)}, bf16[96,512]{1,0:T(8,128)(2,1)S(1)}, u32[]{:S(2)}, u32[]{:S(2)}) collective-permute-start(bf16[96,512]{1,0:T(8,128)(2,1)S(1)} %get-tuple-element.78._), channel_id=1, source_target_pairs={{384,320},{385,321},{386,322},{387,323},{388,324},{389,325},{390,3... | collective-permute-start | bytes 294920 | tf_op jit(solution)/shard_map/ppermute | solution.py:257
  77.1 3.2 %collective-permute-start.8 = (bf16[96,512]{1,0:T(8,128)(2,1)S(1)}, bf16[96,512]{1,0:T(8,128)(2,1)S(1)}, u32[]{:S(2)}, u32[]{:S(2)}) collective-permute-start(bf16[96,512]{1,0:T(8,128)(2,1)S(1)} %get-tuple-element.80._), channel_id=1, source_target_pairs={{320,256},{321,257},{322,258},{323,259},{324,260},{325,261},{326,2... | collective-permute-start | bytes 294920 | tf_op jit(solution)/shard_map/ppermute | solution.py:257
  78.4 3.2 %collective-permute-start.9 = (bf16[96,512]{1,0:T(8,128)(2,1)S(1)}, bf16[96,512]{1,0:T(8,128)(2,1)S(1)}, u32[]{:S(2)}, u32[]{:S(2)}) collective-permute-start(bf16[96,512]{1,0:T(8,128)(2,1)S(1)} %get-tuple-element.82._), channel_id=1, source_target_pairs={{320,256},{321,257},{322,258},{323,259},{324,260},{325,261},{326,2... | collective-permute-start | bytes 294920 | tf_op jit(solution)/shard_map/ppermute | solution.py:257
  79.7 3.2 %collective-permute-start.10 = (bf16[96,512]{1,0:T(8,128)(2,1)S(1)}, bf16[96,512]{1,0:T(8,128)(2,1)S(1)}, u32[]{:S(2)}, u32[]{:S(2)}) collective-permute-start(bf16[96,512]{1,0:T(8,128)(2,1)S(1)} %get-tuple-element.84._), channel_id=1, source_target_pairs={{320,256},{321,257},{322,258},{323,259},{324,260},{325,261},{326,2... | collective-permute-start | bytes 294920 | tf_op jit(solution)/shard_map/ppermute | solution.py:257
  81.0 3.2 %collective-permute-start.11 = (bf16[96,512]{1,0:T(8,128)(2,1)S(1)}, bf16[96,512]{1,0:T(8,128)(2,1)S(1)}, u32[]{:S(2)}, u32[]{:S(2)}) collective-permute-start(bf16[96,512]{1,0:T(8,128)(2,1)S(1)} %get-tuple-element.86._), channel_id=1, source_target_pairs={{256,192},{257,193},{258,194},{259,195},{260,196},{261,197},{262,1... | collective-permute-start | bytes 294920 | tf_op jit(solution)/shard_map/ppermute | solution.py:257
  82.2 3.2 %collective-permute-start.12 = (bf16[96,512]{1,0:T(8,128)(2,1)S(1)}, bf16[96,512]{1,0:T(8,128)(2,1)S(1)}, u32[]{:S(2)}, u32[]{:S(2)}) collective-permute-start(bf16[96,512]{1,0:T(8,128)(2,1)S(1)} %get-tuple-element.88._), channel_id=1, source_target_pairs={{256,192},{257,193},{258,194},{259,195},{260,196},{261,197},{262,1... | collective-permute-start | bytes 294920 | tf_op jit(solution)/shard_map/ppermute | solution.py:257
  83.5 3.2 %collective-permute-start.13 = (bf16[96,512]{1,0:T(8,128)(2,1)S(1)}, bf16[96,512]{1,0:T(8,128)(2,1)S(1)}, u32[]{:S(2)}, u32[]{:S(2)}) collective-permute-start(bf16[96,512]{1,0:T(8,128)(2,1)S(1)} %get-tuple-element.90._), channel_id=1, source_target_pairs={{256,192},{257,193},{258,194},{259,195},{260,196},{261,197},{262,1... | collective-permute-start | bytes 294920 | tf_op jit(solution)/shard_map/ppermute | solution.py:257
  84.8 3.4 %collective-permute-start.14 = (bf16[96,512]{1,0:T(8,128)(2,1)S(1)}, bf16[96,512]{1,0:T(8,128)(2,1)S(1)}, u32[]{:S(2)}, u32[]{:S(2)}) collective-permute-start(bf16[96,512]{1,0:T(8,128)(2,1)S(1)} %get-tuple-element.92._), channel_id=1, source_target_pairs={{192,128},{193,129},{194,130},{195,131},{196,132},{197,133},{198,1... | collective-permute-start | bytes 294920 | tf_op jit(solution)/shard_map/ppermute | solution.py:257
  86.0 3.4 %collective-permute-start.15 = (bf16[96,512]{1,0:T(8,128)(2,1)S(1)}, bf16[96,512]{1,0:T(8,128)(2,1)S(1)}, u32[]{:S(2)}, u32[]{:S(2)}) collective-permute-start(bf16[96,512]{1,0:T(8,128)(2,1)S(1)} %get-tuple-element.94._), channel_id=1, source_target_pairs={{192,128},{193,129},{194,130},{195,131},{196,132},{197,133},{198,1... | collective-permute-start | bytes 294920 | tf_op jit(solution)/shard_map/ppermute | solution.py:257
  87.5 3.2 %collective-permute-start.16 = (bf16[96,512]{1,0:T(8,128)(2,1)S(1)}, bf16[96,512]{1,0:T(8,128)(2,1)S(1)}, u32[]{:S(2)}, u32[]{:S(2)}) collective-permute-start(bf16[96,512]{1,0:T(8,128)(2,1)S(1)} %get-tuple-element.96._), channel_id=1, source_target_pairs={{192,128},{193,129},{194,130},{195,131},{196,132},{197,133},{198,1... | collective-permute-start | bytes 294920 | tf_op jit(solution)/shard_map/ppermute | solution.py:257
  88.8 5.3 %collective-permute-start.17 = (bf16[96,512]{1,0:T(8,128)(2,1)S(1)}, bf16[96,512]{1,0:T(8,128)(2,1)S(1)}, u32[]{:S(2)}, u32[]{:S(2)}) collective-permute-start(bf16[96,512]{1,0:T(8,128)(2,1)S(1)} %get-tuple-element.98._), channel_id=1, source_target_pairs={{128,64},{129,65},{130,66},{131,67},{132,68},{133,69},{134,70},{13... | collective-permute-start | bytes 294920 | tf_op jit(solution)/shard_map/ppermute | solution.py:257
  90.0 5.9 %collective-permute-start.18 = (bf16[96,512]{1,0:T(8,128)(2,1)S(1)}, bf16[96,512]{1,0:T(8,128)(2,1)S(1)}, u32[]{:S(2)}, u32[]{:S(2)}) collective-permute-start(bf16[96,512]{1,0:T(8,128)(2,1)S(1)} %get-tuple-element.100._), channel_id=1, source_target_pairs={{128,64},{129,65},{130,66},{131,67},{132,68},{133,69},{134,70},{13... | collective-permute-start | bytes 294920 | tf_op jit(solution)/shard_map/ppermute | solution.py:257
  91.3 6.5 %collective-permute-start.19 = (bf16[96,512]{1,0:T(8,128)(2,1)S(1)}, bf16[96,512]{1,0:T(8,128)(2,1)S(1)}, u32[]{:S(2)}, u32[]{:S(2)}) collective-permute-start(bf16[96,512]{1,0:T(8,128)(2,1)S(1)} %get-tuple-element.102._), channel_id=1, source_target_pairs={{128,64},{129,65},{130,66},{131,67},{132,68},{133,69},{134,70},{13... | collective-permute-start | bytes 294920 | tf_op jit(solution)/shard_map/ppermute | solution.py:257
  94.7 20.9 %collective-permute-start.20 = (bf16[96,512]{1,0:T(8,128)(2,1)S(1)}, bf16[96,512]{1,0:T(8,128)(2,1)S(1)}, u32[]{:S(2)}, u32[]{:S(2)}) collective-permute-start(bf16[96,512]{1,0:T(8,128)(2,1)S(1)} %get-tuple-element.108._), channel_id=1, source_target_pairs={{64,0},{65,1},{66,2},{67,3},{68,4},{69,5},{70,6},{71,7},{72,8},{73... | collective-permute-start | bytes 294920 | tf_op jit(solution)/shard_map/ppermute | solution.py:257
  96.6 24.2 %collective-permute-start.21 = (bf16[96,512]{1,0:T(8,128)(2,1)S(1)}, bf16[96,512]{1,0:T(8,128)(2,1)S(1)}, u32[]{:S(2)}, u32[]{:S(2)}) collective-permute-start(bf16[96,512]{1,0:T(8,128)(2,1)S(1)} %get-tuple-element.110._), channel_id=1, source_target_pairs={{64,0},{65,1},{66,2},{67,3},{68,4},{69,5},{70,6},{71,7},{72,8},{73... | collective-permute-start | bytes 294920 | tf_op jit(solution)/shard_map/ppermute | solution.py:257
  98.5 26.4 %collective-permute-start.22 = (bf16[96,512]{1,0:T(8,128)(2,1)S(1)}, bf16[96,512]{1,0:T(8,128)(2,1)S(1)}, u32[]{:S(2)}, u32[]{:S(2)}) collective-permute-start(bf16[96,512]{1,0:T(8,128)(2,1)S(1)} %get-tuple-element.112._), channel_id=1, source_target_pairs={{64,0},{65,1},{66,2},{67,3},{68,4},{69,5},{70,6},{71,7},{72,8},{73... | collective-permute-start | bytes 294920 | tf_op jit(solution)/shard_map/ppermute | solution.py:257
  142.1 9.7 %collective-permute-start.23 = (bf16[4,2,2,32,512]{4,3,2,1,0:T(8,128)(2,1)S(1)}, bf16[4,2,2,32,512]{4,3,2,1,0:T(8,128)(2,1)S(1)}, u32[]{:S(2)}, u32[]{:S(2)}) collective-permute-start(bf16[4,2,2,32,512]{4,3,2,1,0:T(8,128)(2,1)S(1)} %get-tuple-element.120), channel_id=1, source_target_pairs={{0,1},{1,0},{2,3},{3,2},{4,5},{5,4},{6,7},{7,6},{8,9},{9,8},{10,11... | collective-permute-start | bytes 1572872 | tf_op jit(solution)/shard_map/ppermute | solution.py:293
  164.2 14.4 %collective-permute-start.24 = (bf16[2,32,512]{2,1,0:T(8,128)(2,1)S(1)}, bf16[2,32,512]{2,1,0:T(8,128)(2,1)S(1)}, u32[]{:S(2)}, u32[]{:S(2)}) collective-permute-start(bf16[2,32,512]{2,1,0:T(8,128)(2,1)S(1)} %get-tuple-element.122._), channel_id=1, source_target_pairs={{0,8},{8,0},{1,9},{9,1},{2,10},{10,2},{3,11},{11,3},{4,12},{12,4},... | collective-permute-start | bytes 196616 | tf_op jit(solution)/shard_map/ppermute | solution.py:312
  (6 other events, 25.3 us)

commit v8 on v7

--- a/solution.py
+++ b/solution.py
@@ -96,8 +96,9 @@
             weights[s, w] = natural[s, w].T
 
 
-def stage_kernel(stage, chunk, place, arriving, weights, slopes, kept_in, *rest):
+def stage_kernel(stage, chunk, arriving, weights, slopes, kept_in, *rest):
     last = stage == NZ - 1
+    here = lax.axis_index("z_lo")
     joined = last and chunk == CHUNKS - 1
     earlier, outs = rest[: chunk if joined else 0], rest[chunk if joined else 0 :]
     part = arriving.shape[0]
@@ -107,7 +108,7 @@
         for s in range(NY):
             outs[0][s, pl.ds(m * part, part)] = rows[s]
 
-    @pl.when(place[0] == NZ - 1 - stage)
+    @pl.when(here == NZ - 1 - stage)
     def _():
         g = arriving[...]
         for s in reversed(range(NY)):
@@ -119,7 +120,7 @@
         if not last:
             outs[1][...] = g
 
-    @pl.when(place[0] != NZ - 1 - stage)
+    @pl.when(here != NZ - 1 - stage)
     def _():
         for s in range(NY):
             outs[0][s, into] = kept_in[s]
@@ -243,7 +244,6 @@
             result = call(
                 functools.partial(stage_kernel, stage, m),
                 tuple(outs),
-                place,
                 arriving[m],
                 weights,
                 slopes,

time: 180 us -> 174 us (0.967)
  Pallas kernels: 29 us -> 16.1 us
  waiting for transfers between devices: 31.8 us -> 36.9 us
    pallas_call x31, Pallas kernels: 29 us -> 16.1 us  [call(): pl.pallas_call(kernel, out_shape=out_shape, in_specs=specs, out_specs=jax...]
    ppermute x21, waiting for transfers between devices: 22 us -> 28.8 us  [body(): lax.ppermute(sending, 'z_lo', [(NZ - 1 - stage, NZ - 2 - stage)])]
  transfers between devices with their start and end apart: 26 -> 26, of which waited for: 7 -> 7; matrix products, arithmetic and copies ran while one was open for 1% -> 1% of each run, Pallas kernels for 12% -> 5%
where the time goes in v8:
time: 174 us; the launch traced here: 173 us
  starting transfers between devices  59.9 us (34%)
  blocking collectives  55.8 us (32%)
  waiting for transfers between devices  36.9 us (21%)
  Pallas kernels  16.1 us (9%)
  local copies, waits for them, and re-layouts  2.96 us (2%)
    all_to_all x2, blocking collectives, gather_step(): lax.all_to_all(pieces, PLANE, 0, 0, axis_index_groups=plane_groups(first))  30.4 us
    ppermute x21, waiting for transfers between devices, body(): lax.ppermute(sending, 'z_lo', [(NZ - 1 - stage, NZ - 2 - stage)])  28.8 us
    pallas_call x31, Pallas kernels, call(): pl.pallas_call(kernel, out_shape=out_shape, in_specs=specs, out_specs=jax...  16.1 us
    ppermute x21, starting transfers between devices, body(): lax.ppermute(sending, 'z_lo', [(NZ - 1 - stage, NZ - 2 - stage)])  16 us
    ppermute x1, starting transfers between devices, body(): far = lax.ppermute(own, 'z_hi', SWAP)  15.4 us
    all_to_all x1, blocking collectives, body(): home_g = lax.all_to_all(kept[-1], 'y', 0, 0).reshape(micro * rows, width)  13.7 us
    all_to_all x1, blocking collectives, body(): parts = lax.all_to_all(total, 'x', 0, 0)  11.6 us
    ppermute x1, starting transfers between devices, body(): lax.ppermute(sent, 'core', SWAP)  8.08 us
  transfers between devices with their start and end apart: 26, of which 7 were waited for; matrix products, arithmetic and copies ran while one was open for 1% of the time, Pallas kernels for 5%

profile of v8, /device:TPU:1, one launch (start us, length us, event | category | flops | bytes accessed | tf_op | source)
XLA Modules:
  0.0 173.0 jit_solution(16091135502623439487)
XLA Ops:
  0.7 5.2 %all-to-all-start = ((bf16[4,288,512]{2,1,0:T(8,128)(2,1)}), bf16[4,288,512]{2,1,0:T(8,128)(2,1)S(1)}, u32[]{:S(2)}, u32[]{:S(2)}) async-start(bf16[4,288,512]{2,1,0:T(8,128)(2,1)} %bitcast.23), calls=%async_computation | async-start | bytes 2359296 | tf_op jit(solution)/shard_map/all_to_all | solution.py:215
  5.8 15.4 %collective-permute-start = (bf16[2,32,512]{2,1,0:T(8,128)(2,1)S(1)}, bf16[2,32,512]{2,1,0:T(8,128)(2,1)S(1)}, u32[]{:S(2)}, u32[]{:S(2)}) collective-permute-start(bf16[2,32,512]{2,1,0:T(8,128)(2,1)S(1)} %pad_maximum_fusion.1), channel_id=1, source_target_pairs={{0,8},{8,0},{1,9},{9,1},{2,10},{10,2},{3,11},{11,3},{4,12},{12,4},... | collective-permute-start | bytes 196616 | tf_op jit(solution)/shard_map/ppermute | solution.py:217
  21.3 1.7 dynamic-slice_bitcast_fusion
  23.1 10.7 %all_to_all.25 = bf16[4,128,512]{2,1,0:T(8,128)(2,1)S(1)} all-to-all(bf16[4,128,512]{2,1,0:T(8,128)(2,1)S(1)} %broadcast_in_dim.15), channel_id=1, replica_groups={{0,16,32,48},{2,18,34,50},{4,20,36,52},{6,22,38,54},{1,3,5,7},{17,19,21..., dimensions={0} | all-to-all | bytes 1048576 | tf_op jit(solution)/shard_map/all_to_all | solution.py:38
  34.0 19.7 %all_to_all.26 = bf16[4,512,512]{2,1,0:T(8,128)(2,1)S(1)} all-to-all(bf16[4,512,512]{2,1,0:T(8,128)(2,1)S(1)} %broadcast_in_dim.17), channel_id=1, replica_groups={{0,2,4,6},{16,18,20,22},{32,34,36,38},{48,50,52,54},{1,17,33,49},{3,19,..., dimensions={0} | all-to-all | bytes 4194304 | tf_op jit(solution)/shard_map/all_to_all | solution.py:38
  53.7 7.9 %collective-permute-start.1 = (bf16[16,2,2,32,512]{4,3,2,1,0:T(8,128)(2,1)S(1)}, bf16[16,2,2,32,512]{4,3,2,1,0:T(8,128)(2,1)}, u32[]{:S(2)}, u32[]{:S(2)}) collective-permute-start(bf16[16,2,2,32,512]{4,3,2,1,0:T(8,128)(2,1)S(1)} %bitcast.21), channel_id=1, source_target_pairs={{0,1},{1,0},{2,3},{3,2},{4,5},{5,4},{6,7},{7,6},{8,9},{9,8},{10,11... | collective-permute-start | bytes 6291464 | tf_op jit(solution)/shard_map/ppermute | solution.py:224
  61.7 3.8 %collective-permute-done.1.other = bf16[16,2,2,32,512]{4,3,2,1,0:T(8,128)(2,1)} collective-permute-done((bf16[16,2,2,32,512]{4,3,2,1,0:T(8,128)(2,1)S(1)}, bf16[16,2,2,32,512]{4,3,2,1,0:T(8,128)(2,1)}, u32[]{:S(2)}, u32[]{:S(2)}) %collective-permute-start.1) | collective-permute-done | bytes 2097184 | tf_op jit(solution)/shard_map/ppermute | solution.py:224
  65.5 3.4 %shard_map.67 = (bf16[4,2,512,512]{3,2,1,0:T(8,128)(2,1)S(1)}, f32[4,288,512]{2,1,0:T(8,128)S(1)}) custom-call(s32[4]{0:T(128)S(1)} %pad_add_fusion.place.refs_0_, bf16[16,2,2,32,512]{4,3,2,1,0:T(8,128)(2,1)S(1)} %bitcast.22, bf16[16,2,2,32,512]{4,3,2,1,0:T(8,128)(2,1)} %collective-permute-done.1.other, bf16[4,288,512]{2,1,0:T(8,128)(2,1)S(1)} %all-to-all-done.inputs), custom_call_target="tpu_custom_call" | custom-call | flops 603979776 | tf_op jit(solution)/shard_map/pallas_call | solution.py:68
  82.9 2.0 %shard_map.86 = (f32[1152,512]{1,0:T(8,128)S(1)}, bf16[2,256,1152]{2,1,0:T(8,128)(2,1)S(1)}, bf16[2,256,1152]{2,1,0:T(8,128)(2,1)S(1)}) custom-call(bf16[96,512]{1,0:T(8,128)(2,1)S(1)} %get-tuple-element.102._, s32[4]{0:T(128)S(1)} %pad_add_fusion.place.refs_0_, bf16[1152,512]{1,0:T(8,128)(2,1)S(1)} %bitcast.24, ...), custom_call_target="tpu_custom_call" | custom-call | flops 603979776 | tf_op jit(solution)/shard_map/pallas_call | solution.py:68
  85.0 1.3 collective-permute-start.20
  86.4 1.3 collective-permute-start.21
  87.7 1.3 collective-permute-start.22
  89.0 22.7 %collective-permute-done.20.refs_0_ = bf16[96,512]{1,0:T(8,128)(2,1)S(1)} collective-permute-done((bf16[96,512]{1,0:T(8,128)(2,1)S(1)}, bf16[96,512]{1,0:T(8,128)(2,1)S(1)}, u32[]{:S(2)}, u32[]{:S(2)}) %collective-permute-start.20) | collective-permute-done | bytes 98336 | tf_op jit(solution)/shard_map/ppermute | solution.py:257
  112.8 3.6 %collective-permute-done.21.refs_0_ = bf16[96,512]{1,0:T(8,128)(2,1)S(1)} collective-permute-done((bf16[96,512]{1,0:T(8,128)(2,1)S(1)}, bf16[96,512]{1,0:T(8,128)(2,1)S(1)}, u32[]{:S(2)}, u32[]{:S(2)}) %collective-permute-start.21) | collective-permute-done | bytes 98336 | tf_op jit(solution)/shard_map/ppermute | solution.py:257
  117.4 2.4 %collective-permute-done.22.refs_0_ = bf16[96,512]{1,0:T(8,128)(2,1)S(1)} collective-permute-done((bf16[96,512]{1,0:T(8,128)(2,1)S(1)}, bf16[96,512]{1,0:T(8,128)(2,1)S(1)}, u32[]{:S(2)}, u32[]{:S(2)}) %collective-permute-start.22) | collective-permute-done | bytes 98336 | tf_op jit(solution)/shard_map/ppermute | solution.py:257
  119.9 1.1 shard_map.92
  121.0 13.7 %all_to_all.27 = bf16[4,288,512]{2,1,0:T(8,128)(2,1)S(1)} all-to-all(bf16[4,288,512]{2,1,0:T(8,128)(2,1)S(1)} %shard_map.92), channel_id=1, replica_groups=mesh['z_lo'=8,'y'=4,'z_hi'=2,'x'=4,'core'=2] {'y'}, dimensions={0} | all-to-all | bytes 2359296 | tf_op jit(solution)/shard_map/all_to_all | solution.py:271
  134.7 2.0 %shard_map.93 = (bf16[1152,512]{1,0:T(8,128)(2,1)S(1)}, bf16[4,2,2,32,512]{4,3,2,1,0:T(8,128)(2,1)S(1)}) custom-call(s32[4]{0:T(128)S(1)} %pad_add_fusion.place.refs_0_, bf16[1152,512]{1,0:T(8,128)(2,1)S(1)} %bitcast.18, bf16[4,2,512,512]{3,2,1,0:T(8,128)(2,1)S(1)} %get-tuple-element.66.weights.refs_1_.refs_2_.refs_3_, ...), custom_call_target="tpu_custom_call" | custom-call | flops 1207959552 | tf_op jit(solution)/shard_map/pallas_call | solution.py:68
  136.7 8.1 %collective-permute-start.23 = (bf16[4,2,2,32,512]{4,3,2,1,0:T(8,128)(2,1)S(1)}, bf16[4,2,2,32,512]{4,3,2,1,0:T(8,128)(2,1)S(1)}, u32[]{:S(2)}, u32[]{:S(2)}) collective-permute-start(bf16[4,2,2,32,512]{4,3,2,1,0:T(8,128)(2,1)S(1)} %get-tuple-element.120), channel_id=1, source_target_pairs={{0,1},{1,0},{2,3},{3,2},{4,5},{5,4},{6,7},{7,6},{8,9},{9,8},{10,11... | collective-permute-start | bytes 1572872 | tf_op jit(solution)/shard_map/ppermute | solution.py:293
  144.8 1.4 shard_map.94.own
  146.4 11.6 %all_to_all.28.parts = bf16[4,2,2,32,512]{4,3,2,1,0:T(8,128)(2,1)S(1)} all-to-all(bf16[4,2,2,32,512]{4,3,2,1,0:T(8,128)(2,1)S(1)} %shard_map.95), channel_id=1, replica_groups=mesh['z_lo'=8,'y'=4,'z_hi'=2,'x'=4,'core'=2] {'x'}, dimensions={0} | all-to-all | bytes 1048576 | tf_op jit(solution)/shard_map/all_to_all | solution.py:294
  158.6 7.3 %collective-permute-start.24 = (bf16[2,32,512]{2,1,0:T(8,128)(2,1)S(1)}, bf16[2,32,512]{2,1,0:T(8,128)(2,1)S(1)}, u32[]{:S(2)}, u32[]{:S(2)}) collective-permute-start(bf16[2,32,512]{2,1,0:T(8,128)(2,1)S(1)} %get-tuple-element.122._), channel_id=1, source_target_pairs={{0,8},{8,0},{1,9},{9,1},{2,10},{10,2},{3,11},{11,3},{4,12},{12,4},... | collective-permute-start | bytes 196616 | tf_op jit(solution)/shard_map/ppermute | solution.py:312
  165.9 2.3 %shard_map.97 = bf16[1152,512]{1,0:T(8,128)(2,1)} custom-call(bf16[2,32,512]{2,1,0:T(8,128)(2,1)S(1)} %get-tuple-element.122._, s32[4]{0:T(128)S(1)} %pad_add_fusion.place.refs_0_, bf16[1152,512]{1,0:T(8,128)(2,1)S(1)} %bitcast.20, bf16[1152,512]{1,0:T(8,128)(2,1)S(1)} %get-tuple-element.119.dz.refs_2_, ...), custom_call_target="tpu_custom_call" | custom-call | flops 603979776 | tf_op jit(solution)/shard_map/pallas_call | solution.py:68
  168.3 4.1 %collective-permute-done.24 = bf16[2,32,512]{2,1,0:T(8,128)(2,1)S(1)} collective-permute-done((bf16[2,32,512]{2,1,0:T(8,128)(2,1)S(1)}, bf16[2,32,512]{2,1,0:T(8,128)(2,1)S(1)}, u32[]{:S(2)}, u32[]{:S(2)}) %collective-permute-start.24) | collective-permute-done | bytes 65568 | tf_op jit(solution)/shard_map/ppermute | solution.py:312
  (80 shorter events, 17.8 us)
Async XLA Ops:
  0.7 22.4 %all-to-all-start = ((bf16[4,288,512]{2,1,0:T(8,128)(2,1)}), bf16[4,288,512]{2,1,0:T(8,128)(2,1)S(1)}, u32[]{:S(2)}, u32[]{:S(2)}) async-start(bf16[4,288,512]{2,1,0:T(8,128)(2,1)} %bitcast.23), calls=%async_computation | async-start | bytes 2359296 | tf_op jit(solution)/shard_map/all_to_all | solution.py:215
  5.8 17.2 %collective-permute-start = (bf16[2,32,512]{2,1,0:T(8,128)(2,1)S(1)}, bf16[2,32,512]{2,1,0:T(8,128)(2,1)S(1)}, u32[]{:S(2)}, u32[]{:S(2)}) collective-permute-start(bf16[2,32,512]{2,1,0:T(8,128)(2,1)S(1)} %pad_maximum_fusion.1), channel_id=1, source_target_pairs={{0,8},{8,0},{1,9},{9,1},{2,10},{10,2},{3,11},{11,3},{4,12},{12,4},... | collective-permute-start | bytes 196616 | tf_op jit(solution)/shard_map/ppermute | solution.py:217
  53.7 11.8 %collective-permute-start.1 = (bf16[16,2,2,32,512]{4,3,2,1,0:T(8,128)(2,1)S(1)}, bf16[16,2,2,32,512]{4,3,2,1,0:T(8,128)(2,1)}, u32[]{:S(2)}, u32[]{:S(2)}) collective-permute-start(bf16[16,2,2,32,512]{4,3,2,1,0:T(8,128)(2,1)S(1)} %bitcast.21), channel_id=1, source_target_pairs={{0,1},{1,0},{2,3},{3,2},{4,5},{5,4},{6,7},{7,6},{8,9},{9,8},{10,11... | collective-permute-start | bytes 6291464 | tf_op jit(solution)/shard_map/ppermute | solution.py:224
  70.4 2.2 %collective-permute-start.4 = (bf16[96,512]{1,0:T(8,128)(2,1)S(1)}, bf16[96,512]{1,0:T(8,128)(2,1)S(1)}, u32[]{:S(2)}, u32[]{:S(2)}) collective-permute-start(bf16[96,512]{1,0:T(8,128)(2,1)S(1)} %get-tuple-element.72._), channel_id=1, source_target_pairs={{448,384},{449,385},{450,386},{451,387},{452,388},{453,389},{454,3... | collective-permute-start | bytes 294920 | tf_op jit(solution)/shard_map/ppermute | solution.py:257
  71.2 2.2 %collective-permute-start.5 = (bf16[96,512]{1,0:T(8,128)(2,1)S(1)}, bf16[96,512]{1,0:T(8,128)(2,1)S(1)}, u32[]{:S(2)}, u32[]{:S(2)}) collective-permute-start(bf16[96,512]{1,0:T(8,128)(2,1)S(1)} %get-tuple-element.74._), channel_id=1, source_target_pairs={{384,320},{385,321},{386,322},{387,323},{388,324},{389,325},{390,3... | collective-permute-start | bytes 294920 | tf_op jit(solution)/shard_map/ppermute | solution.py:257
  71.9 2.2 %collective-permute-start.6 = (bf16[96,512]{1,0:T(8,128)(2,1)S(1)}, bf16[96,512]{1,0:T(8,128)(2,1)S(1)}, u32[]{:S(2)}, u32[]{:S(2)}) collective-permute-start(bf16[96,512]{1,0:T(8,128)(2,1)S(1)} %get-tuple-element.76._), channel_id=1, source_target_pairs={{384,320},{385,321},{386,322},{387,323},{388,324},{389,325},{390,3... | collective-permute-start | bytes 294920 | tf_op jit(solution)/shard_map/ppermute | solution.py:257
  72.6 2.2 %collective-permute-start.7 = (bf16[96,512]{1,0:T(8,128)(2,1)S(1)}, bf16[96,512]{1,0:T(8,128)(2,1)S(1)}, u32[]{:S(2)}, u32[]{:S(2)}) collective-permute-start(bf16[96,512]{1,0:T(8,128)(2,1)S(1)} %get-tuple-element.78._), channel_id=1, source_target_pairs={{384,320},{385,321},{386,322},{387,323},{388,324},{389,325},{390,3... | collective-permute-start | bytes 294920 | tf_op jit(solution)/shard_map/ppermute | solution.py:257
  73.4 2.2 %collective-permute-start.8 = (bf16[96,512]{1,0:T(8,128)(2,1)S(1)}, bf16[96,512]{1,0:T(8,128)(2,1)S(1)}, u32[]{:S(2)}, u32[]{:S(2)}) collective-permute-start(bf16[96,512]{1,0:T(8,128)(2,1)S(1)} %get-tuple-element.80._), channel_id=1, source_target_pairs={{320,256},{321,257},{322,258},{323,259},{324,260},{325,261},{326,2... | collective-permute-start | bytes 294920 | tf_op jit(solution)/shard_map/ppermute | solution.py:257
  74.1 2.2 %collective-permute-start.9 = (bf16[96,512]{1,0:T(8,128)(2,1)S(1)}, bf16[96,512]{1,0:T(8,128)(2,1)S(1)}, u32[]{:S(2)}, u32[]{:S(2)}) collective-permute-start(bf16[96,512]{1,0:T(8,128)(2,1)S(1)} %get-tuple-element.82._), channel_id=1, source_target_pairs={{320,256},{321,257},{322,258},{323,259},{324,260},{325,261},{326,2... | collective-permute-start | bytes 294920 | tf_op jit(solution)/shard_map/ppermute | solution.py:257
  74.9 2.2 %collective-permute-start.10 = (bf16[96,512]{1,0:T(8,128)(2,1)S(1)}, bf16[96,512]{1,0:T(8,128)(2,1)S(1)}, u32[]{:S(2)}, u32[]{:S(2)}) collective-permute-start(bf16[96,512]{1,0:T(8,128)(2,1)S(1)} %get-tuple-element.84._), channel_id=1, source_target_pairs={{320,256},{321,257},{322,258},{323,259},{324,260},{325,261},{326,2... | collective-permute-start | bytes 294920 | tf_op jit(solution)/shard_map/ppermute | solution.py:257
  75.6 2.2 %collective-permute-start.11 = (bf16[96,512]{1,0:T(8,128)(2,1)S(1)}, bf16[96,512]{1,0:T(8,128)(2,1)S(1)}, u32[]{:S(2)}, u32[]{:S(2)}) collective-permute-start(bf16[96,512]{1,0:T(8,128)(2,1)S(1)} %get-tuple-element.86._), channel_id=1, source_target_pairs={{256,192},{257,193},{258,194},{259,195},{260,196},{261,197},{262,1... | collective-permute-start | bytes 294920 | tf_op jit(solution)/shard_map/ppermute | solution.py:257
  76.3 2.2 %collective-permute-start.12 = (bf16[96,512]{1,0:T(8,128)(2,1)S(1)}, bf16[96,512]{1,0:T(8,128)(2,1)S(1)}, u32[]{:S(2)}, u32[]{:S(2)}) collective-permute-start(bf16[96,512]{1,0:T(8,128)(2,1)S(1)} %get-tuple-element.88._), channel_id=1, source_target_pairs={{256,192},{257,193},{258,194},{259,195},{260,196},{261,197},{262,1... | collective-permute-start | bytes 294920 | tf_op jit(solution)/shard_map/ppermute | solution.py:257
  77.1 2.2 %collective-permute-start.13 = (bf16[96,512]{1,0:T(8,128)(2,1)S(1)}, bf16[96,512]{1,0:T(8,128)(2,1)S(1)}, u32[]{:S(2)}, u32[]{:S(2)}) collective-permute-start(bf16[96,512]{1,0:T(8,128)(2,1)S(1)} %get-tuple-element.90._), channel_id=1, source_target_pairs={{256,192},{257,193},{258,194},{259,195},{260,196},{261,197},{262,1... | collective-permute-start | bytes 294920 | tf_op jit(solution)/shard_map/ppermute | solution.py:257
  77.8 2.3 %collective-permute-start.14 = (bf16[96,512]{1,0:T(8,128)(2,1)S(1)}, bf16[96,512]{1,0:T(8,128)(2,1)S(1)}, u32[]{:S(2)}, u32[]{:S(2)}) collective-permute-start(bf16[96,512]{1,0:T(8,128)(2,1)S(1)} %get-tuple-element.92._), channel_id=1, source_target_pairs={{192,128},{193,129},{194,130},{195,131},{196,132},{197,133},{198,1... | collective-permute-start | bytes 294920 | tf_op jit(solution)/shard_map/ppermute | solution.py:257
  78.5 2.3 %collective-permute-start.15 = (bf16[96,512]{1,0:T(8,128)(2,1)S(1)}, bf16[96,512]{1,0:T(8,128)(2,1)S(1)}, u32[]{:S(2)}, u32[]{:S(2)}) collective-permute-start(bf16[96,512]{1,0:T(8,128)(2,1)S(1)} %get-tuple-element.94._), channel_id=1, source_target_pairs={{192,128},{193,129},{194,130},{195,131},{196,132},{197,133},{198,1... | collective-permute-start | bytes 294920 | tf_op jit(solution)/shard_map/ppermute | solution.py:257
  79.5 2.2 %collective-permute-start.16 = (bf16[96,512]{1,0:T(8,128)(2,1)S(1)}, bf16[96,512]{1,0:T(8,128)(2,1)S(1)}, u32[]{:S(2)}, u32[]{:S(2)}) collective-permute-start(bf16[96,512]{1,0:T(8,128)(2,1)S(1)} %get-tuple-element.96._), channel_id=1, source_target_pairs={{192,128},{193,129},{194,130},{195,131},{196,132},{197,133},{198,1... | collective-permute-start | bytes 294920 | tf_op jit(solution)/shard_map/ppermute | solution.py:257
  80.2 4.7 %collective-permute-start.17 = (bf16[96,512]{1,0:T(8,128)(2,1)S(1)}, bf16[96,512]{1,0:T(8,128)(2,1)S(1)}, u32[]{:S(2)}, u32[]{:S(2)}) collective-permute-start(bf16[96,512]{1,0:T(8,128)(2,1)S(1)} %get-tuple-element.98._), channel_id=1, source_target_pairs={{128,64},{129,65},{130,66},{131,67},{132,68},{133,69},{134,70},{13... | collective-permute-start | bytes 294920 | tf_op jit(solution)/shard_map/ppermute | solution.py:257
  80.9 5.4 %collective-permute-start.18 = (bf16[96,512]{1,0:T(8,128)(2,1)S(1)}, bf16[96,512]{1,0:T(8,128)(2,1)S(1)}, u32[]{:S(2)}, u32[]{:S(2)}) collective-permute-start(bf16[96,512]{1,0:T(8,128)(2,1)S(1)} %get-tuple-element.100._), channel_id=1, source_target_pairs={{128,64},{129,65},{130,66},{131,67},{132,68},{133,69},{134,70},{13... | collective-permute-start | bytes 294920 | tf_op jit(solution)/shard_map/ppermute | solution.py:257
  81.7 6.0 %collective-permute-start.19 = (bf16[96,512]{1,0:T(8,128)(2,1)S(1)}, bf16[96,512]{1,0:T(8,128)(2,1)S(1)}, u32[]{:S(2)}, u32[]{:S(2)}) collective-permute-start(bf16[96,512]{1,0:T(8,128)(2,1)S(1)} %get-tuple-element.102._), channel_id=1, source_target_pairs={{128,64},{129,65},{130,66},{131,67},{132,68},{133,69},{134,70},{13... | collective-permute-start | bytes 294920 | tf_op jit(solution)/shard_map/ppermute | solution.py:257
  85.0 26.8 %collective-permute-start.20 = (bf16[96,512]{1,0:T(8,128)(2,1)S(1)}, bf16[96,512]{1,0:T(8,128)(2,1)S(1)}, u32[]{:S(2)}, u32[]{:S(2)}) collective-permute-start(bf16[96,512]{1,0:T(8,128)(2,1)S(1)} %get-tuple-element.108._), channel_id=1, source_target_pairs={{64,0},{65,1},{66,2},{67,3},{68,4},{69,5},{70,6},{71,7},{72,8},{73... | collective-permute-start | bytes 294920 | tf_op jit(solution)/shard_map/ppermute | solution.py:257
  86.4 30.0 %collective-permute-start.21 = (bf16[96,512]{1,0:T(8,128)(2,1)S(1)}, bf16[96,512]{1,0:T(8,128)(2,1)S(1)}, u32[]{:S(2)}, u32[]{:S(2)}) collective-permute-start(bf16[96,512]{1,0:T(8,128)(2,1)S(1)} %get-tuple-element.110._), channel_id=1, source_target_pairs={{64,0},{65,1},{66,2},{67,3},{68,4},{69,5},{70,6},{71,7},{72,8},{73... | collective-permute-start | bytes 294920 | tf_op jit(solution)/shard_map/ppermute | solution.py:257
  87.7 32.1 %collective-permute-start.22 = (bf16[96,512]{1,0:T(8,128)(2,1)S(1)}, bf16[96,512]{1,0:T(8,128)(2,1)S(1)}, u32[]{:S(2)}, u32[]{:S(2)}) collective-permute-start(bf16[96,512]{1,0:T(8,128)(2,1)S(1)} %get-tuple-element.112._), channel_id=1, source_target_pairs={{64,0},{65,1},{66,2},{67,3},{68,4},{69,5},{70,6},{71,7},{72,8},{73... | collective-permute-start | bytes 294920 | tf_op jit(solution)/shard_map/ppermute | solution.py:257
  136.7 9.6 %collective-permute-start.23 = (bf16[4,2,2,32,512]{4,3,2,1,0:T(8,128)(2,1)S(1)}, bf16[4,2,2,32,512]{4,3,2,1,0:T(8,128)(2,1)S(1)}, u32[]{:S(2)}, u32[]{:S(2)}) collective-permute-start(bf16[4,2,2,32,512]{4,3,2,1,0:T(8,128)(2,1)S(1)} %get-tuple-element.120), channel_id=1, source_target_pairs={{0,1},{1,0},{2,3},{3,2},{4,5},{5,4},{6,7},{7,6},{8,9},{9,8},{10,11... | collective-permute-start | bytes 1572872 | tf_op jit(solution)/shard_map/ppermute | solution.py:293
  158.6 13.7 %collective-permute-start.24 = (bf16[2,32,512]{2,1,0:T(8,128)(2,1)S(1)}, bf16[2,32,512]{2,1,0:T(8,128)(2,1)S(1)}, u32[]{:S(2)}, u32[]{:S(2)}) collective-permute-start(bf16[2,32,512]{2,1,0:T(8,128)(2,1)S(1)} %get-tuple-element.122._), channel_id=1, source_target_pairs={{0,8},{8,0},{1,9},{9,1},{2,10},{10,2},{3,11},{11,3},{4,12},{12,4},... | collective-permute-start | bytes 196616 | tf_op jit(solution)/shard_map/ppermute | solution.py:312
  (6 other events, 23.1 us)
